TPU v7x, 256 devices: a whole 4x4x8 slice. The times are simulated.
256 devices in a mesh: dp: 64 (over x, z_hi, y), vocab: 4 (over z_lo, core).
Axes of the slice: x: 4, y: 4, z: 8 (z_hi: 4, z_lo: 2; z = z_hi * 2 + z_lo), core: 2. Of those that a mesh axis runs over, the one named last changes fastest.
Arguments:
- hidden: bfloat16 [512, 4608], P('dp'), may hold values from -1.5 to 1.5
- table: bfloat16 [131072, 4608], P(('dp', 'vocab')), may hold values from -1 to 1
- target_ids: int32 [512], P('dp'), may hold values from 0 to 131071
- loss_weight: bfloat16 [512], P('dp'), may hold values from 2 to 8
- input_ids: int32 [512], P('dp'), may hold values from 0 to 131071
- emb_grad_in: bfloat16 [512, 4608], P('dp'), may hold values from -6 to 6
Outputs:
- grad_hidden: bfloat16 [512, 4608], P('dp')
- grad_table: bfloat16 [131072, 4608], P(('dp', 'vocab'))
All inputs are finite; a program needn't handle non-finite values.
Results may differ from a plain program's by a relative error of at most 0.0045.
Values may be sent and summed in bfloat16 or wider, within the bound.
No kernel may reach another device: no remote copies, remote signals or barrier semaphores. Data moves between devices by JAX's collectives and lax.ppermute only.
A program may use at most 128 MiB of HBM per device.

v0:
```python
import jax
import jax.numpy as jnp
from jax import lax
from jax.sharding import PartitionSpec as P


def body(hidden, table, target_ids, loss_weight, input_ids, emb_grad_in):
    own_rows = table.shape[0]
    row_start = lax.axis_index(("dp", "vocab")) * own_rows
    all_hidden, all_grad_in, all_weight = (
        lax.all_gather(hidden, "dp", axis=0, tiled=True),
        lax.all_gather(emb_grad_in, "dp", axis=0, tiled=True),
        lax.all_gather(loss_weight, "dp", axis=0, tiled=True),
    )
    all_target, all_input = (
        lax.all_gather(target_ids, "dp", axis=0, tiled=True),
        lax.all_gather(input_ids, "dp", axis=0, tiled=True),
    )
    logits = jnp.dot(all_hidden, table.T, preferred_element_type=jnp.float32)
    squash = jnp.tanh(logits / 30.0)
    expo = jnp.exp(30.0 * squash)
    total = lax.psum(jnp.sum(expo, axis=1), ("dp", "vocab"))
    columns = row_start + lax.iota(jnp.int32, own_rows)
    hits = columns[None, :] == all_target[:, None]
    weight = all_weight.astype(jnp.float32)[:, None]
    dlogit = (
        weight * (expo / total[:, None] - hits.astype(jnp.float32)) * (1.0 - squash * squash)
    ).astype(jnp.bfloat16)
    summed = lax.psum_scatter(
        jnp.dot(dlogit, table, preferred_element_type=jnp.float32),
        ("dp", "vocab"),
        scatter_dimension=0,
        tiled=True,
    )
    grad_hidden = lax.all_gather(summed.astype(jnp.bfloat16), "vocab", axis=0, tiled=True)
    onehot_in = (all_input[:, None] == columns[None, :]).astype(jnp.bfloat16)
    contract = (((0,), (0,)), ((), ()))
    head = lax.dot_general(dlogit, all_hidden, contract, preferred_element_type=jnp.float32)
    embed = lax.dot_general(onehot_in, all_grad_in, contract, preferred_element_type=jnp.float32)
    grad_table = head + embed
    return (grad_hidden, grad_table.astype(jnp.bfloat16))


def solution(mesh):
    placed = (P("dp", None), P(("dp", "vocab"), None), P("dp"), P("dp"), P("dp"), P("dp", None))
    return jax.shard_map(
        body,
        mesh=mesh,
        in_specs=placed,
        out_specs=(P("dp", None), P(("dp", "vocab"), None)),
        check_vma=False,
    )
```

profile of v0, /device:TPU:1, one launch (start us, length us, event | category | flops | bytes accessed | tf_op | source)
XLA Modules:
  0.0 496.4 jit_solution(14603721903495976927)
XLA Ops:
  7.2 0.0 all-gather.4.cloned.1.call-start
  7.2 0.7 all-gather.4.cloned.1.call-update
  7.9 0.0 all-gather.6.cloned.1.call-start
  7.9 0.7 all-gather.6.cloned.1.call-update
  8.7 1.3 dynamic-slice
  10.6 0.9 dynamic-update-slice
  11.4 173.3 %all-reduce = bf16[512]{0:T(512)(128)(2,1)S(1)} all-reduce(bf16[512]{0:T(512)(128)(2,1)S(1)} %dynamic-update-slice), channel_id=1, replica_groups=mesh['dp'=64,'vocab'=4] {'dp'}, use_global_device_ids=true, to_apply=%add | all-reduce | flops 512 | bytes 2048
  184.7 0.9 dynamic-update-slice.1
  185.6 0.8 dynamic-update-slice.2
  186.4 14.2 %all-reduce.4 = (s32[512]{0:T(512)S(1)}, s32[512]{0:T(512)S(1)}) all-reduce(s32[512]{0:T(512)S(1)} %dynamic-update-slice.1, s32[512]{0:T(512)S(1)} %dynamic-update-slice.2), channel_id=1, replica_groups=mesh['dp'=64,'vocab'=4] {'dp'}, use_global_device_ids=true, to_apply=%add.1 | all-reduce | flops 1024 | bytes 8192
  200.6 0.0 all-gather.4.cloned.1.call-done
  200.6 6.1 %fusion.1 = (f32[512]{0:T(512)S(1)}, f32[512,512]{0,1:T(8,128)S(1)}) fusion(bf16[512,4608]{1,0:T(8,128)(2,1)} %all-gather.4.cloned.1.call-done, bf16[512,4608]{1,0:T(8,128)(2,1)} %param.7), kind=kOutput, calls=%fused_computation.5 | convolution fusion | flops 2416705024 | bytes 10487808 | tf_op jit(solution)/shard_map/dot_general | solution.py:19
  206.7 106.8 %psum.7 = f32[512]{0:T(512)S(1)} all-reduce(f32[512]{0:T(512)S(1)} %get-tuple-element.4), channel_id=1, replica_groups=mesh['dp'=64,'vocab'=4] {'dp','vocab'}, use_global_device_ids=true, to_apply=%region_1.0 | all-reduce | flops 512 | bytes 4096 | tf_op jit(solution)/shard_map/psum | solution.py:22
  313.5 7.5 %fusion.7 = f32[512,4608]{1,0:T(8,128)} fusion(bf16[512,4608]{1,0:T(8,128)(2,1)} %param.7, f32[512,512]{0,1:T(8,128)S(1)} %get-tuple-element.5, s32[512]{0:T(512)S(1)} %get-tuple-element.2, f32[512]{0:T(512)S(1)} %psum.7, f32[512]{0:T(512)S(1)} %convert_element_type.16, s32[512]{0:T(512)S(1)} %iota_add_fusion), kind=kOutput, calls=%fused_computation.13 | convolution fusion | flops 2418540544 | bytes 15212544 | tf_op jit(solution)/shard_map/dot_general | solution.py:30
  321.1 143.1 %all-reduce.6 = bf16[512,4608]{1,0:T(8,128)(2,1)} all-reduce(f32[512,4608]{1,0:T(8,128)} %fusion.7), channel_id=2, replica_groups=mesh['dp'=64,'vocab'=4] {'dp','vocab'}, use_global_device_ids=true, to_apply=%region_2.0.clone | all-reduce | flops 2359296 | bytes 14155776
  464.2 0.9 fusion.5
  465.1 8.0 %all-gather = bf16[4,2,4608]{2,1,0:T(2,128)(2,1)S(1)} all-gather(bf16[1,2,4608]{2,1,0:T(2,128)(2,1)S(1)} %fusion.5), channel_id=1, replica_groups=mesh['dp'=64,'vocab'=4] {'vocab'}, dimensions={0}, use_global_device_ids=true | all-gather | bytes 92160 | tf_op jit(solution)/shard_map/all_gather | solution.py:35
  473.1 0.7 reshape.22
  473.8 7.7 %fusion.6 = f32[512,4608]{1,0:T(8,128)} fusion(bf16[512,4608]{1,0:T(8,128)(2,1)} %all-gather.4.cloned.1.call-done, f32[512,512]{0,1:T(8,128)S(1)} %get-tuple-element.5, s32[512]{0:T(512)S(1)} %get-tuple-element.2, f32[512]{0:T(512)S(1)} %psum.7, f32[512]{0:T(512)S(1)} %convert_element_type.16, s32[512]{0:T(512)S(1)} %iota_add_fusion), kind=kOutput, calls=%fused_computation.12 | convolution fusion | flops 2418540544 | bytes 15212544 | tf_op jit(solution)/shard_map/dot_general | solution.py:38
  481.5 0.0 all-gather.6.cloned.1.call-done
  481.5 8.1 %add_convert_fusion = bf16[512,4608]{1,0:T(8,128)(2,1)} fusion(f32[512,4608]{1,0:T(8,128)} %fusion.6, bf16[512,4608]{1,0:T(8,128)(2,1)} %all-gather.6.cloned.1.call-done, s32[512]{0:T(512)S(1)} %get-tuple-element.3, s32[512]{0:T(512)S(1)} %iota_add_fusion), kind=kOutput, calls=%fused_computation | convolution fusion | flops 2420899840 | bytes 18878464 | tf_op jit(solution)/shard_map/dot_general | solution.py:39
  (5 shorter events, 0.0 us)
Async XLA Ops:
  7.2 193.4 %all-gather.4.cloned.1.call-start = ((), (), s32[]{:S(2)}) async-start(), calls=%async_computation | async-start | bytes 4792320 | tf_op jit(solution)/shard_map/all_gather | solution.py:11
  7.9 473.6 %all-gather.6.cloned.1.call-start = ((), (), s32[]{:S(2)}) async-start(), calls=%async_computation.1 | async-start | bytes 4792320 | tf_op jit(solution)/shard_map/all_gather | solution.py:12
Sparse Core Ops, SparseCore 0:
  11.2 95.0 all-gather.3
  109.5 89.8 all-gather.5
where the time goes:
time: 497 us; the launch traced here: 496 us
  blocking collectives  445 us (90%)
  matrix products  29.4 us (6%)
  between operations  14.7 us (3%)
  local copies, waits for them, and re-layouts  5.4 us (1%)
    unnamed x3, blocking collectives  331 us
    psum x1, blocking collectives, body(): total = lax.psum(jnp.sum(expo, axis=1), ('dp', 'vocab'))  107 us
  transfers between devices with their start and end apart: 2, of which 0 were waited for; matrix products, arithmetic and copies ran while one was open for 5% of the time, Pallas kernels for 0%

commit v1 on v0

v1 whole, which is shorter than its diff:
```python
import jax
import jax.numpy as jnp
from jax import lax
from jax.sharding import Mesh, PartitionSpec as P

DP = ("x", "zh", "y")
AXES = ("x", "zh", "y", "zl", "c")
F32, BF16 = jnp.float32, jnp.bfloat16


def pull(value, axis, shift, size=4):
    return lax.ppermute(value, axis, [(i, (i - shift) % size) for i in range(size)])


def push(value, axis, shift, size=4):
    return lax.ppermute(value, axis, [(i, (i + shift) % size) for i in range(size)])


def swap(value, axis):
    return lax.ppermute(value, axis, [(0, 1), (1, 0)])


def digits(ids):
    return [ids // 65536, (ids // 256) % 256, ids % 256]


def joined(cols):
    return (cols[:, 0] * 65536.0 + cols[:, 1] * 256.0 + cols[:, 2]).astype(jnp.int32)


def whole(core, own, other):
    return jnp.where(
        core == 0, jnp.concatenate([own, other], 1), jnp.concatenate([other, own], 1)
    )


def body(hidden, table, target_ids, loss_weight, input_ids, emb_grad_in):
    own_rows, width = table.shape
    half = width // 2
    core = lax.axis_index("c")
    row_start = lax.axis_index(AXES) * own_rows
    tokens = hidden.shape[0] * 64
    slab = tokens // 4

    def my_half(a):
        return lax.dynamic_slice_in_dim(a, core * half, half, 1)

    def other_half(a):
        return lax.dynamic_slice_in_dim(a, (1 - core) * half, half, 1)

    emb_half = lax.all_gather(my_half(emb_grad_in), DP, axis=0, tiled=True)

    info = jnp.stack(
        [v.astype(BF16) for v in digits(target_ids) + digits(input_ids)] + [loss_weight], 1
    )
    info = jnp.pad(info, ((0, 0), (0, 128 - info.shape[1])))
    block = jnp.concatenate([my_half(hidden), info], 1)
    block = jnp.concatenate([block] + [pull(block, "zh", d) for d in (1, 2, 3)], 0)
    block = jnp.concatenate([block] + [pull(block, "y", d) for d in (1, 2, 3)], 0)
    slabs = [block] + [pull(block, "x", d) for d in (1, 2, 3)]

    pair = jnp.concatenate([my_half(table), swap(other_half(table), "c")], 0)

    facts = jnp.concatenate([s[:, half : half + 8] for s in slabs], 0).astype(F32)
    target_rel, input_rel, weight = joined(facts[:, 0:3]), joined(facts[:, 3:6]), facts[:, 6]

    place = lax.iota(jnp.int32, tokens)
    dx, dy, dz, i = place // 128, (place // 32) % 4, (place // 8) % 4, place % 8
    ax, ay, az = (lax.axis_index(n) for n in ("x", "y", "zh"))
    absolute = (((ax + dx) % 4) * 16 + ((az + dz) % 4) * 4 + (ay + dy) % 4) * 8 + i
    perm = absolute[:, None] == place[None, :]

    full, squash, expo = [], [], []
    for s in slabs:
        own = s[:, :half]
        f = whole(core, own, swap(own, "c"))
        logits = lax.dot_general(f, table, (((1,), (1,)), ((), ())), preferred_element_type=F32)
        q = jnp.tanh(logits / 30.0)
        full.append(f)
        squash.append(q)
        expo.append(jnp.exp(30.0 * q))
    squash, expo = jnp.concatenate(squash, 0), jnp.concatenate(expo, 0)
    local = jnp.sum(expo, 1)
    local = jnp.sum(jnp.where(perm, local[:, None], 0.0), 0).reshape(4, 128)
    local = lax.psum(local, "c")
    local = lax.all_to_all(jnp.broadcast_to(local, (16, 4, 128)), ("x", "y"), 0, 0)
    total = lax.psum(jnp.sum(local, 0), ("zh", "zl")).reshape(tokens)
    total = jnp.sum(jnp.where(perm, total[None, :], 0.0), 1)

    columns = row_start + lax.iota(jnp.int32, own_rows)
    hits = columns[None, :] == target_rel[:, None]
    dlogit = (
        weight[:, None]
        * (expo / total[:, None] - hits.astype(F32))
        * (1.0 - squash * squash)
    ).astype(BF16)
    both = jnp.concatenate([dlogit, swap(dlogit, "c")], 1)

    parts = [
        jnp.dot(both[d * slab : (d + 1) * slab], pair, preferred_element_type=F32)
        for d in (1, 2, 3)
    ]
    got = [push(p.astype(BF16), "x", d) for p, d in zip(parts, (1, 2, 3))]
    acc = jnp.dot(both[:slab], pair, preferred_element_type=F32)
    acc = acc + got[0].astype(F32) + got[1].astype(F32) + got[2].astype(F32)
    got = [push(acc[32 * d : 32 * d + 32].astype(BF16), "y", d) for d in (1, 2, 3)]
    acc = acc[:32] + got[0].astype(F32) + got[1].astype(F32) + got[2].astype(F32)
    got = [push(acc[8 * d : 8 * d + 8], "zh", d) for d in (1, 2, 3)]
    acc = acc[:8] + got[0] + got[1] + got[2]
    acc = (acc + swap(acc, "zl")).astype(BF16)
    grad_hidden = whole(core, acc, swap(acc, "c"))

    emb = whole(core, emb_half, swap(emb_half, "c"))
    input_abs = jnp.sum(jnp.where(perm, input_rel[:, None], 0), 0)
    onehot_in = (input_abs[:, None] == columns[None, :]).astype(BF16)
    contract = (((0,), (0,)), ((), ()))
    grad_table = lax.dot_general(
        jnp.concatenate([dlogit, onehot_in], 0),
        jnp.concatenate(full + [emb], 0),
        contract,
        preferred_element_type=F32,
    )
    return (grad_hidden, grad_table.astype(BF16))


def solution(mesh):
    fine = Mesh(mesh.devices.reshape(4, 4, 4, 2, 2), AXES)
    rows, every = P(DP, None), P(AXES, None)
    return jax.shard_map(
        body,
        mesh=fine,
        in_specs=(rows, every, P(DP), P(DP), P(DP), rows),
        out_specs=(rows, every),
        check_vma=False,
    )
```

time: 497 us -> 249 us (0.50)
  blocking collectives: 445 us -> 18.9 us
  waiting for transfers between devices: 1.38 us -> 70.9 us
  starting transfers between devices: 0.08 us -> 57.5 us
  other arithmetic: 0.01 us -> 25 us
  local copies, waits for them, and re-layouts: 5.4 us -> 21.6 us
  matrix products: 29.4 us -> 40 us
    unnamed x3 -> x0, blocking collectives: 331 us -> none
    psum x1 -> x2, blocking collectives: 107 us -> 18.9 us  [the longest x1 15.6 us: body(): total = lax.psum(jnp.sum(local, 0), ('zh', 'zl')).reshape(tokens)]
    ppermute x0 -> x27, starting transfers between devices: none -> 53.3 us  [the longest x9 23.8 us: swap(): return lax.ppermute(value, axis, [(0, 1), (1, 0)])]
    ppermute x0 -> x27, waiting for transfers between devices: none -> 48.2 us  [the longest x9 35.4 us: push(): lax.ppermute(value, axis, [(i, (i + shift) % size) for i in range(size)])]
    all_gather x2 -> x1, waiting for transfers between devices: 0.01 us -> 17.7 us  [body(): emb_half = lax.all_gather(my_half(emb_grad_in), DP, axis=0, tiled=True)]
    unnamed x0 -> x5, other arithmetic: none -> 11.3 us
    dot_general x4 -> x9, matrix products: 29.4 us -> 40 us  [the longest x4 19.3 us: body(): lax.dot_general(f, table, (((1,), (1,)), ((), ())), preferred_element_typ...]
    slice x0 -> x14, local copies, waits for them, and re-layouts: none -> 10.3 us  [the longest x4 6.94 us: body(): own = s[:, :half]]
  transfers between devices with their start and end apart: 2 -> 29, of which waited for: 0 -> 15; matrix products, arithmetic and copies ran while one was open for 5% -> 28% of each run, Pallas kernels for 0% -> 0%
where the time goes in v1:
time: 249 us; the launch traced here: 248 us
  waiting for transfers between devices  70.9 us (28%)
  starting transfers between devices  57.5 us (23%)
  matrix products  40 us (16%)
  other arithmetic  25 us (10%)
  local copies, waits for them, and re-layouts  21.6 us (9%)
  blocking collectives  18.9 us (8%)
  between operations  14.3 us (6%)
    ppermute x9, waiting for transfers between devices, push(): lax.ppermute(value, axis, [(i, (i + shift) % size) for i in range(size)])  35.4 us
    ppermute x9, starting transfers between devices, swap(): return lax.ppermute(value, axis, [(0, 1), (1, 0)])  23.8 us
    dot_general x4, matrix products, body(): lax.dot_general(f, table, (((1,), (1,)), ((), ())), preferred_element_typ...  19.3 us
    ppermute x9, starting transfers between devices, pull(): lax.ppermute(value, axis, [(i, (i - shift) % size) for i in range(size)])  18.8 us
    all_gather x1, waiting for transfers between devices, body(): emb_half = lax.all_gather(my_half(emb_grad_in), DP, axis=0, tiled=True)  17.7 us
    psum x1, blocking collectives, body(): total = lax.psum(jnp.sum(local, 0), ('zh', 'zl')).reshape(tokens)  15.6 us
    ppermute x9, waiting for transfers between devices, pull(): lax.ppermute(value, axis, [(i, (i - shift) % size) for i in range(size)])  11.7 us
    unnamed x5, other arithmetic  11.3 us
  transfers between devices with their start and end apart: 29, of which 15 were waited for; matrix products, arithmetic and copies ran while one was open for 28% of the time, Pallas kernels for 0%

profile of v1, /device:TPU:1, one launch (start us, length us, event | category | flops | bytes accessed | tf_op | source)
XLA Modules:
  0.0 248.2 jit_solution(7129793549643095007)
XLA Ops:
  9.3 6.8 %collective-permute-start = (bf16[8,2432]{1,0:T(8,128)(2,1)S(1)}, bf16[8,2432]{1,0:T(8,128)(2,1)S(1)}, u32[]{:S(2)}, u32[]{:S(2)}) collective-permute-start(bf16[8,2432]{1,0:T(8,128)(2,1)S(1)} %get-tuple-element.10), channel_id=1, source_target_pairs={{0,48},{16,0},{32,16},{48,32},{1,49},{17,1},{33,17},{49,33},{2,50}... | collective-permute-start | bytes 116744 | tf_op jit(solution)/shard_map/ppermute | solution.py:12
  19.4 3.5 %collective-permute-done.1 = bf16[8,2432]{1,0:T(8,128)(2,1)S(1)} collective-permute-done((bf16[8,2432]{1,0:T(8,128)(2,1)S(1)}, bf16[8,2432]{1,0:T(8,128)(2,1)S(1)}, u32[]{:S(2)}, u32[]{:S(2)}) %collective-permute-start.1) | collective-permute-done | bytes 38944 | tf_op jit(solution)/shard_map/ppermute | solution.py:12
  40.0 3.9 %collective-permute-start.9 = (bf16[128,2304]{1,0:T(8,128)(2,1)}, bf16[128,2304]{1,0:T(8,128)(2,1)}, u32[]{:S(2)}, u32[]{:S(2)}) collective-permute-start(bf16[128,2304]{1,0:T(8,128)(2,1)} %slice.123), channel_id=1, source_target_pairs={{0,1},{1,0},{2,3},{3,2},{4,5},{5,4},{6,7},{7,6},{8,9},{9,8},{10,11... | collective-permute-start | bytes 1769480 | tf_op jit(solution)/shard_map/ppermute | solution.py:20
  43.9 4.1 %constant_dynamic-slice_fusion.2 = (bf16[512,2304]{1,0:T(8,128)(2,1)S(1)}, bf16[512,2304]{1,0:T(8,128)(2,1)}) fusion(bf16[512,4608]{1,0:T(8,128)(2,1)} %param.7, s32[]{:T(128)S(6)} %select_n.163, s32[]{:T(128)S(6)} %select_n.188), kind=kLoop, calls=%fused_computation.150 | loop fusion | bytes 9437192 | tf_op jit(solution)/shard_map/dynamic_slice | solution.py:46
  50.3 6.1 %collective-permute-start.12 = (bf16[128,2304]{1,0:T(8,128)(2,1)S(1)}, bf16[128,2304]{1,0:T(8,128)(2,1)}, u32[]{:S(2)}, u32[]{:S(2)}) collective-permute-start(bf16[128,2304]{1,0:T(8,128)(2,1)S(1)} %slice.126), channel_id=1, source_target_pairs={{0,1},{1,0},{2,3},{3,2},{4,5},{5,4},{6,7},{7,6},{8,9},{9,8},{10,11... | collective-permute-start | bytes 1769480 | tf_op jit(solution)/shard_map/ppermute | solution.py:20
  57.8 4.5 %collective-permute-done.7 = bf16[128,2432]{1,0:T(8,128)(2,1)} collective-permute-done((bf16[128,2432]{1,0:T(8,128)(2,1)}, bf16[128,2432]{1,0:T(8,128)(2,1)}, u32[]{:S(2)}, u32[]{:S(2)}) %collective-permute-start.7) | collective-permute-done | bytes 622624 | tf_op jit(solution)/shard_map/ppermute | solution.py:12
  64.3 4.3 %collective-permute-start.11 = (bf16[128,2304]{1,0:T(8,128)(2,1)}, bf16[128,2304]{1,0:T(8,128)(2,1)}, u32[]{:S(2)}, u32[]{:S(2)}) collective-permute-start(bf16[128,2304]{1,0:T(8,128)(2,1)} %slice.125), channel_id=1, source_target_pairs={{0,1},{1,0},{2,3},{3,2},{4,5},{5,4},{6,7},{7,6},{8,9},{9,8},{10,11... | collective-permute-start | bytes 1769480 | tf_op jit(solution)/shard_map/ppermute | solution.py:20
  68.6 5.5 %multiply_exponential_fusion.3 = (f32[128,512]{1,0:T(8,128)S(1)}, f32[128,512]{1,0:T(8,128)}) fusion(bf16[512,4608]{1,0:T(8,128)(2,1)} %param.7, bf16[128,2304]{1,0:T(8,128)(2,1)} %collective-permute-done.9, bf16[128,2304]{1,0:T(8,128)(2,1)} %slice.123, pred[]{:T(512)S(6)} %eq.59), kind=kOutput, calls=%fused_computation.53 | convolution fusion | flops 609419264 | bytes 6422529 | tf_op jit(solution)/shard_map/dot_general | solution.py:77
  79.2 5.5 %multiply_exponential_fusion = (f32[128,512]{1,0:T(8,128)S(1)}, f32[128,512]{1,0:T(8,128)}) fusion(bf16[512,4608]{1,0:T(8,128)(2,1)} %param.7, bf16[128,2304]{1,0:T(8,128)(2,1)} %collective-permute-done.12, bf16[128,2304]{1,0:T(8,128)(2,1)S(1)} %slice.126, pred[]{:T(512)S(6)} %eq.59), kind=kOutput, calls=%fused_computation.50 | convolution fusion | flops 609419264 | bytes 6422529 | tf_op jit(solution)/shard_map/dot_general | solution.py:77
  84.7 4.1 %multiply_exponential_fusion.1 = (f32[128,512]{1,0:T(8,128)S(1)}, f32[128,512]{1,0:T(8,128)}) fusion(bf16[512,4608]{1,0:T(8,128)(2,1)S(1)} %bitcast.24, bf16[128,2304]{1,0:T(8,128)(2,1)} %collective-permute-done.11, bf16[128,2304]{1,0:T(8,128)(2,1)} %slice.125, pred[]{:T(512)S(6)} %eq.59), kind=kOutput, calls=%fused_computation.51 | convolution fusion | flops 609419264 | bytes 6422529 | tf_op jit(solution)/shard_map/dot_general | solution.py:77
  88.8 4.2 %multiply_exponential_fusion.2 = (f32[128,512]{1,0:T(8,128)S(1)}, f32[128,512]{1,0:T(8,128)}) fusion(bf16[512,4608]{1,0:T(8,128)(2,1)S(1)} %bitcast.24, bf16[128,2304]{1,0:T(8,128)(2,1)} %collective-permute-done.10, bf16[128,2304]{1,0:T(8,128)(2,1)} %slice.124, pred[]{:T(512)S(6)} %eq.59), kind=kOutput, calls=%fused_computation.52 | convolution fusion | flops 609419264 | bytes 6422529 | tf_op jit(solution)/shard_map/dot_general | solution.py:77
  94.5 3.3 %psum.14 = f32[4,128]{1,0:T(4,128)} all-reduce(f32[4,128]{1,0:T(4,128)} %bitcast.29), channel_id=1, replica_groups=mesh['x'=4,'zh'=4,'y'=4,'zl'=2,'c'=2] {'c'}, use_global_device_ids=true, to_apply=%region_2.3 | all-reduce | flops 512 | bytes 4096 | tf_op jit(solution)/shard_map/psum | solution.py:85
  99.1 4.2 %all-to-all-start = ((f32[16,4,128]{2,1,0:T(4,128)}), f32[16,4,128]{2,1,0:T(4,128)}, u32[]{:S(2)}, u32[]{:S(2)}) async-start(f32[16,4,128]{2,1,0:T(4,128)} %broadcast_in_dim.52), calls=%async_computation | async-start | bytes 65536 | tf_op jit(solution)/shard_map/all_to_all | solution.py:86
  104.7 5.0 %all-to-all-done = f32[16,4,128]{2,1,0:T(4,128)} async-done(((f32[16,4,128]{2,1,0:T(4,128)}), f32[16,4,128]{2,1,0:T(4,128)}, u32[]{:S(2)}, u32[]{:S(2)}) %all-to-all-start) | async-done | bytes 32800 | tf_op jit(solution)/shard_map/all_to_all | solution.py:86
  111.1 15.6 %psum.15 = f32[512]{0:T(512)} all-reduce(f32[512]{0:T(512)} %bitcast.28), channel_id=1, replica_groups=mesh['x'=4,'zh'=4,'y'=4,'zl'=2,'c'=2] {'zh','zl'}, use_global_device_ids=true, to_apply=%region_4.5 | all-reduce | flops 512 | bytes 4096 | tf_op jit(solution)/shard_map/psum | solution.py:87
  130.2 5.0 %collective-permute-start.13 = (bf16[512,512]{1,0:T(8,128)(2,1)}, bf16[512,512]{1,0:T(8,128)(2,1)S(1)}, u32[]{:S(2)}, u32[]{:S(2)}) collective-permute-start(bf16[512,512]{1,0:T(8,128)(2,1)} %fusion.9), channel_id=1, source_target_pairs={{0,1},{1,0},{2,3},{3,2},{4,5},{5,4},{6,7},{7,6},{8,9},{9,8},{10,11... | collective-permute-start | bytes 1572872 | tf_op jit(solution)/shard_map/ppermute | solution.py:20
  147.1 3.0 %fusion.26 = bf16[1024,4608]{1,0:T(8,128)(2,1)} fusion(bf16[128,2304]{1,0:T(8,128)(2,1)} %slice.123, bf16[128,2304]{1,0:T(8,128)(2,1)} %collective-permute-done.9, pred[]{:T(512)S(6)} %eq.59), kind=kLoop, calls=%fused_computation.57 | loop fusion | flops 5308415 | bytes 2359297
  150.4 4.2 %collective-permute-done.17 = bf16[128,2304]{1,0:T(8,128)(2,1)S(1)} collective-permute-done((bf16[128,2304]{1,0:T(8,128)(2,1)S(1)}, bf16[128,2304]{1,0:T(8,128)(2,1)S(1)}, u32[]{:S(2)}, u32[]{:S(2)}) %collective-permute-start.17) | collective-permute-done | bytes 589856 | tf_op jit(solution)/shard_map/ppermute | solution.py:16
  154.6 4.7 %collective-permute-done.16 = bf16[128,2304]{1,0:T(8,128)(2,1)S(1)} collective-permute-done((bf16[128,2304]{1,0:T(8,128)(2,1)S(1)}, bf16[128,2304]{1,0:T(8,128)(2,1)S(1)}, u32[]{:S(2)}, u32[]{:S(2)}) %collective-permute-start.16) | collective-permute-done | bytes 589856 | tf_op jit(solution)/shard_map/ppermute | solution.py:16
  159.3 13.7 %collective-permute-done.15 = bf16[128,2304]{1,0:T(8,128)(2,1)S(1)} collective-permute-done((bf16[128,2304]{1,0:T(8,128)(2,1)S(1)}, bf16[128,2304]{1,0:T(8,128)(2,1)S(1)}, u32[]{:S(2)}, u32[]{:S(2)}) %collective-permute-start.15) | collective-permute-done | bytes 589856 | tf_op jit(solution)/shard_map/ppermute | solution.py:16
  177.8 4.1 %collective-permute-done.20 = bf16[32,2304]{1,0:T(8,128)(2,1)S(1)} collective-permute-done((bf16[32,2304]{1,0:T(8,128)(2,1)S(1)}, bf16[32,2304]{1,0:T(8,128)(2,1)S(1)}, u32[]{:S(2)}, u32[]{:S(2)}) %collective-permute-start.20) | collective-permute-done | bytes 147488 | tf_op jit(solution)/shard_map/ppermute | solution.py:16
  182.8 5.0 %collective-permute-done.18 = bf16[32,2304]{1,0:T(8,128)(2,1)S(1)} collective-permute-done((bf16[32,2304]{1,0:T(8,128)(2,1)S(1)}, bf16[32,2304]{1,0:T(8,128)(2,1)S(1)}, u32[]{:S(2)}, u32[]{:S(2)}) %collective-permute-start.18) | collective-permute-done | bytes 147488 | tf_op jit(solution)/shard_map/ppermute | solution.py:16
  202.2 17.7 %all-gather.2.cloned.1.call-done = bf16[512,2304]{1,0:T(8,128)(2,1)} async-done(((bf16[8,2304]{1,0:T(8,128)(2,1)}), bf16[512,2304]{1,0:T(8,128)(2,1)}) %all-gather.2.cloned.1.call-update) | async-done | bytes 2359312 | tf_op jit(solution)/shard_map/all_gather | solution.py:51
  230.9 10.5 %convolution_convert_fusion = bf16[512,4608]{1,0:T(8,128)(2,1)} fusion(bf16[1024,4608]{1,0:T(8,128)(2,1)} %fusion, bf16[512,512]{1,0:T(8,128)(2,1)S(1)} %compare_convert_fusion, bf16[512,512]{1,0:T(8,128)(2,1)} %fusion.9), kind=kOutput, calls=%fused_computation | convolution fusion | flops 4836294656 | bytes 15204352 | tf_op jit(solution)/shard_map/dot_general | solution.py:117
  (130 shorter events, 85.5 us)
Async XLA Ops:
  9.3 10.1 %collective-permute-start = (bf16[8,2432]{1,0:T(8,128)(2,1)S(1)}, bf16[8,2432]{1,0:T(8,128)(2,1)S(1)}, u32[]{:S(2)}, u32[]{:S(2)}) collective-permute-start(bf16[8,2432]{1,0:T(8,128)(2,1)S(1)} %get-tuple-element.10), channel_id=1, source_target_pairs={{0,48},{16,0},{32,16},{48,32},{1,49},{17,1},{33,17},{49,33},{2,50}... | collective-permute-start | bytes 116744 | tf_op jit(solution)/shard_map/ppermute | solution.py:12
  16.2 6.7 %collective-permute-start.1 = (bf16[8,2432]{1,0:T(8,128)(2,1)S(1)}, bf16[8,2432]{1,0:T(8,128)(2,1)S(1)}, u32[]{:S(2)}, u32[]{:S(2)}) collective-permute-start(bf16[8,2432]{1,0:T(8,128)(2,1)S(1)} %get-tuple-element.10), channel_id=1, source_target_pairs={{0,32},{16,48},{32,0},{48,16},{1,33},{17,49},{33,1},{49,17},{2,34}... | collective-permute-start | bytes 116744 | tf_op jit(solution)/shard_map/ppermute | solution.py:12
  26.1 7.5 %collective-permute-start.5 = (bf16[32,2432]{1,0:T(8,128)(2,1)S(1)}, bf16[32,2432]{1,0:T(8,128)(2,1)S(1)}, u32[]{:S(2)}, u32[]{:S(2)}) collective-permute-start(bf16[32,2432]{1,0:T(8,128)(2,1)S(1)} %pad_maximum_fusion.4), channel_id=1, source_target_pairs={{0,4},{4,8},{8,12},{12,0},{1,5},{5,9},{9,13},{13,1},{2,6},{6,10},{... | collective-permute-start | bytes 466952 | tf_op jit(solution)/shard_map/ppermute | solution.py:12
  34.3 14.8 %collective-permute-start.8 = (bf16[128,2432]{1,0:T(8,128)(2,1)}, bf16[128,2432]{1,0:T(8,128)(2,1)}, u32[]{:S(2)}, u32[]{:S(2)}) collective-permute-start(bf16[128,2432]{1,0:T(8,128)(2,1)} %constant_dynamic-update-slice_fusion), channel_id=1, source_target_pairs={{0,64},{64,128},{128,192},{192,0},{1,65},{65,129},{129,193},{193,1... | collective-permute-start | bytes 1867784 | tf_op jit(solution)/shard_map/ppermute | solution.py:12
  35.6 26.8 %collective-permute-start.7 = (bf16[128,2432]{1,0:T(8,128)(2,1)}, bf16[128,2432]{1,0:T(8,128)(2,1)}, u32[]{:S(2)}, u32[]{:S(2)}) collective-permute-start(bf16[128,2432]{1,0:T(8,128)(2,1)} %constant_dynamic-update-slice_fusion), channel_id=1, source_target_pairs={{0,128},{64,192},{128,0},{192,64},{1,129},{65,193},{129,1},{193,65... | collective-permute-start | bytes 1867784 | tf_op jit(solution)/shard_map/ppermute | solution.py:12
  40.0 28.6 %collective-permute-start.9 = (bf16[128,2304]{1,0:T(8,128)(2,1)}, bf16[128,2304]{1,0:T(8,128)(2,1)}, u32[]{:S(2)}, u32[]{:S(2)}) collective-permute-start(bf16[128,2304]{1,0:T(8,128)(2,1)} %slice.123), channel_id=1, source_target_pairs={{0,1},{1,0},{2,3},{3,2},{4,5},{5,4},{6,7},{7,6},{8,9},{9,8},{10,11... | collective-permute-start | bytes 1769480 | tf_op jit(solution)/shard_map/ppermute | solution.py:20
  48.0 88.9 %collective-permute-start.14 = (bf16[512,2304]{1,0:T(8,128)(2,1)}, bf16[512,2304]{1,0:T(8,128)(2,1)}, u32[]{:S(2)}, u32[]{:S(2)}) collective-permute-start(bf16[512,2304]{1,0:T(8,128)(2,1)} %get-tuple-element.3), channel_id=1, source_target_pairs={{0,1},{1,0},{2,3},{3,2},{4,5},{5,4},{6,7},{7,6},{8,9},{9,8},{10,11... | collective-permute-start | bytes 7077896 | tf_op jit(solution)/shard_map/ppermute | solution.py:20
  48.0 26.1 %collective-permute-start.6 = (bf16[128,2432]{1,0:T(8,128)(2,1)}, bf16[128,2432]{1,0:T(8,128)(2,1)}, u32[]{:S(2)}, u32[]{:S(2)}) collective-permute-start(bf16[128,2432]{1,0:T(8,128)(2,1)} %constant_dynamic-update-slice_fusion), channel_id=1, source_target_pairs={{0,192},{64,0},{128,64},{192,128},{1,193},{65,1},{129,65},{193,129... | collective-permute-start | bytes 1867784 | tf_op jit(solution)/shard_map/ppermute | solution.py:12
  50.3 28.9 %collective-permute-start.12 = (bf16[128,2304]{1,0:T(8,128)(2,1)S(1)}, bf16[128,2304]{1,0:T(8,128)(2,1)}, u32[]{:S(2)}, u32[]{:S(2)}) collective-permute-start(bf16[128,2304]{1,0:T(8,128)(2,1)S(1)} %slice.126), channel_id=1, source_target_pairs={{0,1},{1,0},{2,3},{3,2},{4,5},{5,4},{6,7},{7,6},{8,9},{9,8},{10,11... | collective-permute-start | bytes 1769480 | tf_op jit(solution)/shard_map/ppermute | solution.py:20
  64.3 20.4 %collective-permute-start.11 = (bf16[128,2304]{1,0:T(8,128)(2,1)}, bf16[128,2304]{1,0:T(8,128)(2,1)}, u32[]{:S(2)}, u32[]{:S(2)}) collective-permute-start(bf16[128,2304]{1,0:T(8,128)(2,1)} %slice.125), channel_id=1, source_target_pairs={{0,1},{1,0},{2,3},{3,2},{4,5},{5,4},{6,7},{7,6},{8,9},{9,8},{10,11... | collective-permute-start | bytes 1769480 | tf_op jit(solution)/shard_map/ppermute | solution.py:20
  76.0 12.8 %collective-permute-start.10 = (bf16[128,2304]{1,0:T(8,128)(2,1)}, bf16[128,2304]{1,0:T(8,128)(2,1)}, u32[]{:S(2)}, u32[]{:S(2)}) collective-permute-start(bf16[128,2304]{1,0:T(8,128)(2,1)} %slice.124), channel_id=1, source_target_pairs={{0,1},{1,0},{2,3},{3,2},{4,5},{5,4},{6,7},{7,6},{8,9},{9,8},{10,11... | collective-permute-start | bytes 1769480 | tf_op jit(solution)/shard_map/ppermute | solution.py:20
  99.1 10.6 %all-to-all-start = ((f32[16,4,128]{2,1,0:T(4,128)}), f32[16,4,128]{2,1,0:T(4,128)}, u32[]{:S(2)}, u32[]{:S(2)}) async-start(f32[16,4,128]{2,1,0:T(4,128)} %broadcast_in_dim.52), calls=%async_computation | async-start | bytes 65536 | tf_op jit(solution)/shard_map/all_to_all | solution.py:86
  103.3 116.6 %all-gather.2.cloned.1.call-start = ((), (), s32[]{:S(2)}) async-start(), calls=%async_computation.1 | async-start | bytes 2396160 | tf_op jit(solution)/shard_map/all_gather | solution.py:51
  130.2 6.7 %collective-permute-start.13 = (bf16[512,512]{1,0:T(8,128)(2,1)}, bf16[512,512]{1,0:T(8,128)(2,1)S(1)}, u32[]{:S(2)}, u32[]{:S(2)}) collective-permute-start(bf16[512,512]{1,0:T(8,128)(2,1)} %fusion.9), channel_id=1, source_target_pairs={{0,1},{1,0},{2,3},{3,2},{4,5},{5,4},{6,7},{7,6},{8,9},{9,8},{10,11... | collective-permute-start | bytes 1572872 | tf_op jit(solution)/shard_map/ppermute | solution.py:20
  139.6 15.0 %collective-permute-start.17 = (bf16[128,2304]{1,0:T(8,128)(2,1)S(1)}, bf16[128,2304]{1,0:T(8,128)(2,1)S(1)}, u32[]{:S(2)}, u32[]{:S(2)}) collective-permute-start(bf16[128,2304]{1,0:T(8,128)(2,1)S(1)} %convolution_convert_fusion.1), channel_id=1, source_target_pairs={{0,192},{64,0},{128,64},{192,128},{1,193},{65,1},{129,65},{193,129... | collective-permute-start | bytes 1769480 | tf_op jit(solution)/shard_map/ppermute | solution.py:16
  143.1 16.2 %collective-permute-start.16 = (bf16[128,2304]{1,0:T(8,128)(2,1)S(1)}, bf16[128,2304]{1,0:T(8,128)(2,1)S(1)}, u32[]{:S(2)}, u32[]{:S(2)}) collective-permute-start(bf16[128,2304]{1,0:T(8,128)(2,1)S(1)} %convolution_convert_fusion.2), channel_id=1, source_target_pairs={{0,128},{64,192},{128,0},{192,64},{1,129},{65,193},{129,1},{193,65... | collective-permute-start | bytes 1769480 | tf_op jit(solution)/shard_map/ppermute | solution.py:16
  147.0 26.0 %collective-permute-start.15 = (bf16[128,2304]{1,0:T(8,128)(2,1)S(1)}, bf16[128,2304]{1,0:T(8,128)(2,1)S(1)}, u32[]{:S(2)}, u32[]{:S(2)}) collective-permute-start(bf16[128,2304]{1,0:T(8,128)(2,1)S(1)} %convolution_convert_fusion.3), channel_id=1, source_target_pairs={{0,64},{64,128},{128,192},{192,0},{1,65},{65,129},{129,193},{193,1... | collective-permute-start | bytes 1769480 | tf_op jit(solution)/shard_map/ppermute | solution.py:16
  175.5 6.4 %collective-permute-start.20 = (bf16[32,2304]{1,0:T(8,128)(2,1)S(1)}, bf16[32,2304]{1,0:T(8,128)(2,1)S(1)}, u32[]{:S(2)}, u32[]{:S(2)}) collective-permute-start(bf16[32,2304]{1,0:T(8,128)(2,1)S(1)} %get-tuple-element.5), channel_id=1, source_target_pairs={{0,12},{4,0},{8,4},{12,8},{1,13},{5,1},{9,5},{13,9},{2,14},{6,2},{... | collective-permute-start | bytes 442376 | tf_op jit(solution)/shard_map/ppermute | solution.py:16
  177.7 10.1 %collective-permute-start.18 = (bf16[32,2304]{1,0:T(8,128)(2,1)S(1)}, bf16[32,2304]{1,0:T(8,128)(2,1)S(1)}, u32[]{:S(2)}, u32[]{:S(2)}) collective-permute-start(bf16[32,2304]{1,0:T(8,128)(2,1)S(1)} %get-tuple-element.4), channel_id=1, source_target_pairs={{0,4},{4,8},{8,12},{12,0},{1,5},{5,9},{9,13},{13,1},{2,6},{6,10},{... | collective-permute-start | bytes 442376 | tf_op jit(solution)/shard_map/ppermute | solution.py:16
  187.9 9.1 %collective-permute-start.23 = (f32[8,2304]{1,0:T(8,128)S(1)}, f32[8,2304]{1,0:T(8,128)S(1)}, u32[]{:S(2)}, u32[]{:S(2)}) collective-permute-start(f32[8,2304]{1,0:T(8,128)S(1)} %get-tuple-element.8), channel_id=1, source_target_pairs={{0,48},{16,0},{32,16},{48,32},{1,49},{17,1},{33,17},{49,33},{2,50}... | collective-permute-start | bytes 221192 | tf_op jit(solution)/shard_map/ppermute | solution.py:16
  189.4 7.6 %collective-permute-start.22 = (f32[8,2304]{1,0:T(8,128)S(1)}, f32[8,2304]{1,0:T(8,128)S(1)}, u32[]{:S(2)}, u32[]{:S(2)}) collective-permute-start(f32[8,2304]{1,0:T(8,128)S(1)} %get-tuple-element.9), channel_id=1, source_target_pairs={{0,32},{16,48},{32,0},{48,16},{1,33},{17,49},{33,1},{49,17},{2,34}... | collective-permute-start | bytes 221192 | tf_op jit(solution)/shard_map/ppermute | solution.py:16
  191.9 8.0 %collective-permute-start.21 = (f32[8,2304]{1,0:T(8,128)S(1)}, f32[8,2304]{1,0:T(8,128)S(1)}, u32[]{:S(2)}, u32[]{:S(2)}) collective-permute-start(f32[8,2304]{1,0:T(8,128)S(1)} %get-tuple-element.7), channel_id=1, source_target_pairs={{0,16},{16,32},{32,48},{48,0},{1,17},{17,33},{33,49},{49,1},{2,18}... | collective-permute-start | bytes 221192 | tf_op jit(solution)/shard_map/ppermute | solution.py:16
  199.8 24.8 %collective-permute-start.24 = (f32[8,2304]{1,0:T(8,128)S(1)}, f32[8,2304]{1,0:T(8,128)S(1)}, u32[]{:S(2)}, u32[]{:S(2)}) collective-permute-start(f32[8,2304]{1,0:T(8,128)S(1)} %fusion.28), channel_id=1, source_target_pairs={{0,2},{2,0},{1,3},{3,1},{4,6},{6,4},{5,7},{7,5},{8,10},{10,8},{9,1... | collective-permute-start | bytes 221192 | tf_op jit(solution)/shard_map/ppermute | solution.py:20
  219.8 8.3 %collective-permute-start.26 = (bf16[512,2304]{1,0:T(8,128)(2,1)}, bf16[512,2304]{1,0:T(8,128)(2,1)S(1)}, u32[]{:S(2)}, u32[]{:S(2)}) collective-permute-start(bf16[512,2304]{1,0:T(8,128)(2,1)} %all-gather.2.cloned.1.call-done), channel_id=1, source_target_pairs={{0,1},{1,0},{2,3},{3,2},{4,5},{5,4},{6,7},{7,6},{8,9},{9,8},{10,11... | collective-permute-start | bytes 7077896 | tf_op jit(solution)/shard_map/ppermute | solution.py:20
  (21 other events, 136.2 us)
Sparse Core Ops, SparseCore 0:
  135.9 83.8 all-gather.1

commit v2 on v1

v2 whole, which is shorter than its diff:
```python
import functools

import jax
import jax.numpy as jnp
from jax import lax
from jax.experimental import pallas as pl
from jax.experimental.pallas import tpu as pltpu
from jax.sharding import Mesh, PartitionSpec as P

DP = ("x", "zh", "y")
AXES = ("x", "zh", "y", "zl", "c")
F32, BF16 = jnp.float32, jnp.bfloat16
VMEM_LIMIT = 56 * 1024 * 1024
INFO = 128
SLAB = 128
TILE = 768


def pull(value, axis, shift, size=4):
    return lax.ppermute(value, axis, [(i, (i - shift) % size) for i in range(size)])


def push(value, axis, shift, size=4):
    return lax.ppermute(value, axis, [(i, (i + shift) % size) for i in range(size)])


def swap(value, axis):
    return lax.ppermute(value, axis, [(0, 1), (1, 0)])


def digits(ids):
    return [ids // 65536, (ids // 256) % 256, ids % 256]


def info_columns(values):
    info = jnp.stack([v.astype(BF16) for v in values], 1)
    return jnp.pad(info, ((0, 0), (0, INFO - info.shape[1])))


def whole(core, own, other):
    return jnp.where(
        core == 0, jnp.concatenate([own, other], 1), jnp.concatenate([other, own], 1)
    )


def joined(info):
    info = info.astype(F32)
    return (info[:, 0:1] * 65536.0 + info[:, 1:2] * 256.0 + info[:, 2:3]).astype(jnp.int32)


def global_lane(place):
    r = lax.broadcasted_iota(jnp.int32, (SLAB, 1), 0)
    zh = (place[3] + (r // 8) % 4) % 4
    y = (place[2] + r // 32) % 4
    return zh * 32 + y * 8 + r % 8


def logits_kernel(shifts, place, *refs):
    n = len(shifts)
    own, other = refs[:n], refs[n : 2 * n]
    t_own, t_other, before, squash, expo, sums = refs[2 * n :]
    trans = (((1,), (1,)), ((), ()))

    @pl.when(pl.program_id(0) == 0)
    def _():
        sums[...] = before[...]

    acc = lax.dot_general(
        jnp.concatenate([s[...] for s in own], 0), t_own[...], trans, preferred_element_type=F32
    )
    acc += lax.dot_general(
        jnp.concatenate([s[...] for s in other], 0), t_other[...], trans, preferred_element_type=F32
    )
    q = jnp.tanh(acc * (1.0 / 30.0))
    e = jnp.exp(30.0 * q)
    squash[...] = q
    expo[...] = e
    lanes = lax.broadcasted_iota(jnp.int32, (SLAB, SLAB), 1)
    hit = lanes == global_lane(place)
    rows = lax.broadcasted_iota(jnp.int32, (4, SLAB), 0)
    add = jnp.zeros((4, SLAB), F32)
    for k, shift in enumerate(shifts):
        row = jnp.sum(e[k * SLAB : (k + 1) * SLAB], 1, keepdims=True)
        lane = jnp.sum(jnp.where(hit, row, 0.0), 0, keepdims=True)
        add = add + jnp.where(rows == (place[1] + shift) % 4, lane, 0.0)
    sums[...] += add


def logits_call(place, shifts, own, other, table, before):
    n, (rows, width) = len(shifts), table.shape
    half, tile = width // 2, rows // 2
    slab_spec = pl.BlockSpec((SLAB, half), lambda v, p: (0, 0))
    out = pl.BlockSpec((n * SLAB, tile), lambda v, p: (0, v))
    small = pl.BlockSpec((4, SLAB), lambda v, p: (0, 0))
    return pl.pallas_call(
        functools.partial(logits_kernel, shifts),
        grid_spec=pltpu.PrefetchScalarGridSpec(
            num_scalar_prefetch=1,
            grid=(rows // tile,),
            in_specs=[slab_spec] * (2 * n)
            + [
                pl.BlockSpec((tile, half), lambda v, p: (v, p[0])),
                pl.BlockSpec((tile, half), lambda v, p: (v, 1 - p[0])),
                small,
            ],
            out_specs=[out, out, small],
        ),
        out_shape=[
            jax.ShapeDtypeStruct((n * SLAB, rows), F32),
            jax.ShapeDtypeStruct((n * SLAB, rows), F32),
            jax.ShapeDtypeStruct((4, SLAB), F32),
        ],
        compiler_params=pltpu.CompilerParams(vmem_limit_bytes=VMEM_LIMIT),
    )(place, *own, *other, table, table, before)


def dlogit_kernel(place, i0, i1, i2, i3, q0, q1, e0, e1, total, out):
    hit_lane = lax.broadcasted_iota(jnp.int32, (SLAB, SLAB), 1) == global_lane(place)
    columns = place[4] + lax.broadcasted_iota(jnp.int32, (SLAB, out.shape[1]), 1)
    for d, info in enumerate((i0, i1, i2, i3)):
        q, e = (q0, e0) if d == 0 else (q1, e1)
        part = pl.ds(max(d - 1, 0) * SLAB, SLAB)
        tot = jnp.zeros((1, SLAB), F32)
        for k in range(4):
            tot = jnp.where((place[1] + d) % 4 == k, total[k : k + 1, :], tot)
        tot = jnp.sum(jnp.where(hit_lane, tot, 0.0), 1, keepdims=True)
        hits = (columns == joined(info[...])).astype(F32)
        weight = info[:, 3:4].astype(F32)
        s = q[part, :]
        out[pl.ds(d * SLAB, SLAB), :] = (
            weight * (e[part, :] / tot - hits) * (1.0 - s * s)
        ).astype(BF16)


def dlogit_call(place, slabs, q, e, total):
    rows, half = q[0].shape[1], slabs[0].shape[1] - INFO
    every = lambda a: pl.BlockSpec(a.shape, lambda i, p: (0, 0))
    return pl.pallas_call(
        dlogit_kernel,
        grid_spec=pltpu.PrefetchScalarGridSpec(
            num_scalar_prefetch=1,
            grid=(1,),
            in_specs=[pl.BlockSpec((SLAB, INFO), lambda i, p: (0, half // INFO))] * 4
            + [every(a) for a in (*q, *e, total)],
            out_specs=pl.BlockSpec((4 * SLAB, rows), lambda i, p: (0, 0)),
        ),
        out_shape=jax.ShapeDtypeStruct((4 * SLAB, rows), BF16),
        compiler_params=pltpu.CompilerParams(vmem_limit_bytes=VMEM_LIMIT),
    )(place, *slabs, *q, *e, total)


def hidden_grad_kernel(place, own, other, t_own, t_other, g0, g1, g2, g3):
    acc = jnp.dot(own[...], t_own[...], preferred_element_type=F32)
    acc += jnp.dot(other[...], t_other[...], preferred_element_type=F32)
    for d, g in enumerate((g0, g1, g2, g3)):
        g[...] = acc[d * SLAB : (d + 1) * SLAB].astype(g.dtype)


def hidden_grad_call(place, own, other, table, t_other):
    rows, half = t_other.shape
    steps = half // TILE
    full = pl.BlockSpec(own.shape, lambda j, p: (0, 0))
    return pl.pallas_call(
        hidden_grad_kernel,
        grid_spec=pltpu.PrefetchScalarGridSpec(
            num_scalar_prefetch=1,
            grid=(steps,),
            in_specs=[
                full,
                full,
                pl.BlockSpec((rows, TILE), lambda j, p: (0, p[0] * steps + j)),
                pl.BlockSpec((rows, TILE), lambda j, p: (0, j)),
            ],
            out_specs=[pl.BlockSpec((SLAB, TILE), lambda j, p: (0, j))] * 4,
        ),
        out_shape=[jax.ShapeDtypeStruct((SLAB, half), F32)]
        + [jax.ShapeDtypeStruct((SLAB, half), BF16)] * 3,
        compiler_params=pltpu.CompilerParams(vmem_limit_bytes=VMEM_LIMIT),
    )(place, own, other, table, t_other)


def table_grad_kernel(place, dlogit, i0, i1, i2, i3, *refs):
    blocks, out, turned = refs[:16], refs[16], refs[17]
    h, j = pl.program_id(0), pl.program_id(1)
    tokens, rows = dlogit.shape

    @pl.when((h == 0) & (j == 0))
    def _():
        turned[:, :tokens] = dlogit[...].T
        columns = place[4] + lax.broadcasted_iota(jnp.int32, (SLAB, rows), 1)
        for d, info in enumerate((i0, i1, i2, i3)):
            hit = (columns == joined(info[...])).astype(F32).astype(BF16)
            turned[:, tokens + d * SLAB : tokens + (d + 1) * SLAB] = hit.T

    def product(group):
        right = jnp.concatenate([r[...] for r in group], 0)
        out[...] = jnp.dot(turned[...], right, preferred_element_type=F32).astype(BF16)

    @pl.when(h == 0)
    def _():
        product(blocks[:8])

    @pl.when(h == 1)
    def _():
        product(blocks[8:])


def table_grad_call(place, dlogit, own, other):
    tokens, rows = dlogit.shape
    half = own[0].shape[1] - INFO
    steps = half // TILE
    first = pl.BlockSpec((SLAB, TILE), lambda h, j, p: (0, jnp.where(h == 0, j, steps - 1)))
    second = pl.BlockSpec((SLAB, TILE), lambda h, j, p: (0, jnp.where(h == 1, j, 0)))
    return pl.pallas_call(
        table_grad_kernel,
        grid_spec=pltpu.PrefetchScalarGridSpec(
            num_scalar_prefetch=1,
            grid=(2, steps),
            in_specs=[pl.BlockSpec((tokens, rows), lambda h, j, p: (0, 0))]
            + [pl.BlockSpec((SLAB, INFO), lambda h, j, p: (0, half // INFO))] * 4
            + [first] * 8
            + [second] * 8,
            out_specs=pl.BlockSpec(
                (rows, TILE),
                lambda h, j, p: (0, jnp.where(h == 0, p[0], 1 - p[0]) * steps + j),
            ),
            scratch_shapes=[pltpu.VMEM((rows, 2 * tokens), BF16)],
        ),
        out_shape=jax.ShapeDtypeStruct((rows, 2 * half), BF16),
        compiler_params=pltpu.CompilerParams(vmem_limit_bytes=VMEM_LIMIT),
    )(place, dlogit, *own[4:], *own, *other)


def body(hidden, table, target_ids, loss_weight, input_ids, emb_grad_in):
    own_rows, width = table.shape
    half = width // 2
    core = lax.axis_index("c")
    row_start = lax.axis_index(AXES) * own_rows
    place = jnp.stack(
        [core, lax.axis_index("x"), lax.axis_index("y"), lax.axis_index("zh"), row_start]
    ).astype(jnp.int32)

    def my_half(a):
        return lax.dynamic_slice_in_dim(a, core * half, half, 1)

    joint = jnp.concatenate(
        [
            my_half(hidden),
            info_columns(digits(target_ids) + [loss_weight]),
            my_half(emb_grad_in),
            info_columns(digits(input_ids)),
        ],
        1,
    )
    joint = [joint] + [pull(joint, "zh", d) for d in (1, 2, 3)]
    hid = jnp.concatenate([b[:, : half + INFO] for b in joint], 0)
    emb = jnp.concatenate([b[:, half + INFO :] for b in joint], 0)
    hid = jnp.concatenate([hid] + [pull(hid, "y", d) for d in (1, 2, 3)], 0)
    hids = [hid] + [pull(hid, "x", d) for d in (1, 2, 3)]
    emb = jnp.concatenate([emb] + [pull(emb, "x", d) for d in (1, 2, 3)], 0)
    embs = [emb] + [pull(emb, "y", d) for d in (1, 2, 3)]
    t_other = swap(lax.dynamic_slice_in_dim(table, (1 - core) * half, half, 1), "c")

    others = [swap(s, "c") for s in hids]
    q0, e0, sums = logits_call(
        place, (0,), hids[:1], others[:1], table, jnp.zeros((4, SLAB), F32)
    )
    q1, e1, sums = logits_call(place, (1, 2, 3), hids[1:], others[1:], table, sums)
    total = sums
    for axes in (("zh", "zl", "c"), ("x", "y")):
        total = jnp.sum(
            lax.all_to_all(jnp.broadcast_to(total, (16, 4, SLAB)), axes, 0, 0), 0
        )

    dlogit = dlogit_call(place, hids, (q0, q1), (e0, e1), total)
    acc, *parts = hidden_grad_call(place, dlogit, swap(dlogit, "c"), table, t_other)
    got = [push(p, "x", d) for p, d in zip(parts, (1, 2, 3))]
    acc = acc + got[0].astype(F32) + got[1].astype(F32) + got[2].astype(F32)
    got = [push(acc[32 * d : 32 * d + 32].astype(BF16), "y", d) for d in (1, 2, 3)]
    acc = acc[:32] + got[0].astype(F32) + got[1].astype(F32) + got[2].astype(F32)
    got = [push(acc[8 * d : 8 * d + 8], "zh", d) for d in (1, 2, 3)]
    acc = acc[:8] + got[0] + got[1] + got[2]
    acc = (acc + swap(acc, "zl")).astype(BF16)
    grad_hidden = whole(core, acc, swap(acc, "c"))

    emb_others = [swap(s, "c") for s in embs]
    grad_table = table_grad_call(place, dlogit, hids + embs, others + emb_others)
    return grad_hidden, grad_table


def solution(mesh):
    fine = Mesh(mesh.devices.reshape(4, 4, 4, 2, 2), AXES)
    rows, every = P(DP, None), P(AXES, None)
    return jax.shard_map(
        body,
        mesh=fine,
        in_specs=(rows, every, P(DP), P(DP), P(DP), rows),
        out_specs=(rows, every),
        check_vma=False,
    )
```

time: 249 us -> 224 us (0.90)
  matrix products: 40 us -> 0 us
  Pallas kernels: 0 us -> 35.3 us
  other arithmetic: 25 us -> 3.82 us
  starting transfers between devices: 57.5 us -> 71.6 us
  between operations: 14.3 us -> 0.89 us
  local copies, waits for them, and re-layouts: 21.6 us -> 8.28 us
  waiting for transfers between devices: 70.9 us -> 81.7 us
  blocking collectives: 18.9 us -> 22.2 us
    ppermute x9 -> x15, waiting for transfers between devices: 11.7 us -> 67.4 us  [pull(): lax.ppermute(value, axis, [(i, (i - shift) % size) for i in range(size)])]
    dot_general x9 -> x0, matrix products: 40 us -> none  [the longest x4 19.3 us: body(): lax.dot_general(f, table, (((1,), (1,)), ((), ())), preferred_element_typ...]
    pallas_call x0 -> x5, Pallas kernels: none -> 35.3 us  [the longest x1 12.6 us: table_grad_call(): pl.pallas_call(table_grad_kernel, grid_spec=pltpu.PrefetchScalarGridSpec(...]
    ppermute x9, waiting for transfers between devices: 35.4 us -> 10.9 us  [push(): lax.ppermute(value, axis, [(i, (i + shift) % size) for i in range(size)])]
    all_to_all x0 -> x2, blocking collectives: none -> 22.2 us  [body(): lax.all_to_all(jnp.broadcast_to(total, (16, 4, SLAB)), axes, 0, 0)]
    psum x2 -> x0, blocking collectives: 18.9 us -> none  [the longest x1 15.6 us: body(): total = lax.psum(jnp.sum(local, 0), ('zh', 'zl')).reshape(tokens)]
    all_gather x1 -> x0, waiting for transfers between devices: 17.7 us -> none  [body(): emb_half = lax.all_gather(my_half(emb_grad_in), DP, axis=0, tiled=True)]
    unnamed x5 -> x2, other arithmetic: 11.3 us -> 0.01 us
  transfers between devices with their start and end apart: 29 -> 36, of which waited for: 15 -> 15; matrix products, arithmetic and copies ran while one was open for 28% -> 3% of each run, Pallas kernels for 0% -> 13%
where the time goes in v2:
time: 224 us
  waiting for transfers between devices  81.7 us (36%)
  starting transfers between devices  71.6 us (32%)
  Pallas kernels  35.3 us (16%)
  blocking collectives  22.2 us (10%)
  local copies, waits for them, and re-layouts  8.28 us (4%)
  other arithmetic  3.82 us (2%)
    ppermute x15, waiting for transfers between devices, pull(): lax.ppermute(value, axis, [(i, (i - shift) % size) for i in range(size)])  67.4 us
    ppermute x12, starting transfers between devices, swap(): return lax.ppermute(value, axis, [(0, 1), (1, 0)])  35.1 us
    ppermute x15, starting transfers between devices, pull(): lax.ppermute(value, axis, [(i, (i - shift) % size) for i in range(size)])  26.2 us
    all_to_all x2, blocking collectives, body(): lax.all_to_all(jnp.broadcast_to(total, (16, 4, SLAB)), axes, 0, 0)  22.2 us
    pallas_call x1, Pallas kernels, table_grad_call(): pl.pallas_call(table_grad_kernel, grid_spec=pltpu.PrefetchScalarGridSpec(...  12.6 us
    pallas_call x2, Pallas kernels, logits_call(): pl.pallas_call(functools.partial(logits_kernel, shifts), grid_spec=pltpu....  12 us
    ppermute x9, waiting for transfers between devices, push(): lax.ppermute(value, axis, [(i, (i + shift) % size) for i in range(size)])  10.9 us
    ppermute x9, starting transfers between devices, push(): lax.ppermute(value, axis, [(i, (i + shift) % size) for i in range(size)])  10.3 us
  transfers between devices with their start and end apart: 36, of which 15 were waited for; matrix products, arithmetic and copies ran while one was open for 3% of the time, Pallas kernels for 13%

profile of v2, /device:TPU:1, one launch (start us, length us, event | category | flops | bytes accessed | tf_op | source)
XLA Modules:
  0.0 223.7 jit_solution(16128438046940315631)
XLA Ops:
  3.6 6.9 %collective-permute-start = (bf16[8,4864]{1,0:T(8,128)(2,1)S(1)}, bf16[8,4864]{1,0:T(8,128)(2,1)S(1)}, u32[]{:S(2)}, u32[]{:S(2)}) collective-permute-start(bf16[8,4864]{1,0:T(8,128)(2,1)S(1)} %pad_maximum_fusion.2), channel_id=1, source_target_pairs={{0,48},{16,0},{32,16},{48,32},{1,49},{17,1},{33,17},{49,33},{2,50}... | collective-permute-start | bytes 233480 | tf_op jit(solution)/shard_map/ppermute | solution.py:20
  13.8 4.1 %collective-permute-done.1 = bf16[8,4864]{1,0:T(8,128)(2,1)S(1)} collective-permute-done((bf16[8,4864]{1,0:T(8,128)(2,1)S(1)}, bf16[8,4864]{1,0:T(8,128)(2,1)S(1)}, u32[]{:S(2)}, u32[]{:S(2)}) %collective-permute-start.1) | collective-permute-done | bytes 77856 | tf_op jit(solution)/shard_map/ppermute | solution.py:20
  18.9 2.8 %collective-permute-start.3 = (bf16[32,2432]{1,0:T(8,128)(2,1)S(1)}, bf16[32,2432]{1,0:T(8,128)(2,1)S(1)}, u32[]{:S(2)}, u32[]{:S(2)}) collective-permute-start(bf16[32,2432]{1,0:T(8,128)(2,1)S(1)} %pad_maximum_fusion), channel_id=1, source_target_pairs={{0,12},{4,0},{8,4},{12,8},{1,13},{5,1},{9,5},{13,9},{2,14},{6,2},{... | collective-permute-start | bytes 466952 | tf_op jit(solution)/shard_map/ppermute | solution.py:20
  21.7 3.2 %constant_dynamic-slice_fusion = bf16[512,2304]{1,0:T(8,128)(2,1)} fusion(bf16[512,4608]{1,0:T(8,128)(2,1)} %t_own.1, s32[]{:T(128)S(6)} %select_n.58), kind=kLoop, calls=%fused_computation.62 | loop fusion | bytes 4718596 | tf_op jit(solution)/shard_map/dynamic_slice | solution.py:262
  24.9 2.9 %collective-permute-start.14 = (bf16[512,2304]{1,0:T(8,128)(2,1)}, bf16[512,2304]{1,0:T(8,128)(2,1)}, u32[]{:S(2)}, u32[]{:S(2)}) collective-permute-start(bf16[512,2304]{1,0:T(8,128)(2,1)} %constant_dynamic-slice_fusion), channel_id=1, source_target_pairs={{0,1},{1,0},{2,3},{3,2},{4,5},{5,4},{6,7},{7,6},{8,9},{9,8},{10,11... | collective-permute-start | bytes 7077896 | tf_op jit(solution)/shard_map/ppermute | solution.py:28
  28.9 6.1 %collective-permute-done.4 = bf16[32,2432]{1,0:T(8,128)(2,1)S(1)} collective-permute-done((bf16[32,2432]{1,0:T(8,128)(2,1)S(1)}, bf16[32,2432]{1,0:T(8,128)(2,1)S(1)}, u32[]{:S(2)}, u32[]{:S(2)}) %collective-permute-start.4) | collective-permute-done | bytes 155680 | tf_op jit(solution)/shard_map/ppermute | solution.py:20
  35.0 3.6 %collective-permute-done.5 = bf16[32,2432]{1,0:T(8,128)(2,1)S(1)} collective-permute-done((bf16[32,2432]{1,0:T(8,128)(2,1)S(1)}, bf16[32,2432]{1,0:T(8,128)(2,1)S(1)}, u32[]{:S(2)}, u32[]{:S(2)}) %collective-permute-start.5) | collective-permute-done | bytes 155680 | tf_op jit(solution)/shard_map/ppermute | solution.py:20
  38.6 2.6 %collective-permute-start.6 = (bf16[128,2432]{1,0:T(8,128)(2,1)S(1)}, bf16[128,2432]{1,0:T(8,128)(2,1)S(1)}, u32[]{:S(2)}, u32[]{:S(2)}) collective-permute-start(bf16[128,2432]{1,0:T(8,128)(2,1)S(1)} %constant_dynamic-update-slice_fusion.refs_0_.i0), channel_id=1, source_target_pairs={{0,192},{64,0},{128,64},{192,128},{1,193},{65,1},{129,65},{193,129... | collective-permute-start | bytes 1867784 | tf_op jit(solution)/shard_map/ppermute | solution.py:20
  43.6 11.3 %collective-permute-done.6.refs_0_.i1.refs_1_ = bf16[128,2432]{1,0:T(8,128)(2,1)S(1)} collective-permute-done((bf16[128,2432]{1,0:T(8,128)(2,1)S(1)}, bf16[128,2432]{1,0:T(8,128)(2,1)S(1)}, u32[]{:S(2)}, u32[]{:S(2)}) %collective-permute-start.6) | collective-permute-done | bytes 622624 | tf_op jit(solution)/shard_map/ppermute | solution.py:20
  54.9 13.9 %collective-permute-start.10 = (bf16[128,2432]{1,0:T(8,128)(2,1)S(1)}, bf16[128,2432]{1,0:T(8,128)(2,1)}, u32[]{:S(2)}, u32[]{:S(2)}) collective-permute-start(bf16[128,2432]{1,0:T(8,128)(2,1)S(1)} %collective-permute-done.6.refs_0_.i1.refs_1_), channel_id=1, source_target_pairs={{0,1},{1,0},{2,3},{3,2},{4,5},{5,4},{6,7},{7,6},{8,9},{9,8},{10,11... | collective-permute-start | bytes 1867784 | tf_op jit(solution)/shard_map/ppermute | solution.py:28
  68.9 3.1 %collective-permute-done.8.refs_2_.i3.refs_3_ = bf16[128,2432]{1,0:T(8,128)(2,1)S(1)} collective-permute-done((bf16[128,2432]{1,0:T(8,128)(2,1)S(1)}, bf16[128,2432]{1,0:T(8,128)(2,1)S(1)}, u32[]{:S(2)}, u32[]{:S(2)}) %collective-permute-start.8) | collective-permute-done | bytes 622624 | tf_op jit(solution)/shard_map/ppermute | solution.py:20
  73.7 5.3 %shard_map.77 = (f32[128,512]{1,0:T(8,128)}, f32[128,512]{1,0:T(8,128)}, f32[4,128]{1,0:T(4,128)}) custom-call(s32[5]{0:T(128)} %stack.50.place, bf16[128,2432]{1,0:T(8,128)(2,1)} %copy-done, bf16[128,2432]{1,0:T(8,128)(2,1)} %collective-permute-done.9.refs_1_.refs_8_, bf16[512,4608]{1,0:T(8,128)(2,1)} %t_own.1, bf16[512,4608]{1,0:T(8,128)(2,1)} %t_own.1, ...), custom_call_target="tpu_custom_call" | custom-call | tf_op jit(solution)/shard_map/pallas_call | solution.py:95
  79.0 6.7 %shard_map.78 = (f32[384,512]{1,0:T(8,128)}, f32[384,512]{1,0:T(8,128)}, f32[4,128]{1,0:T(4,128)}) custom-call(s32[5]{0:T(128)} %stack.50.place, bf16[128,2432]{1,0:T(8,128)(2,1)} %copy-done.1, bf16[128,2432]{1,0:T(8,128)(2,1)} %copy-done.2, bf16[128,2432]{1,0:T(8,128)(2,1)} %copy-done.3, bf16[128,2432]{1,0:T(8,128)(2,1)} %collective-permute-done.10.refs_3_.refs_9_, ...), custom_call_target="tpu_custom_call" | custom-call | tf_op jit(solution)/shard_map/pallas_call | solution.py:95
  86.4 13.2 %all_to_all.10 = f32[16,4,128]{2,1,0:T(4,128)S(1)} all-to-all(f32[16,4,128]{2,1,0:T(4,128)S(1)} %broadcast_in_dim.10), channel_id=1, replica_groups=mesh['x'=4,'zh'=4,'y'=4,'zl'=2,'c'=2] {'zh','zl','c'}, dimensions={0} | all-to-all | bytes 65536 | tf_op jit(solution)/shard_map/all_to_all | solution.py:272
  99.6 9.0 %all_to_all.11 = f32[16,4,128]{2,1,0:T(4,128)S(1)} all-to-all(f32[16,4,128]{2,1,0:T(4,128)S(1)} %broadcast_in_dim.11), channel_id=1, replica_groups=mesh['x'=4,'zh'=4,'y'=4,'zl'=2,'c'=2] {'x','y'}, dimensions={0} | all-to-all | bytes 65536 | tf_op jit(solution)/shard_map/all_to_all | solution.py:272
  109.2 3.7 %shard_map.79.own.dlogit = bf16[512,512]{1,0:T(8,128)(2,1)} custom-call(s32[5]{0:T(128)} %stack.50.place, bf16[128,2432]{1,0:T(8,128)(2,1)} %copy-done, bf16[128,2432]{1,0:T(8,128)(2,1)} %copy-done.1, bf16[128,2432]{1,0:T(8,128)(2,1)} %copy-done.2, bf16[128,2432]{1,0:T(8,128)(2,1)} %copy-done.3, f32[128,512]{1,0:T(8,128)} %get-tuple-element.12.q0, ...), custom_call_target="tpu_custom_call" | custom-call | tf_op jit(solution)/shard_map/pallas_call | solution.py:138
  117.1 6.9 %shard_map.80 = (f32[128,2304]{1,0:T(8,128)}, bf16[128,2304]{1,0:T(8,128)(2,1)}, bf16[128,2304]{1,0:T(8,128)(2,1)}, bf16[128,2304]{1,0:T(8,128)(2,1)}) custom-call(s32[5]{0:T(128)} %stack.50.place, bf16[512,512]{1,0:T(8,128)(2,1)} %shard_map.79.own.dlogit, bf16[512,512]{1,0:T(8,128)(2,1)} %copy-done.9, bf16[512,4608]{1,0:T(8,128)(2,1)} %t_own.1, ...), custom_call_target="tpu_custom_call" | custom-call | tf_op jit(solution)/shard_map/pallas_call | solution.py:163
  129.4 27.3 %collective-permute-done.26 = bf16[32,2432]{1,0:T(8,128)(2,1)S(1)} collective-permute-done((bf16[32,2432]{1,0:T(8,128)(2,1)S(1)}, bf16[32,2432]{1,0:T(8,128)(2,1)S(1)}, u32[]{:S(2)}, u32[]{:S(2)}) %collective-permute-start.26) | collective-permute-done | bytes 155680 | tf_op jit(solution)/shard_map/ppermute | solution.py:20
  163.3 3.3 %collective-permute-done.18 = bf16[32,2304]{1,0:T(8,128)(2,1)S(1)} collective-permute-done((bf16[32,2304]{1,0:T(8,128)(2,1)S(1)}, bf16[32,2304]{1,0:T(8,128)(2,1)S(1)}, u32[]{:S(2)}, u32[]{:S(2)}) %collective-permute-start.18) | collective-permute-done | bytes 147488 | tf_op jit(solution)/shard_map/ppermute | solution.py:24
  173.9 3.6 %collective-permute-start.29 = (bf16[128,2432]{1,0:T(8,128)(2,1)S(1)}, bf16[128,2432]{1,0:T(8,128)(2,1)S(1)}, u32[]{:S(2)}, u32[]{:S(2)}) collective-permute-start(bf16[128,2432]{1,0:T(8,128)(2,1)S(1)} %constant_dynamic-update-slice_fusion.6.i0.refs_4_), channel_id=1, source_target_pairs={{0,12},{4,0},{8,4},{12,8},{1,13},{5,1},{9,5},{13,9},{2,14},{6,2},{... | collective-permute-start | bytes 1867784 | tf_op jit(solution)/shard_map/ppermute | solution.py:20
  178.2 4.6 %collective-permute-done.23 = f32[8,2304]{1,0:T(8,128)S(1)} collective-permute-done((f32[8,2304]{1,0:T(8,128)S(1)}, f32[8,2304]{1,0:T(8,128)S(1)}, u32[]{:S(2)}, u32[]{:S(2)}) %collective-permute-start.23) | collective-permute-done | bytes 73760 | tf_op jit(solution)/shard_map/ppermute | solution.py:24
  183.9 8.4 %collective-permute-done.29.i1.refs_5_ = bf16[128,2432]{1,0:T(8,128)(2,1)S(1)} collective-permute-done((bf16[128,2432]{1,0:T(8,128)(2,1)S(1)}, bf16[128,2432]{1,0:T(8,128)(2,1)S(1)}, u32[]{:S(2)}, u32[]{:S(2)}) %collective-permute-start.29) | collective-permute-done | bytes 622624 | tf_op jit(solution)/shard_map/ppermute | solution.py:20
  192.4 12.7 %collective-permute-start.33 = (bf16[128,2432]{1,0:T(8,128)(2,1)S(1)}, bf16[128,2432]{1,0:T(8,128)(2,1)}, u32[]{:S(2)}, u32[]{:S(2)}) collective-permute-start(bf16[128,2432]{1,0:T(8,128)(2,1)S(1)} %collective-permute-done.29.i1.refs_5_), channel_id=1, source_target_pairs={{0,1},{1,0},{2,3},{3,2},{4,5},{5,4},{6,7},{7,6},{8,9},{9,8},{10,11... | collective-permute-start | bytes 1867784 | tf_op jit(solution)/shard_map/ppermute | solution.py:28
  210.4 12.6 %shard_map.81 = bf16[512,4608]{1,0:T(8,128)(2,1)} custom-call(s32[5]{0:T(128)} %stack.50.place, bf16[512,512]{1,0:T(8,128)(2,1)} %shard_map.79.own.dlogit, bf16[128,2432]{1,0:T(8,128)(2,1)} %copy-done.4, bf16[128,2432]{1,0:T(8,128)(2,1)} %copy-done.5, bf16[128,2432]{1,0:T(8,128)(2,1)} %copy-done.6, bf16[128,2432]{1,0:T(8,128)(2,1)} %copy-done.7, ...), custom_call_target="tpu_custom_call" | custom-call | tf_op jit(solution)/shard_map/pallas_call | solution.py:214
  (114 shorter events, 44.9 us)
Async XLA Ops:
  3.6 10.2 %collective-permute-start = (bf16[8,4864]{1,0:T(8,128)(2,1)S(1)}, bf16[8,4864]{1,0:T(8,128)(2,1)S(1)}, u32[]{:S(2)}, u32[]{:S(2)}) collective-permute-start(bf16[8,4864]{1,0:T(8,128)(2,1)S(1)} %pad_maximum_fusion.2), channel_id=1, source_target_pairs={{0,48},{16,0},{32,16},{48,32},{1,49},{17,1},{33,17},{49,33},{2,50}... | collective-permute-start | bytes 233480 | tf_op jit(solution)/shard_map/ppermute | solution.py:20
  18.9 9.9 %collective-permute-start.3 = (bf16[32,2432]{1,0:T(8,128)(2,1)S(1)}, bf16[32,2432]{1,0:T(8,128)(2,1)S(1)}, u32[]{:S(2)}, u32[]{:S(2)}) collective-permute-start(bf16[32,2432]{1,0:T(8,128)(2,1)S(1)} %pad_maximum_fusion), channel_id=1, source_target_pairs={{0,12},{4,0},{8,4},{12,8},{1,13},{5,1},{9,5},{13,9},{2,14},{6,2},{... | collective-permute-start | bytes 466952 | tf_op jit(solution)/shard_map/ppermute | solution.py:20
  24.9 91.3 %collective-permute-start.14 = (bf16[512,2304]{1,0:T(8,128)(2,1)}, bf16[512,2304]{1,0:T(8,128)(2,1)}, u32[]{:S(2)}, u32[]{:S(2)}) collective-permute-start(bf16[512,2304]{1,0:T(8,128)(2,1)} %constant_dynamic-slice_fusion), channel_id=1, source_target_pairs={{0,1},{1,0},{2,3},{3,2},{4,5},{5,4},{6,7},{7,6},{8,9},{9,8},{10,11... | collective-permute-start | bytes 7077896 | tf_op jit(solution)/shard_map/ppermute | solution.py:28
  28.1 10.5 %collective-permute-start.5 = (bf16[32,2432]{1,0:T(8,128)(2,1)S(1)}, bf16[32,2432]{1,0:T(8,128)(2,1)S(1)}, u32[]{:S(2)}, u32[]{:S(2)}) collective-permute-start(bf16[32,2432]{1,0:T(8,128)(2,1)S(1)} %pad_maximum_fusion), channel_id=1, source_target_pairs={{0,4},{4,8},{8,12},{12,0},{1,5},{5,9},{9,13},{13,1},{2,6},{6,10},{... | collective-permute-start | bytes 466952 | tf_op jit(solution)/shard_map/ppermute | solution.py:20
  38.6 16.3 %collective-permute-start.6 = (bf16[128,2432]{1,0:T(8,128)(2,1)S(1)}, bf16[128,2432]{1,0:T(8,128)(2,1)S(1)}, u32[]{:S(2)}, u32[]{:S(2)}) collective-permute-start(bf16[128,2432]{1,0:T(8,128)(2,1)S(1)} %constant_dynamic-update-slice_fusion.refs_0_.i0), channel_id=1, source_target_pairs={{0,192},{64,0},{128,64},{192,128},{1,193},{65,1},{129,65},{193,129... | collective-permute-start | bytes 1867784 | tf_op jit(solution)/shard_map/ppermute | solution.py:20
  41.2 27.6 %collective-permute-start.7 = (bf16[128,2432]{1,0:T(8,128)(2,1)S(1)}, bf16[128,2432]{1,0:T(8,128)(2,1)S(1)}, u32[]{:S(2)}, u32[]{:S(2)}) collective-permute-start(bf16[128,2432]{1,0:T(8,128)(2,1)S(1)} %constant_dynamic-update-slice_fusion.refs_0_.i0), channel_id=1, source_target_pairs={{0,128},{64,192},{128,0},{192,64},{1,129},{65,193},{129,1},{193,65... | collective-permute-start | bytes 1867784 | tf_op jit(solution)/shard_map/ppermute | solution.py:20
  41.7 30.3 %collective-permute-start.8 = (bf16[128,2432]{1,0:T(8,128)(2,1)S(1)}, bf16[128,2432]{1,0:T(8,128)(2,1)S(1)}, u32[]{:S(2)}, u32[]{:S(2)}) collective-permute-start(bf16[128,2432]{1,0:T(8,128)(2,1)S(1)} %constant_dynamic-update-slice_fusion.refs_0_.i0), channel_id=1, source_target_pairs={{0,64},{64,128},{128,192},{192,0},{1,65},{65,129},{129,193},{193,1... | collective-permute-start | bytes 1867784 | tf_op jit(solution)/shard_map/ppermute | solution.py:20
  42.3 30.8 %collective-permute-start.9 = (bf16[128,2432]{1,0:T(8,128)(2,1)S(1)}, bf16[128,2432]{1,0:T(8,128)(2,1)}, u32[]{:S(2)}, u32[]{:S(2)}) collective-permute-start(bf16[128,2432]{1,0:T(8,128)(2,1)S(1)} %constant_dynamic-update-slice_fusion.refs_0_.i0), channel_id=1, source_target_pairs={{0,1},{1,0},{2,3},{3,2},{4,5},{5,4},{6,7},{7,6},{8,9},{9,8},{10,11... | collective-permute-start | bytes 1867784 | tf_op jit(solution)/shard_map/ppermute | solution.py:28
  54.9 24.1 %collective-permute-start.10 = (bf16[128,2432]{1,0:T(8,128)(2,1)S(1)}, bf16[128,2432]{1,0:T(8,128)(2,1)}, u32[]{:S(2)}, u32[]{:S(2)}) collective-permute-start(bf16[128,2432]{1,0:T(8,128)(2,1)S(1)} %collective-permute-done.6.refs_0_.i1.refs_1_), channel_id=1, source_target_pairs={{0,1},{1,0},{2,3},{3,2},{4,5},{5,4},{6,7},{7,6},{8,9},{9,8},{10,11... | collective-permute-start | bytes 1867784 | tf_op jit(solution)/shard_map/ppermute | solution.py:28
  68.8 10.2 %collective-permute-start.11 = (bf16[128,2432]{1,0:T(8,128)(2,1)S(1)}, bf16[128,2432]{1,0:T(8,128)(2,1)}, u32[]{:S(2)}, u32[]{:S(2)}) collective-permute-start(bf16[128,2432]{1,0:T(8,128)(2,1)S(1)} %collective-permute-done.7.refs_1_.i2.refs_2_), channel_id=1, source_target_pairs={{0,1},{1,0},{2,3},{3,2},{4,5},{5,4},{6,7},{7,6},{8,9},{9,8},{10,11... | collective-permute-start | bytes 1867784 | tf_op jit(solution)/shard_map/ppermute | solution.py:28
  124.0 34.6 %collective-permute-start.15 = (bf16[128,2304]{1,0:T(8,128)(2,1)}, bf16[128,2304]{1,0:T(8,128)(2,1)S(1)}, u32[]{:S(2)}, u32[]{:S(2)}) collective-permute-start(bf16[128,2304]{1,0:T(8,128)(2,1)} %get-tuple-element.19), channel_id=1, source_target_pairs={{0,64},{64,128},{128,192},{192,0},{1,65},{65,129},{129,193},{193,1... | collective-permute-start | bytes 1769480 | tf_op jit(solution)/shard_map/ppermute | solution.py:24
  124.3 34.3 %collective-permute-start.16 = (bf16[128,2304]{1,0:T(8,128)(2,1)}, bf16[128,2304]{1,0:T(8,128)(2,1)S(1)}, u32[]{:S(2)}, u32[]{:S(2)}) collective-permute-start(bf16[128,2304]{1,0:T(8,128)(2,1)} %get-tuple-element.20), channel_id=1, source_target_pairs={{0,128},{64,192},{128,0},{192,64},{1,129},{65,193},{129,1},{193,65... | collective-permute-start | bytes 1769480 | tf_op jit(solution)/shard_map/ppermute | solution.py:24
  126.0 32.6 %collective-permute-start.17 = (bf16[128,2304]{1,0:T(8,128)(2,1)}, bf16[128,2304]{1,0:T(8,128)(2,1)S(1)}, u32[]{:S(2)}, u32[]{:S(2)}) collective-permute-start(bf16[128,2304]{1,0:T(8,128)(2,1)} %get-tuple-element.21), channel_id=1, source_target_pairs={{0,192},{64,0},{128,64},{192,128},{1,193},{65,1},{129,65},{193,129... | collective-permute-start | bytes 1769480 | tf_op jit(solution)/shard_map/ppermute | solution.py:24
  127.0 29.7 %collective-permute-start.26 = (bf16[32,2432]{1,0:T(8,128)(2,1)S(1)}, bf16[32,2432]{1,0:T(8,128)(2,1)S(1)}, u32[]{:S(2)}, u32[]{:S(2)}) collective-permute-start(bf16[32,2432]{1,0:T(8,128)(2,1)S(1)} %pad_maximum_fusion.1), channel_id=1, source_target_pairs={{0,192},{64,0},{128,64},{192,128},{1,193},{65,1},{129,65},{193,129... | collective-permute-start | bytes 466952 | tf_op jit(solution)/shard_map/ppermute | solution.py:20
  127.6 35.7 %collective-permute-start.27 = (bf16[32,2432]{1,0:T(8,128)(2,1)S(1)}, bf16[32,2432]{1,0:T(8,128)(2,1)S(1)}, u32[]{:S(2)}, u32[]{:S(2)}) collective-permute-start(bf16[32,2432]{1,0:T(8,128)(2,1)S(1)} %pad_maximum_fusion.1), channel_id=1, source_target_pairs={{0,128},{64,192},{128,0},{192,64},{1,129},{65,193},{129,1},{193,65... | collective-permute-start | bytes 466952 | tf_op jit(solution)/shard_map/ppermute | solution.py:20
  156.7 17.2 %collective-permute-start.28 = (bf16[32,2432]{1,0:T(8,128)(2,1)S(1)}, bf16[32,2432]{1,0:T(8,128)(2,1)S(1)}, u32[]{:S(2)}, u32[]{:S(2)}) collective-permute-start(bf16[32,2432]{1,0:T(8,128)(2,1)S(1)} %pad_maximum_fusion.1), channel_id=1, source_target_pairs={{0,64},{64,128},{128,192},{192,0},{1,65},{65,129},{129,193},{193,1... | collective-permute-start | bytes 466952 | tf_op jit(solution)/shard_map/ppermute | solution.py:20
  172.2 10.6 %collective-permute-start.23 = (f32[8,2304]{1,0:T(8,128)S(1)}, f32[8,2304]{1,0:T(8,128)S(1)}, u32[]{:S(2)}, u32[]{:S(2)}) collective-permute-start(f32[8,2304]{1,0:T(8,128)S(1)} %get-tuple-element.28), channel_id=1, source_target_pairs={{0,48},{16,0},{32,16},{48,32},{1,49},{17,1},{33,17},{49,33},{2,50}... | collective-permute-start | bytes 221192 | tf_op jit(solution)/shard_map/ppermute | solution.py:24
  173.9 18.5 %collective-permute-start.29 = (bf16[128,2432]{1,0:T(8,128)(2,1)S(1)}, bf16[128,2432]{1,0:T(8,128)(2,1)S(1)}, u32[]{:S(2)}, u32[]{:S(2)}) collective-permute-start(bf16[128,2432]{1,0:T(8,128)(2,1)S(1)} %constant_dynamic-update-slice_fusion.6.i0.refs_4_), channel_id=1, source_target_pairs={{0,12},{4,0},{8,4},{12,8},{1,13},{5,1},{9,5},{13,9},{2,14},{6,2},{... | collective-permute-start | bytes 1867784 | tf_op jit(solution)/shard_map/ppermute | solution.py:20
  177.5 27.6 %collective-permute-start.30 = (bf16[128,2432]{1,0:T(8,128)(2,1)S(1)}, bf16[128,2432]{1,0:T(8,128)(2,1)S(1)}, u32[]{:S(2)}, u32[]{:S(2)}) collective-permute-start(bf16[128,2432]{1,0:T(8,128)(2,1)S(1)} %constant_dynamic-update-slice_fusion.6.i0.refs_4_), channel_id=1, source_target_pairs={{0,8},{4,12},{8,0},{12,4},{1,9},{5,13},{9,1},{13,5},{2,10},{6,14},... | collective-permute-start | bytes 1867784 | tf_op jit(solution)/shard_map/ppermute | solution.py:20
  177.5 30.1 %collective-permute-start.31 = (bf16[128,2432]{1,0:T(8,128)(2,1)S(1)}, bf16[128,2432]{1,0:T(8,128)(2,1)S(1)}, u32[]{:S(2)}, u32[]{:S(2)}) collective-permute-start(bf16[128,2432]{1,0:T(8,128)(2,1)S(1)} %constant_dynamic-update-slice_fusion.6.i0.refs_4_), channel_id=1, source_target_pairs={{0,4},{4,8},{8,12},{12,0},{1,5},{5,9},{9,13},{13,1},{2,6},{6,10},{... | collective-permute-start | bytes 1867784 | tf_op jit(solution)/shard_map/ppermute | solution.py:20
  182.8 25.7 %collective-permute-start.24 = (f32[8,2304]{1,0:T(8,128)S(1)}, f32[8,2304]{1,0:T(8,128)S(1)}, u32[]{:S(2)}, u32[]{:S(2)}) collective-permute-start(f32[8,2304]{1,0:T(8,128)S(1)} %fusion.3), channel_id=1, source_target_pairs={{0,2},{2,0},{1,3},{3,1},{4,6},{6,4},{5,7},{7,5},{8,10},{10,8},{9,1... | collective-permute-start | bytes 221192 | tf_op jit(solution)/shard_map/ppermute | solution.py:28
  182.9 25.7 %collective-permute-start.32 = (bf16[128,2432]{1,0:T(8,128)(2,1)S(1)}, bf16[128,2432]{1,0:T(8,128)(2,1)S(1)}, u32[]{:S(2)}, u32[]{:S(2)}) collective-permute-start(bf16[128,2432]{1,0:T(8,128)(2,1)S(1)} %constant_dynamic-update-slice_fusion.6.i0.refs_4_), channel_id=1, source_target_pairs={{0,1},{1,0},{2,3},{3,2},{4,5},{5,4},{6,7},{7,6},{8,9},{9,8},{10,11... | collective-permute-start | bytes 1867784 | tf_op jit(solution)/shard_map/ppermute | solution.py:28
  192.4 16.3 %collective-permute-start.33 = (bf16[128,2432]{1,0:T(8,128)(2,1)S(1)}, bf16[128,2432]{1,0:T(8,128)(2,1)}, u32[]{:S(2)}, u32[]{:S(2)}) collective-permute-start(bf16[128,2432]{1,0:T(8,128)(2,1)S(1)} %collective-permute-done.29.i1.refs_5_), channel_id=1, source_target_pairs={{0,1},{1,0},{2,3},{3,2},{4,5},{5,4},{6,7},{7,6},{8,9},{9,8},{10,11... | collective-permute-start | bytes 1867784 | tf_op jit(solution)/shard_map/ppermute | solution.py:28
  208.6 14.5 %collective-permute-start.25 = (bf16[8,2304]{1,0:T(8,128)(2,1)S(1)}, bf16[8,2304]{1,0:T(8,128)(2,1)S(1)}, u32[]{:S(2)}, u32[]{:S(2)}) collective-permute-start(bf16[8,2304]{1,0:T(8,128)(2,1)S(1)} %add_convert_fusion), channel_id=1, source_target_pairs={{0,1},{1,0},{2,3},{3,2},{4,5},{5,4},{6,7},{7,6},{8,9},{9,8},{10,11... | collective-permute-start | bytes 110600 | tf_op jit(solution)/shard_map/ppermute | solution.py:28
  (22 other events, 217.3 us)

commit v3 on v2

v3 whole, which is shorter than its diff:
```python
import functools

import jax
import jax.numpy as jnp
from jax import lax
from jax.experimental import pallas as pl
from jax.experimental.pallas import tpu as pltpu
from jax.sharding import Mesh, PartitionSpec as P

DP = ("x", "zh", "y")
AXES = ("x", "zh", "y", "zl", "c")
F32, BF16 = jnp.float32, jnp.bfloat16
VMEM_LIMIT = 56 * 1024 * 1024
INFO = 128
SLAB = 128
TILE = 768


def pull(value, axis, shift, size=4):
    return lax.ppermute(value, axis, [(i, (i - shift) % size) for i in range(size)])


def push(value, axis, shift, size=4):
    return lax.ppermute(value, axis, [(i, (i + shift) % size) for i in range(size)])


def swap(value, axis):
    return lax.ppermute(value, axis, [(0, 1), (1, 0)])


def digits(ids):
    return [ids // 65536, (ids // 256) % 256, ids % 256]


def info_columns(values):
    info = jnp.stack([v.astype(BF16) for v in values], 1)
    return jnp.pad(info, ((0, 0), (0, INFO - info.shape[1])))


def whole(core, own, other):
    return jnp.where(
        core == 0, jnp.concatenate([own, other], 1), jnp.concatenate([other, own], 1)
    )


def joined(info):
    info = info.astype(F32)
    return (info[:, 0:1] * 65536.0 + info[:, 1:2] * 256.0 + info[:, 2:3]).astype(jnp.int32)


def global_lane(place):
    r = lax.broadcasted_iota(jnp.int32, (SLAB, 1), 0)
    zh = (place[3] + (r // 8) % 4) % 4
    y = (place[2] + r // 32) % 4
    return zh * 32 + y * 8 + r % 8


def logits_kernel(shifts, place, *refs):
    n = len(shifts)
    own, other, infos = refs[:n], refs[n : 2 * n], refs[2 * n : 3 * n]
    t_own, t_other, before, squash, expo, slope, sums = refs[3 * n :]
    trans = (((1,), (1,)), ((), ()))
    step, tile = pl.program_id(0), expo.shape[1]

    @pl.when(step == 0)
    def _():
        sums[...] = before[...]

    acc = lax.dot_general(
        jnp.concatenate([s[...] for s in own], 0), t_own[...], trans, preferred_element_type=F32
    )
    acc += lax.dot_general(
        jnp.concatenate([s[...] for s in other], 0), t_other[...], trans, preferred_element_type=F32
    )
    q = jnp.tanh(acc * (1.0 / 30.0))
    e = jnp.exp(30.0 * q)
    squash[...] = q
    expo[...] = e
    columns = place[4] + step * tile + lax.broadcasted_iota(jnp.int32, (SLAB, tile), 1)
    hit_lane = lax.broadcasted_iota(jnp.int32, (SLAB, SLAB), 1) == global_lane(place)
    rows = lax.broadcasted_iota(jnp.int32, (8, SLAB), 0)
    add = jnp.zeros((8, SLAB), F32)
    for k, shift in enumerate(shifts):
        part = slice(k * SLAB, (k + 1) * SLAB)
        hits = columns == joined(infos[k][...])
        qk, ek = q[part], e[part]
        slope[part, :] = jnp.where(hits, 0.0, ek * (1.0 - qk * qk)).astype(BF16)
        at = (place[1] + shift) % 4
        for base, values in ((0, ek), (4, jnp.where(hits, qk, 0.0))):
            row = jnp.sum(values, 1, keepdims=True)
            lane = jnp.sum(jnp.where(hit_lane, row, 0.0), 0, keepdims=True)
            add = add + jnp.where(rows == at + base, lane, 0.0)
    sums[...] += add


def logits_call(place, shifts, own, other, table, before):
    n, (rows, width) = len(shifts), table.shape
    half, tile = width // 2, rows // 2
    slab_spec = pl.BlockSpec((SLAB, half), lambda v, p: (0, 0))
    out = pl.BlockSpec((n * SLAB, tile), lambda v, p: (0, v))
    small = pl.BlockSpec((8, SLAB), lambda v, p: (0, 0))
    return pl.pallas_call(
        functools.partial(logits_kernel, shifts),
        grid_spec=pltpu.PrefetchScalarGridSpec(
            num_scalar_prefetch=1,
            grid=(rows // tile,),
            in_specs=[slab_spec] * (2 * n)
            + [pl.BlockSpec((SLAB, INFO), lambda v, p: (0, half // INFO))] * n
            + [
                pl.BlockSpec((tile, half), lambda v, p: (v, p[0])),
                pl.BlockSpec((tile, half), lambda v, p: (v, 1 - p[0])),
                small,
            ],
            out_specs=[out, out, out, small],
        ),
        out_shape=[
            jax.ShapeDtypeStruct((n * SLAB, rows), F32),
            jax.ShapeDtypeStruct((n * SLAB, rows), F32),
            jax.ShapeDtypeStruct((n * SLAB, rows), BF16),
            jax.ShapeDtypeStruct((8, SLAB), F32),
        ],
        compiler_params=pltpu.CompilerParams(vmem_limit_bytes=VMEM_LIMIT),
        cost_estimate=cost(n * SLAB * rows * width),
        name="logits",
    )(place, *own, *other, *own, table, table, before)


def cost(macs):
    return pl.CostEstimate(flops=4 * macs, bytes_accessed=10_000_000, transcendentals=0)


def dlogit_kernel(place, *refs):
    infos, embs = refs[:4], refs[4:8]
    q0, q1, e0, e1, total, turned = refs[8:]
    hit_lane = lax.broadcasted_iota(jnp.int32, (SLAB, SLAB), 1) == global_lane(place)
    columns = place[4] + lax.broadcasted_iota(jnp.int32, (SLAB, turned.shape[0]), 1)
    for d in range(4):
        q, e = (q0, e0) if d == 0 else (q1, e1)
        part = pl.ds(max(d - 1, 0) * SLAB, SLAB)
        tot = jnp.zeros((1, SLAB), F32)
        for k in range(4):
            tot = jnp.where((place[1] + d) % 4 == k, total[k : k + 1, :], tot)
        tot = jnp.sum(jnp.where(hit_lane, tot, 0.0), 1, keepdims=True)
        hits = (columns == joined(infos[d][...])).astype(F32)
        weight = infos[d][:, 3:4].astype(F32)
        s = q[part, :]
        value = (weight * (e[part, :] / tot - hits) * (1.0 - s * s)).astype(BF16)
        turned[:, d * SLAB : (d + 1) * SLAB] = value.T
        hit = (columns == joined(embs[d][...])).astype(F32).astype(BF16)
        turned[:, (4 + d) * SLAB : (5 + d) * SLAB] = hit.T


def dlogit_call(place, slabs, embs, q, e, total):
    rows, half = q[0].shape[1], slabs[0].shape[1] - INFO
    every = lambda a: pl.BlockSpec(a.shape, lambda i, p: (0, 0))
    return pl.pallas_call(
        dlogit_kernel,
        grid_spec=pltpu.PrefetchScalarGridSpec(
            num_scalar_prefetch=1,
            grid=(1,),
            in_specs=[pl.BlockSpec((SLAB, INFO), lambda i, p: (0, half // INFO))] * 8
            + [every(a) for a in (*q, *e, total)],
            out_specs=pl.BlockSpec((rows, 8 * SLAB), lambda i, p: (0, 0)),
        ),
        out_shape=jax.ShapeDtypeStruct((rows, 8 * SLAB), BF16),
        compiler_params=pltpu.CompilerParams(vmem_limit_bytes=VMEM_LIMIT),
        cost_estimate=cost(1 << 29),
        name="dlogit",
    )(place, *slabs, *embs, *q, *e, total)


def slope_product_kernel(place, own, other, t_own, t_other, *outs):
    acc = jnp.dot(own[...], t_own[...], preferred_element_type=F32)
    acc += jnp.dot(other[...], t_other[...], preferred_element_type=F32)
    for d, g in enumerate(outs):
        g[...] = acc[d * SLAB : (d + 1) * SLAB].astype(g.dtype)


def pick_kernel(place, info, t_own, t_other, *refs):
    outs, mine, theirs = refs[:4], refs[4], refs[5]

    @pl.when(pl.program_id(0) == 0)
    def _():
        ids = joined(info[...])
        columns = lax.broadcasted_iota(jnp.int32, mine.shape, 1)
        mine[...] = (columns + place[4] == ids).astype(F32).astype(BF16)
        theirs[...] = (columns + place[5] == ids).astype(F32).astype(BF16)

    acc = jnp.dot(mine[...], t_own[...], preferred_element_type=F32)
    acc += jnp.dot(theirs[...], t_other[...], preferred_element_type=F32)
    for d, g in enumerate(outs):
        g[...] = acc[d * SLAB : (d + 1) * SLAB].astype(g.dtype)


def table_product(kernel, place, left, table, t_other, outs, scratch, name):
    rows, half = t_other.shape
    steps = half // TILE
    return pl.pallas_call(
        kernel,
        grid_spec=pltpu.PrefetchScalarGridSpec(
            num_scalar_prefetch=1,
            grid=(steps,),
            in_specs=[pl.BlockSpec(a.shape, lambda j, p: (0, 0)) for a in left]
            + [
                pl.BlockSpec((rows, TILE), lambda j, p: (0, p[0] * steps + j)),
                pl.BlockSpec((rows, TILE), lambda j, p: (0, j)),
            ],
            out_specs=[pl.BlockSpec((SLAB, TILE), lambda j, p: (0, j))] * len(outs),
            scratch_shapes=scratch,
        ),
        out_shape=[jax.ShapeDtypeStruct((SLAB, half), t) for t in outs],
        compiler_params=pltpu.CompilerParams(vmem_limit_bytes=VMEM_LIMIT),
        cost_estimate=cost(len(outs) * SLAB * 2 * rows * half),
        name=name,
    )(place, *left, table, t_other)


def table_grad_kernel(place, turned, *refs):
    blocks, out = refs[:8], refs[-1]
    right = jnp.concatenate([r[...] for r in blocks], 0)
    out[...] = jnp.dot(turned[...], right, preferred_element_type=F32).astype(BF16)


def table_grad_call(place, turned, slabs, other, before=None):
    rows, half = turned.shape[0], slabs[0].shape[1] - INFO
    steps = half // TILE
    return pl.pallas_call(
        table_grad_kernel,
        grid_spec=pltpu.PrefetchScalarGridSpec(
            num_scalar_prefetch=1,
            grid=(steps,),
            in_specs=[pl.BlockSpec(turned.shape, lambda j, p: (0, 0))]
            + [pl.BlockSpec((SLAB, TILE), lambda j, p: (0, j))] * 8
            + ([] if before is None else [pl.BlockSpec(memory_space=pl.ANY)]),
            out_specs=pl.BlockSpec(
                (rows, TILE),
                lambda j, p: (0, (1 - p[0] if other else p[0]) * steps + j),
            ),
        ),
        out_shape=jax.ShapeDtypeStruct((rows, 2 * half), BF16),
        input_output_aliases={} if before is None else {10: 0},
        compiler_params=pltpu.CompilerParams(vmem_limit_bytes=VMEM_LIMIT),
        cost_estimate=cost(rows * 8 * SLAB * half),
        name="table_grad",
    )(place, turned, *slabs, *([] if before is None else [before]))


def body(hidden, table, target_ids, loss_weight, input_ids, emb_grad_in):
    own_rows, width = table.shape
    half = width // 2
    core, ax, ay, az = (lax.axis_index(n) for n in ("c", "x", "y", "zh"))
    row_start = lax.axis_index(AXES) * own_rows
    place = jnp.stack(
        [core, ax, ay, az, row_start, row_start + (1 - 2 * core) * own_rows]
    ).astype(jnp.int32)

    def my_half(a):
        return lax.dynamic_slice_in_dim(a, core * half, half, 1)

    joint = jnp.concatenate(
        [
            my_half(hidden),
            info_columns(digits(target_ids) + [loss_weight]),
            my_half(emb_grad_in),
            info_columns(digits(input_ids)),
        ],
        1,
    )
    joint = [joint] + [pull(joint, "zh", d) for d in (1, 2, 3)]
    hid = jnp.concatenate([b[:, : half + INFO] for b in joint], 0)
    emb = jnp.concatenate([b[:, half + INFO :] for b in joint], 0)
    hid = [hid] + [pull(hid, "y", d) for d in (1, 2, 3)]
    emb = [emb] + [pull(emb, "x", d) for d in (1, 2, 3)]
    t_other = swap(lax.dynamic_slice_in_dim(table, (1 - core) * half, half, 1), "c")
    hid, emb, t_other = lax.optimization_barrier((hid, emb, t_other))
    hid, emb = jnp.concatenate(hid, 0), jnp.concatenate(emb, 0)
    hids = [pull(hid, "x", d) for d in (1, 2, 3)]
    embs = [pull(emb, "y", d) for d in (1, 2, 3)]

    hid_other = swap(hid, "c")
    q0, e0, slope0, sums = logits_call(
        place, (0,), [hid], [hid_other], table, jnp.zeros((8, SLAB), F32)
    )
    hids, embs, sums = lax.optimization_barrier((hids, embs, sums))
    others = [swap(s, "c") for s in hids]
    q1, e1, slope1, sums = logits_call(place, (1, 2, 3), hids, others, table, sums)
    hids, embs, others = [hid] + hids, [emb] + embs, [hid_other] + others

    parts = table_product(
        slope_product_kernel, place, [slope1, swap(slope1, "c")], table, t_other,
        [BF16] * 3, [], "slope_product",
    )
    got = [push(p, "x", d) for p, d in zip(parts, (1, 2, 3))]
    info = jnp.concatenate([s[:, half:].reshape(4, 32, INFO) for s in hids], 1)
    pick, *parts = table_product(
        pick_kernel, place, [info.reshape(4 * SLAB, INFO)], table, t_other,
        [BF16] * 4, [pltpu.VMEM((4 * SLAB, own_rows), BF16)] * 2, "pick",
    )
    got_pick = [push(p, "y", d) for p, d in zip(parts, (1, 2, 3))]
    (mean,) = table_product(
        slope_product_kernel, place, [slope0, swap(slope0, "c")], table, t_other,
        [F32], [], "slope_product",
    )

    total = sums
    for axes in (("zh", "zl", "c"), ("x", "y")):
        total = jnp.sum(
            lax.all_to_all(jnp.broadcast_to(total, (16, 8, SLAB)), axes, 0, 0), 0
        )

    mean = mean + got[0].astype(F32) + got[1].astype(F32) + got[2].astype(F32)
    pick = pick + got_pick[0] + got_pick[1] + got_pick[2]
    got = [push(mean[32 * d : 32 * d + 32].astype(BF16), "y", d) for d in (1, 2, 3)]
    got_pick = [push(pick[32 * d : 32 * d + 32], "x", d) for d in (1, 2, 3)]
    mean = mean[:32] + got[0].astype(F32) + got[1].astype(F32) + got[2].astype(F32)
    pick = pick[:32] + got_pick[0] + got_pick[1] + got_pick[2]
    both = jnp.concatenate([mean.astype(BF16), pick], 1)
    got = [push(both[8 * d : 8 * d + 8], "zh", d).astype(F32) for d in (1, 2, 3)]
    mean = mean[:8] + got[0][:, :half] + got[1][:, :half] + got[2][:, :half]
    pick = pick[:8].astype(F32) + got[0][:, half:] + got[1][:, half:] + got[2][:, half:]

    flat = total.reshape(8 * SLAB)
    start = (ax * 16 + az * 4 + ay) * 8
    norm = lax.dynamic_slice_in_dim(flat, start, 8, 0)
    s = lax.dynamic_slice_in_dim(flat, 4 * SLAB + start, 8, 0)
    weight = loss_weight.astype(F32)
    at_target = weight * (jnp.exp(30.0 * s) / norm - 1.0) * (1.0 - s * s)
    acc = mean * (weight / norm)[:, None] + pick * at_target[:, None]
    acc = (acc + swap(acc, "zl")).astype(BF16)
    grad_hidden = whole(core, acc, swap(acc, "c"))

    turned = dlogit_call(place, hids, embs, (q0, q1), (e0, e1), total)
    emb_others = [swap(s, "c") for s in embs]
    grad_table = table_grad_call(place, turned, hids + embs, 0)
    grad_table = table_grad_call(place, turned, others + emb_others, 1, grad_table)
    return grad_hidden, grad_table


def solution(mesh):
    fine = Mesh(mesh.devices.reshape(4, 4, 4, 2, 2), AXES)
    rows, every = P(DP, None), P(AXES, None)
    return jax.shard_map(
        body,
        mesh=fine,
        in_specs=(rows, every, P(DP), P(DP), P(DP), rows),
        out_specs=(rows, every),
        check_vma=False,
    )
```

time: 224 us -> 254 us (1.13); the launches traced: 224 us -> 249 us
  blocking collectives: 22.2 us -> 0 us
  Pallas kernels: 35.3 us -> 50.7 us
  starting transfers between devices: 71.6 us -> 84.4 us
  waiting for transfers between devices: 81.7 us -> 93.6 us
  local copies, waits for them, and re-layouts: 8.28 us -> 13.8 us
    ppermute x9 -> x15, waiting for transfers between devices: 10.9 us -> 52.6 us  [push(): lax.ppermute(value, axis, [(i, (i + shift) % size) for i in range(size)])]
    ppermute x15, waiting for transfers between devices: 67.4 us -> 35.5 us  [pull(): lax.ppermute(value, axis, [(i, (i - shift) % size) for i in range(size)])]
    all_to_all x2 -> x0, blocking collectives: 22.2 us -> none  [body(): lax.all_to_all(jnp.broadcast_to(total, (16, 4, SLAB)), axes, 0, 0)]
    ppermute x12 -> x13, starting transfers between devices: 35.1 us -> 17.6 us  [swap(): return lax.ppermute(value, axis, [(0, 1), (1, 0)])]
    ppermute x9 -> x15, starting transfers between devices: 10.3 us -> 26 us  [push(): lax.ppermute(value, axis, [(i, (i + shift) % size) for i in range(size)])]
    pallas_call x1 -> x3, Pallas kernels: 6.9 us -> 18.7 us  [table_product(): pl.pallas_call(kernel, grid_spec=pltpu.PrefetchScalarGridSpec(num_scalar_...]
    all_to_all x0 -> x2, starting transfers between devices: none -> 10.3 us  [body(): lax.all_to_all(jnp.broadcast_to(total, (16, 8, SLAB)), axes, 0, 0)]
    unnamed x24 -> x44, local copies, waits for them, and re-layouts: 0.92 us -> 5.92 us
  transfers between devices with their start and end apart: 36 -> 45, of which waited for: 15 -> 19; matrix products, arithmetic and copies ran while one was open for 3% -> 4% of each run, Pallas kernels for 13% -> 18%
where the time goes in v3:
time: 254 us; the launch traced here: 249 us
  waiting for transfers between devices  93.6 us (37%)
  starting transfers between devices  84.4 us (33%)
  Pallas kernels  50.7 us (20%)
  local copies, waits for them, and re-layouts  13.8 us (5%)
  other arithmetic  5.43 us (2%)
    ppermute x15, waiting for transfers between devices, push(): lax.ppermute(value, axis, [(i, (i + shift) % size) for i in range(size)])  52.6 us
    ppermute x15, waiting for transfers between devices, pull(): lax.ppermute(value, axis, [(i, (i - shift) % size) for i in range(size)])  35.5 us
    ppermute x15, starting transfers between devices, pull(): lax.ppermute(value, axis, [(i, (i - shift) % size) for i in range(size)])  30.5 us
    ppermute x15, starting transfers between devices, push(): lax.ppermute(value, axis, [(i, (i + shift) % size) for i in range(size)])  26 us
    pallas_call x3, Pallas kernels, table_product(): pl.pallas_call(kernel, grid_spec=pltpu.PrefetchScalarGridSpec(num_scalar_...  18.7 us
    ppermute x13, starting transfers between devices, swap(): return lax.ppermute(value, axis, [(0, 1), (1, 0)])  17.6 us
    pallas_call x2, Pallas kernels, table_grad_call(): pl.pallas_call(table_grad_kernel, grid_spec=pltpu.PrefetchScalarGridSpec(...  14.3 us
    pallas_call x2, Pallas kernels, logits_call(): pl.pallas_call(functools.partial(logits_kernel, shifts), grid_spec=pltpu....  12.4 us
  transfers between devices with their start and end apart: 45, of which 19 were waited for; matrix products, arithmetic and copies ran while one was open for 4% of the time, Pallas kernels for 18%

profile of v3, /device:TPU:1, one launch (start us, length us, event | category | flops | bytes accessed | tf_op | source)
XLA Modules:
  0.0 249.2 jit_solution(10996997816506683857)
XLA Ops:
  7.5 5.1 %collective-permute-start.1 = (bf16[8,4864]{1,0:T(8,128)(2,1)S(1)}, bf16[8,4864]{1,0:T(8,128)(2,1)S(1)}, u32[]{:S(2)}, u32[]{:S(2)}) collective-permute-start(bf16[8,4864]{1,0:T(8,128)(2,1)S(1)} %pad_maximum_fusion.3), channel_id=1, source_target_pairs={{0,32},{16,48},{32,0},{48,16},{1,33},{17,49},{33,1},{49,17},{2,34}... | collective-permute-start | bytes 233480 | tf_op jit(solution)/shard_map/ppermute | solution.py:20
  35.8 4.6 %collective-permute-done.8 = bf16[32,2432]{1,0:T(8,128)(2,1)S(1)} collective-permute-done((bf16[32,2432]{1,0:T(8,128)(2,1)S(1)}, bf16[32,2432]{1,0:T(8,128)(2,1)S(1)}, u32[]{:S(2)}, u32[]{:S(2)}) %collective-permute-start.8) | collective-permute-done | bytes 155680 | tf_op jit(solution)/shard_map/ppermute | solution.py:20
  54.7 4.5 %collective-permute-start.17 = (bf16[128,2432]{1,0:T(8,128)(2,1)}, bf16[128,2432]{1,0:T(8,128)(2,1)}, u32[]{:S(2)}, u32[]{:S(2)}) collective-permute-start(bf16[128,2432]{1,0:T(8,128)(2,1)} %constant_dynamic-update-slice_fusion.4.refs_4_), channel_id=1, source_target_pairs={{0,4},{4,8},{8,12},{12,0},{1,5},{5,9},{9,13},{13,1},{2,6},{6,10},{... | collective-permute-start | bytes 1867784 | tf_op jit(solution)/shard_map/ppermute | solution.py:20
  60.4 5.4 %logits.2 = (f32[128,512]{1,0:T(8,128)}, f32[128,512]{1,0:T(8,128)}, bf16[128,512]{1,0:T(8,128)(2,1)}, f32[8,128]{1,0:T(8,128)}) custom-call(s32[6]{0:T(128)} %stack.54.place, bf16[128,2432]{1,0:T(8,128)(2,1)} %copy-done, bf16[128,2432]{1,0:T(8,128)(2,1)} %copy-done.9, bf16[128,2432]{1,0:T(8,128)(2,1)} %copy-done, bf16[512,4608]{1,0:T(8,128)(2,1)} %t_own.5, ...), custom_call_target="tpu_custom_call" | custom-call | flops 1207959552 | bytes 10000000 | tf_op jit(solution)/shard_map/logits/pallas_call | solution.py:102
  65.9 5.7 %collective-permute-done.14.refs_2_.refs_8_.refs_3_ = bf16[128,2432]{1,0:T(8,128)(2,1)S(1)} collective-permute-done((bf16[128,2432]{1,0:T(8,128)(2,1)S(1)}, bf16[128,2432]{1,0:T(8,128)(2,1)S(1)}, u32[]{:S(2)}, u32[]{:S(2)}) %collective-permute-start.14) | collective-permute-done | bytes 622624 | tf_op jit(solution)/shard_map/ppermute | solution.py:20
  71.6 7.1 %collective-permute-done.15.refs_5_ = bf16[128,2432]{1,0:T(8,128)(2,1)} collective-permute-done((bf16[128,2432]{1,0:T(8,128)(2,1)}, bf16[128,2432]{1,0:T(8,128)(2,1)}, u32[]{:S(2)}, u32[]{:S(2)}) %collective-permute-start.15) | collective-permute-done | bytes 622624 | tf_op jit(solution)/shard_map/ppermute | solution.py:20
  78.7 7.1 %collective-permute-done.17.refs_7_ = bf16[128,2432]{1,0:T(8,128)(2,1)} collective-permute-done((bf16[128,2432]{1,0:T(8,128)(2,1)}, bf16[128,2432]{1,0:T(8,128)(2,1)}, u32[]{:S(2)}, u32[]{:S(2)}) %collective-permute-start.17) | collective-permute-done | bytes 622624 | tf_op jit(solution)/shard_map/ppermute | solution.py:20
  86.5 7.0 %pick.1 = (bf16[128,2304]{1,0:T(8,128)(2,1)}, bf16[128,2304]{1,0:T(8,128)(2,1)}, bf16[128,2304]{1,0:T(8,128)(2,1)}, bf16[128,2304]{1,0:T(8,128)(2,1)}) custom-call(s32[6]{0:T(128)} %stack.54.place, bf16[512,128]{1,0:T(8,128)(2,1)} %bitcast.25, bf16[512,4608]{1,0:T(8,128)(2,1)} %t_own.5, bf16[512,2304]{1,0:T(8,128)(2,1)} %copy-done.5), custom_call_target="tpu_custom_call" | custom-call | flops 4831838208 | bytes 10000000 | tf_op jit(solution)/shard_map/pick/pallas_call | solution.py:198
  97.7 5.4 %slope_product.2 = f32[128,2304]{1,0:T(8,128)} custom-call(s32[6]{0:T(128)} %stack.54.place, bf16[128,512]{1,0:T(8,128)(2,1)} %get-tuple-element.37.own, bf16[128,512]{1,0:T(8,128)(2,1)} %copy-done.13, bf16[512,4608]{1,0:T(8,128)(2,1)} %t_own.5, bf16[512,2304]{1,0:T(8,128)(2,1)} %copy-done.5), custom_call_target="tpu_custom_call" | custom-call | flops 1207959552 | bytes 10000000 | tf_op jit(solution)/shard_map/slope_product/pallas_call | solution.py:198
  103.1 5.0 %collective-permute-done.30 = bf16[128,2304]{1,0:T(8,128)(2,1)S(1)} collective-permute-done((bf16[128,2304]{1,0:T(8,128)(2,1)}, bf16[128,2304]{1,0:T(8,128)(2,1)S(1)}, u32[]{:S(2)}, u32[]{:S(2)}) %collective-permute-start.30) | collective-permute-done | bytes 589856 | tf_op jit(solution)/shard_map/ppermute | solution.py:24
  112.6 10.7 %collective-permute-done.28 = bf16[128,2304]{1,0:T(8,128)(2,1)} collective-permute-done((bf16[128,2304]{1,0:T(8,128)(2,1)}, bf16[128,2304]{1,0:T(8,128)(2,1)}, u32[]{:S(2)}, u32[]{:S(2)}) %collective-permute-start.28) | collective-permute-done | bytes 589856 | tf_op jit(solution)/shard_map/ppermute | solution.py:24
  127.0 7.0 %logits.3 = (f32[384,512]{1,0:T(8,128)}, f32[384,512]{1,0:T(8,128)}, bf16[384,512]{1,0:T(8,128)(2,1)}, f32[8,128]{1,0:T(8,128)}) custom-call(s32[6]{0:T(128)} %stack.54.place, bf16[128,2432]{1,0:T(8,128)(2,1)} %copy-done.1, bf16[128,2432]{1,0:T(8,128)(2,1)} %copy-done.2, bf16[128,2432]{1,0:T(8,128)(2,1)} %copy-done.3, bf16[128,2432]{1,0:T(8,128)(2,1)} %copy-done.6, ...), custom_call_target="tpu_custom_call" | custom-call | flops 3623878656 | bytes 10000000 | tf_op jit(solution)/shard_map/logits/pallas_call | solution.py:102
  135.4 5.2 %all-to-all-start = ((f32[16,8,128]{2,1,0:T(8,128)}), f32[16,8,128]{2,1,0:T(8,128)S(1)}, u32[]{:S(2)}, u32[]{:S(2)}) async-start(f32[16,8,128]{2,1,0:T(8,128)} %broadcast_in_dim.12), calls=%async_computation | async-start | bytes 131072 | tf_op jit(solution)/shard_map/all_to_all | solution.py:308
  143.7 4.6 %all-to-all-done = f32[16,8,128]{2,1,0:T(8,128)S(1)} async-done(((f32[16,8,128]{2,1,0:T(8,128)}), f32[16,8,128]{2,1,0:T(8,128)S(1)}, u32[]{:S(2)}, u32[]{:S(2)}) %all-to-all-start) | async-done | bytes 65568 | tf_op jit(solution)/shard_map/all_to_all | solution.py:308
  149.0 5.2 %all-to-all-start.1 = ((f32[16,8,128]{2,1,0:T(8,128)}), f32[16,8,128]{2,1,0:T(8,128)S(1)}, u32[]{:S(2)}, u32[]{:S(2)}) async-start(f32[16,8,128]{2,1,0:T(8,128)} %broadcast_in_dim.13), calls=%async_computation.1 | async-start | bytes 131072 | tf_op jit(solution)/shard_map/all_to_all | solution.py:308
  154.2 10.6 %collective-permute-start.31 = (bf16[32,2304]{1,0:T(8,128)(2,1)S(1)}, bf16[32,2304]{1,0:T(8,128)(2,1)S(1)}, u32[]{:S(2)}, u32[]{:S(2)}) collective-permute-start(bf16[32,2304]{1,0:T(8,128)(2,1)S(1)} %get-tuple-element.71), channel_id=1, source_target_pairs={{0,64},{64,128},{128,192},{192,0},{1,65},{65,129},{129,193},{193,1... | collective-permute-start | bytes 442376 | tf_op jit(solution)/shard_map/ppermute | solution.py:24
  164.8 6.3 %slope_product.3 = (bf16[128,2304]{1,0:T(8,128)(2,1)}, bf16[128,2304]{1,0:T(8,128)(2,1)}, bf16[128,2304]{1,0:T(8,128)(2,1)}) custom-call(s32[6]{0:T(128)} %stack.54.place, bf16[384,512]{1,0:T(8,128)(2,1)} %get-tuple-element.48.own, bf16[384,512]{1,0:T(8,128)(2,1)} %copy-done.18, bf16[512,4608]{1,0:T(8,128)(2,1)} %t_own.5, bf16[512,2304]{1,0:T(8,128)(2,1)} %copy-done.5), custom_call_target="tpu_custom_call" | custom-call | flops 3623878656 | bytes 10000000 | tf_op jit(solution)/shard_map/slope_product/pallas_call | solution.py:198
  174.5 10.8 %collective-permute-done.24 = bf16[128,2304]{1,0:T(8,128)(2,1)S(1)} collective-permute-done((bf16[128,2304]{1,0:T(8,128)(2,1)}, bf16[128,2304]{1,0:T(8,128)(2,1)S(1)}, u32[]{:S(2)}, u32[]{:S(2)}) %collective-permute-start.24) | collective-permute-done | bytes 589856 | tf_op jit(solution)/shard_map/ppermute | solution.py:24
  188.2 14.0 %collective-permute-done.22 = bf16[128,2304]{1,0:T(8,128)(2,1)} collective-permute-done((bf16[128,2304]{1,0:T(8,128)(2,1)}, bf16[128,2304]{1,0:T(8,128)(2,1)}, u32[]{:S(2)}, u32[]{:S(2)}) %collective-permute-start.22) | collective-permute-done | bytes 589856 | tf_op jit(solution)/shard_map/ppermute | solution.py:24
  207.7 4.5 %collective-permute-done.27 = bf16[32,2304]{1,0:T(8,128)(2,1)S(1)} collective-permute-done((bf16[32,2304]{1,0:T(8,128)(2,1)S(1)}, bf16[32,2304]{1,0:T(8,128)(2,1)S(1)}, u32[]{:S(2)}, u32[]{:S(2)}) %collective-permute-start.27) | collective-permute-done | bytes 147488 | tf_op jit(solution)/shard_map/ppermute | solution.py:24
  212.5 4.3 %collective-permute-done.25 = bf16[32,2304]{1,0:T(8,128)(2,1)S(1)} collective-permute-done((bf16[32,2304]{1,0:T(8,128)(2,1)S(1)}, bf16[32,2304]{1,0:T(8,128)(2,1)S(1)}, u32[]{:S(2)}, u32[]{:S(2)}) %collective-permute-start.25) | collective-permute-done | bytes 147488 | tf_op jit(solution)/shard_map/ppermute | solution.py:24
  220.6 5.4 %dlogit.1.turned = bf16[512,1024]{1,0:T(8,128)(2,1)} custom-call(s32[6]{0:T(128)} %stack.54.place, bf16[128,2432]{1,0:T(8,128)(2,1)} %copy-done, bf16[128,2432]{1,0:T(8,128)(2,1)} %copy-done.1, bf16[128,2432]{1,0:T(8,128)(2,1)} %copy-done.2, bf16[128,2432]{1,0:T(8,128)(2,1)} %copy-done.3, bf16[128,2432]{1,0:T(8,128)(2,1)} %constant_dynamic-update-slice_fusion.4.refs_4_, ...), custom_call_target="tpu_custom_call" | custom-call | flops 2147483648 | bytes 10000000 | tf_op jit(solution)/shard_map/dlogit/pallas_call | solution.py:156
  231.5 7.1 %table_grad.2.refs_8_ = bf16[512,4608]{1,0:T(8,128)(2,1)} custom-call(s32[6]{0:T(128)} %stack.54.place, bf16[512,1024]{1,0:T(8,128)(2,1)} %dlogit.1.turned, bf16[128,2432]{1,0:T(8,128)(2,1)} %copy-done, bf16[128,2432]{1,0:T(8,128)(2,1)} %copy-done.1, bf16[128,2432]{1,0:T(8,128)(2,1)} %copy-done.2, bf16[128,2432]{1,0:T(8,128)(2,1)} %copy-done.3, ...), custom_call_target="tpu_custom_call" | custom-call | flops 4831838208 | bytes 10000000 | tf_op jit(solution)/shard_map/table_grad/pallas_call | solution.py:227
  241.2 7.1 %table_grad.3 = bf16[512,4608]{1,0:T(8,128)(2,1)} custom-call(s32[6]{0:T(128)} %stack.54.place, bf16[512,1024]{1,0:T(8,128)(2,1)} %dlogit.1.turned, bf16[128,2432]{1,0:T(8,128)(2,1)} %copy-done.9, bf16[128,2432]{1,0:T(8,128)(2,1)} %copy-done.6, bf16[128,2432]{1,0:T(8,128)(2,1)} %copy-done.7, ...), custom_call_target="tpu_custom_call", output_to_operand_aliasing={{}: (10, {})} | custom-call | flops 4831838208 | bytes 10000000 | tf_op jit(solution)/shard_map/table_grad/pallas_call | solution.py:227
  (163 shorter events, 88.3 us)
Async XLA Ops:
  3.6 14.8 %collective-permute-start.2 = (bf16[8,4864]{1,0:T(8,128)(2,1)S(1)}, bf16[8,4864]{1,0:T(8,128)(2,1)S(1)}, u32[]{:S(2)}, u32[]{:S(2)}) collective-permute-start(bf16[8,4864]{1,0:T(8,128)(2,1)S(1)} %pad_maximum_fusion.3), channel_id=1, source_target_pairs={{0,16},{16,32},{32,48},{48,0},{1,17},{17,33},{33,49},{49,1},{2,18}... | collective-permute-start | bytes 233480 | tf_op jit(solution)/shard_map/ppermute | solution.py:20
  16.8 23.6 %collective-permute-start.9 = (bf16[512,2304]{1,0:T(8,128)(2,1)S(1)}, bf16[512,2304]{1,0:T(8,128)(2,1)S(1)}, u32[]{:S(2)}, u32[]{:S(2)}) collective-permute-start(bf16[512,2304]{1,0:T(8,128)(2,1)S(1)} %constant_dynamic-slice_fusion), channel_id=1, source_target_pairs={{0,1},{1,0},{2,3},{3,2},{4,5},{5,4},{6,7},{7,6},{8,9},{9,8},{10,11... | collective-permute-start | bytes 7077896 | tf_op jit(solution)/shard_map/ppermute | solution.py:28
  40.5 14.2 %collective-permute-start.12 = (bf16[128,2432]{1,0:T(8,128)(2,1)S(1)}, bf16[128,2432]{1,0:T(8,128)(2,1)S(1)}, u32[]{:S(2)}, u32[]{:S(2)}) collective-permute-start(bf16[128,2432]{1,0:T(8,128)(2,1)S(1)} %constant_dynamic-update-slice_fusion.refs_0_.refs_2_), channel_id=1, source_target_pairs={{0,192},{64,0},{128,64},{192,128},{1,193},{65,1},{129,65},{193,129... | collective-permute-start | bytes 1867784 | tf_op jit(solution)/shard_map/ppermute | solution.py:20
  40.6 25.3 %collective-permute-start.13 = (bf16[128,2432]{1,0:T(8,128)(2,1)S(1)}, bf16[128,2432]{1,0:T(8,128)(2,1)S(1)}, u32[]{:S(2)}, u32[]{:S(2)}) collective-permute-start(bf16[128,2432]{1,0:T(8,128)(2,1)S(1)} %constant_dynamic-update-slice_fusion.refs_0_.refs_2_), channel_id=1, source_target_pairs={{0,128},{64,192},{128,0},{192,64},{1,129},{65,193},{129,1},{193,65... | collective-permute-start | bytes 1867784 | tf_op jit(solution)/shard_map/ppermute | solution.py:20
  42.1 29.5 %collective-permute-start.14 = (bf16[128,2432]{1,0:T(8,128)(2,1)S(1)}, bf16[128,2432]{1,0:T(8,128)(2,1)S(1)}, u32[]{:S(2)}, u32[]{:S(2)}) collective-permute-start(bf16[128,2432]{1,0:T(8,128)(2,1)S(1)} %constant_dynamic-update-slice_fusion.refs_0_.refs_2_), channel_id=1, source_target_pairs={{0,64},{64,128},{128,192},{192,0},{1,65},{65,129},{129,193},{193,1... | collective-permute-start | bytes 1867784 | tf_op jit(solution)/shard_map/ppermute | solution.py:20
  48.0 30.7 %collective-permute-start.15 = (bf16[128,2432]{1,0:T(8,128)(2,1)}, bf16[128,2432]{1,0:T(8,128)(2,1)}, u32[]{:S(2)}, u32[]{:S(2)}) collective-permute-start(bf16[128,2432]{1,0:T(8,128)(2,1)} %constant_dynamic-update-slice_fusion.4.refs_4_), channel_id=1, source_target_pairs={{0,12},{4,0},{8,4},{12,8},{1,13},{5,1},{9,5},{13,9},{2,14},{6,2},{... | collective-permute-start | bytes 1867784 | tf_op jit(solution)/shard_map/ppermute | solution.py:20
  54.7 24.0 %collective-permute-start.16 = (bf16[128,2432]{1,0:T(8,128)(2,1)}, bf16[128,2432]{1,0:T(8,128)(2,1)}, u32[]{:S(2)}, u32[]{:S(2)}) collective-permute-start(bf16[128,2432]{1,0:T(8,128)(2,1)} %constant_dynamic-update-slice_fusion.4.refs_4_), channel_id=1, source_target_pairs={{0,8},{4,12},{8,0},{12,4},{1,9},{5,13},{9,1},{13,5},{2,10},{6,14},... | collective-permute-start | bytes 1867784 | tf_op jit(solution)/shard_map/ppermute | solution.py:20
  54.7 31.1 %collective-permute-start.17 = (bf16[128,2432]{1,0:T(8,128)(2,1)}, bf16[128,2432]{1,0:T(8,128)(2,1)}, u32[]{:S(2)}, u32[]{:S(2)}) collective-permute-start(bf16[128,2432]{1,0:T(8,128)(2,1)} %constant_dynamic-update-slice_fusion.4.refs_4_), channel_id=1, source_target_pairs={{0,4},{4,8},{8,12},{12,0},{1,5},{5,9},{9,13},{13,1},{2,6},{6,10},{... | collective-permute-start | bytes 1867784 | tf_op jit(solution)/shard_map/ppermute | solution.py:20
  93.5 14.6 %collective-permute-start.30 = (bf16[128,2304]{1,0:T(8,128)(2,1)}, bf16[128,2304]{1,0:T(8,128)(2,1)S(1)}, u32[]{:S(2)}, u32[]{:S(2)}) collective-permute-start(bf16[128,2304]{1,0:T(8,128)(2,1)} %get-tuple-element.55), channel_id=1, source_target_pairs={{0,12},{4,0},{8,4},{12,8},{1,13},{5,1},{9,5},{13,9},{2,14},{6,2},{... | collective-permute-start | bytes 1769480 | tf_op jit(solution)/shard_map/ppermute | solution.py:24
  93.5 16.9 %collective-permute-start.29 = (bf16[128,2304]{1,0:T(8,128)(2,1)}, bf16[128,2304]{1,0:T(8,128)(2,1)S(1)}, u32[]{:S(2)}, u32[]{:S(2)}) collective-permute-start(bf16[128,2304]{1,0:T(8,128)(2,1)} %get-tuple-element.54), channel_id=1, source_target_pairs={{0,8},{4,12},{8,0},{12,4},{1,9},{5,13},{9,1},{13,5},{2,10},{6,14},... | collective-permute-start | bytes 1769480 | tf_op jit(solution)/shard_map/ppermute | solution.py:24
  93.6 29.7 %collective-permute-start.28 = (bf16[128,2304]{1,0:T(8,128)(2,1)}, bf16[128,2304]{1,0:T(8,128)(2,1)}, u32[]{:S(2)}, u32[]{:S(2)}) collective-permute-start(bf16[128,2304]{1,0:T(8,128)(2,1)} %get-tuple-element.53), channel_id=1, source_target_pairs={{0,4},{4,8},{8,12},{12,0},{1,5},{5,9},{9,13},{13,1},{2,6},{6,10},{... | collective-permute-start | bytes 1769480 | tf_op jit(solution)/shard_map/ppermute | solution.py:24
  96.0 143.5 %collective-permute-start.39 = (bf16[128,2432]{1,0:T(8,128)(2,1)}, bf16[128,2432]{1,0:T(8,128)(2,1)}, u32[]{:S(2)}, u32[]{:S(2)}) collective-permute-start(bf16[128,2432]{1,0:T(8,128)(2,1)} %constant_dynamic-update-slice_fusion.4.refs_4_), channel_id=1, source_target_pairs={{0,1},{1,0},{2,3},{3,2},{4,5},{5,4},{6,7},{7,6},{8,9},{9,8},{10,11... | collective-permute-start | bytes 1867784 | tf_op jit(solution)/shard_map/ppermute | solution.py:28
  97.0 28.1 %collective-permute-start.18 = (bf16[128,2432]{1,0:T(8,128)(2,1)S(1)}, bf16[128,2432]{1,0:T(8,128)(2,1)S(1)}, u32[]{:S(2)}, u32[]{:S(2)}) collective-permute-start(bf16[128,2432]{1,0:T(8,128)(2,1)S(1)} %collective-permute-done.12.refs_0_.refs_6_.refs_1_), channel_id=1, source_target_pairs={{0,1},{1,0},{2,3},{3,2},{4,5},{5,4},{6,7},{7,6},{8,9},{9,8},{10,11... | collective-permute-start | bytes 1867784 | tf_op jit(solution)/shard_map/ppermute | solution.py:28
  108.1 17.1 %collective-permute-start.19 = (bf16[128,2432]{1,0:T(8,128)(2,1)S(1)}, bf16[128,2432]{1,0:T(8,128)(2,1)S(1)}, u32[]{:S(2)}, u32[]{:S(2)}) collective-permute-start(bf16[128,2432]{1,0:T(8,128)(2,1)S(1)} %collective-permute-done.13.refs_1_.refs_7_.refs_2_), channel_id=1, source_target_pairs={{0,1},{1,0},{2,3},{3,2},{4,5},{5,4},{6,7},{7,6},{8,9},{9,8},{10,11... | collective-permute-start | bytes 1867784 | tf_op jit(solution)/shard_map/ppermute | solution.py:28
  110.4 14.8 %collective-permute-start.20 = (bf16[128,2432]{1,0:T(8,128)(2,1)S(1)}, bf16[128,2432]{1,0:T(8,128)(2,1)S(1)}, u32[]{:S(2)}, u32[]{:S(2)}) collective-permute-start(bf16[128,2432]{1,0:T(8,128)(2,1)S(1)} %collective-permute-done.14.refs_2_.refs_8_.refs_3_), channel_id=1, source_target_pairs={{0,1},{1,0},{2,3},{3,2},{4,5},{5,4},{6,7},{7,6},{8,9},{9,8},{10,11... | collective-permute-start | bytes 1867784 | tf_op jit(solution)/shard_map/ppermute | solution.py:28
  123.3 116.3 %collective-permute-start.40 = (bf16[128,2432]{1,0:T(8,128)(2,1)}, bf16[128,2432]{1,0:T(8,128)(2,1)}, u32[]{:S(2)}, u32[]{:S(2)}) collective-permute-start(bf16[128,2432]{1,0:T(8,128)(2,1)} %collective-permute-done.15.refs_5_), channel_id=1, source_target_pairs={{0,1},{1,0},{2,3},{3,2},{4,5},{5,4},{6,7},{7,6},{8,9},{9,8},{10,11... | collective-permute-start | bytes 1867784 | tf_op jit(solution)/shard_map/ppermute | solution.py:28
  134.0 20.2 %collective-permute-start.21 = (bf16[384,512]{1,0:T(8,128)(2,1)}, bf16[384,512]{1,0:T(8,128)(2,1)S(1)}, u32[]{:S(2)}, u32[]{:S(2)}) collective-permute-start(bf16[384,512]{1,0:T(8,128)(2,1)} %get-tuple-element.48.own), channel_id=1, source_target_pairs={{0,1},{1,0},{2,3},{3,2},{4,5},{5,4},{6,7},{7,6},{8,9},{9,8},{10,11... | collective-permute-start | bytes 1179656 | tf_op jit(solution)/shard_map/ppermute | solution.py:28
  140.5 30.6 %collective-permute-start.33 = (bf16[32,2304]{1,0:T(8,128)(2,1)S(1)}, bf16[32,2304]{1,0:T(8,128)(2,1)S(1)}, u32[]{:S(2)}, u32[]{:S(2)}) collective-permute-start(bf16[32,2304]{1,0:T(8,128)(2,1)S(1)} %get-tuple-element.72), channel_id=1, source_target_pairs={{0,192},{64,0},{128,64},{192,128},{1,193},{65,1},{129,65},{193,129... | collective-permute-start | bytes 442376 | tf_op jit(solution)/shard_map/ppermute | solution.py:24
  142.0 30.5 %collective-permute-start.32 = (bf16[32,2304]{1,0:T(8,128)(2,1)S(1)}, bf16[32,2304]{1,0:T(8,128)(2,1)S(1)}, u32[]{:S(2)}, u32[]{:S(2)}) collective-permute-start(bf16[32,2304]{1,0:T(8,128)(2,1)S(1)} %get-tuple-element.73), channel_id=1, source_target_pairs={{0,128},{64,192},{128,0},{192,64},{1,129},{65,193},{129,1},{193,65... | collective-permute-start | bytes 442376 | tf_op jit(solution)/shard_map/ppermute | solution.py:24
  149.0 25.5 %all-to-all-start.1 = ((f32[16,8,128]{2,1,0:T(8,128)}), f32[16,8,128]{2,1,0:T(8,128)S(1)}, u32[]{:S(2)}, u32[]{:S(2)}) async-start(f32[16,8,128]{2,1,0:T(8,128)} %broadcast_in_dim.13), calls=%async_computation.1 | async-start | bytes 131072 | tf_op jit(solution)/shard_map/all_to_all | solution.py:308
  154.2 20.0 %collective-permute-start.31 = (bf16[32,2304]{1,0:T(8,128)(2,1)S(1)}, bf16[32,2304]{1,0:T(8,128)(2,1)S(1)}, u32[]{:S(2)}, u32[]{:S(2)}) collective-permute-start(bf16[32,2304]{1,0:T(8,128)(2,1)S(1)} %get-tuple-element.71), channel_id=1, source_target_pairs={{0,64},{64,128},{128,192},{192,0},{1,65},{65,129},{129,193},{193,1... | collective-permute-start | bytes 442376 | tf_op jit(solution)/shard_map/ppermute | solution.py:24
  171.1 14.2 %collective-permute-start.24 = (bf16[128,2304]{1,0:T(8,128)(2,1)}, bf16[128,2304]{1,0:T(8,128)(2,1)S(1)}, u32[]{:S(2)}, u32[]{:S(2)}) collective-permute-start(bf16[128,2304]{1,0:T(8,128)(2,1)} %get-tuple-element.51), channel_id=1, source_target_pairs={{0,192},{64,0},{128,64},{192,128},{1,193},{65,1},{129,65},{193,129... | collective-permute-start | bytes 1769480 | tf_op jit(solution)/shard_map/ppermute | solution.py:24
  172.5 15.7 %collective-permute-start.23 = (bf16[128,2304]{1,0:T(8,128)(2,1)}, bf16[128,2304]{1,0:T(8,128)(2,1)}, u32[]{:S(2)}, u32[]{:S(2)}) collective-permute-start(bf16[128,2304]{1,0:T(8,128)(2,1)} %get-tuple-element.50), channel_id=1, source_target_pairs={{0,128},{64,192},{128,0},{192,64},{1,129},{65,193},{129,1},{193,65... | collective-permute-start | bytes 1769480 | tf_op jit(solution)/shard_map/ppermute | solution.py:24
  174.2 28.0 %collective-permute-start.22 = (bf16[128,2304]{1,0:T(8,128)(2,1)}, bf16[128,2304]{1,0:T(8,128)(2,1)}, u32[]{:S(2)}, u32[]{:S(2)}) collective-permute-start(bf16[128,2304]{1,0:T(8,128)(2,1)} %get-tuple-element.49), channel_id=1, source_target_pairs={{0,64},{64,128},{128,192},{192,0},{1,65},{65,129},{129,193},{193,1... | collective-permute-start | bytes 1769480 | tf_op jit(solution)/shard_map/ppermute | solution.py:24
  (40 other events, 527.1 us)

commit v4 on v0

v4 whole, which is shorter than its diff:
```python
import functools

import jax
import jax.numpy as jnp
from jax import lax
from jax.experimental import pallas as pl
from jax.experimental.pallas import tpu as pltpu
from jax.sharding import Mesh, PartitionSpec as P

DP = ("x", "zh", "y")
AXES = ("x", "zh", "y", "zl", "c")
F32, BF16 = jnp.float32, jnp.bfloat16
VMEM_LIMIT = 56 * 1024 * 1024
INFO = 128
SLAB = 128
TILE = 1152
PRODUCTS = 10_000


def pull(value, axis, shift, size=4):
    return lax.ppermute(value, axis, [(i, (i - shift) % size) for i in range(size)])


def push(value, axis, shift, size=4):
    return lax.ppermute(value, axis, [(i, (i + shift) % size) for i in range(size)])


def swap(value, axis):
    return lax.ppermute(value, axis, [(0, 1), (1, 0)])


def digits(ids):
    return [ids // 65536, (ids // 256) % 256, ids % 256]


def info_columns(values):
    info = jnp.stack([v.astype(BF16) for v in values], 1)
    return jnp.pad(info, ((0, 0), (0, INFO - info.shape[1])))


def whole(core, own, other):
    return jnp.where(
        core == 0, jnp.concatenate([own, other], 1), jnp.concatenate([other, own], 1)
    )


def joined(info):
    info = info.astype(F32)
    return (info[:, 0:1] * 65536.0 + info[:, 1:2] * 256.0 + info[:, 2:3]).astype(jnp.int32)


def cost(us):
    return pl.CostEstimate(flops=us * 1_000_000_000 + 1, bytes_accessed=1, transcendentals=0)


def params():
    return pltpu.CompilerParams(vmem_limit_bytes=VMEM_LIMIT)


def matching(place):
    r = lax.broadcasted_iota(jnp.int32, (SLAB, SLAB), 0)
    lane = lax.broadcasted_iota(jnp.int32, (SLAB, SLAB), 1)
    zh = (place[1] + (r // 8) % 4) % 4
    return lane == (r // 32) * 32 + zh * 8 + r % 8


def as_lanes(match, column):
    return jnp.sum(jnp.where(match, column, 0.0), 0, keepdims=True)


def as_column(match, lanes):
    return jnp.sum(jnp.where(match, lanes, 0.0), 1, keepdims=True)


def logits_kernel(place, own, other, info, t_own, t_other, _, squash, expo, slope, sums):
    trans = (((1,), (1,)), ((), ()))
    step, tile = pl.program_id(0), expo.shape[1]

    @pl.when(step == 0)
    def _():
        sums[...] = jnp.zeros_like(sums)

    acc = lax.dot_general(own[...], t_own[...], trans, preferred_element_type=F32)
    acc += lax.dot_general(other[...], t_other[...], trans, preferred_element_type=F32)
    q = jnp.tanh(acc * (1.0 / 30.0))
    e = jnp.exp(30.0 * q)
    squash[...] = q
    expo[...] = e
    columns = place[2] + step * tile + lax.broadcasted_iota(jnp.int32, (SLAB, tile), 1)
    rows = lax.broadcasted_iota(jnp.int32, (8, SLAB), 0)
    match = matching(place)
    add = jnp.zeros((8, SLAB), F32)
    for d in range(4):
        part = slice(d * SLAB, (d + 1) * SLAB)
        hits = columns == joined(info[part, :])
        qd, ed = q[part], e[part]
        slope[part, :] = jnp.where(hits, 0.0, ed * (1.0 - qd * qd)).astype(BF16)
        for base, values in ((0, ed), (4, jnp.where(hits, qd, 0.0))):
            lanes = as_lanes(match, jnp.sum(values, 1, keepdims=True))
            add = add + jnp.where(rows == d + base, lanes, 0.0)
    sums[...] += add


def logits_call(place, own, other, table, after):
    (rows, width), tokens = table.shape, own.shape[0]
    half, tile = width // 2, rows // 2
    whole_block = pl.BlockSpec((tokens, half), lambda v, p: (0, 0))
    out = pl.BlockSpec((tokens, tile), lambda v, p: (0, v))
    return pl.pallas_call(
        logits_kernel,
        grid_spec=pltpu.PrefetchScalarGridSpec(
            num_scalar_prefetch=1,
            grid=(rows // tile,),
            in_specs=[
                whole_block,
                whole_block,
                pl.BlockSpec((tokens, INFO), lambda v, p: (0, half // INFO)),
                pl.BlockSpec((tile, half), lambda v, p: (v, p[0])),
                pl.BlockSpec((tile, half), lambda v, p: (v, 1 - p[0])),
                pl.BlockSpec(memory_space=pl.ANY),
            ],
            out_specs=[out, out, out, pl.BlockSpec((8, SLAB), lambda v, p: (0, 0))],
        ),
        out_shape=[
            jax.ShapeDtypeStruct((tokens, rows), F32),
            jax.ShapeDtypeStruct((tokens, rows), F32),
            jax.ShapeDtypeStruct((tokens, rows), BF16),
            jax.ShapeDtypeStruct((8, SLAB), F32),
        ],
        compiler_params=params(),
        cost_estimate=cost(PRODUCTS),
        name="logits",
    )(place, own, other, own, table, table, after)


def mean_kernel(place, own, other, t_own, t_other, out):
    acc = jnp.dot(own[...], t_own[...], preferred_element_type=F32)
    out[...] = acc + jnp.dot(other[...], t_other[...], preferred_element_type=F32)


def pick_kernel(place, info, _, t_own, t_other, out, mine, theirs):
    @pl.when(pl.program_id(0) == 0)
    def _():
        columns = lax.broadcasted_iota(jnp.int32, mine.shape, 1)
        ids = joined(info[...])
        mine[...] = (columns + place[2] == ids).astype(F32).astype(BF16)
        theirs[...] = (columns + place[3] == ids).astype(F32).astype(BF16)

    acc = jnp.dot(mine[...], t_own[...], preferred_element_type=F32)
    acc += jnp.dot(theirs[...], t_other[...], preferred_element_type=F32)
    out[...] = acc.astype(BF16)


def product_call(kernel, place, left, specs, table, t_other, kind, scratch, name):
    (rows, half), tokens = t_other.shape, 4 * SLAB
    steps = half // TILE
    return pl.pallas_call(
        kernel,
        grid_spec=pltpu.PrefetchScalarGridSpec(
            num_scalar_prefetch=1,
            grid=(steps,),
            in_specs=specs
            + [
                pl.BlockSpec((rows, TILE), lambda j, p: (0, p[0] * steps + j)),
                pl.BlockSpec((rows, TILE), lambda j, p: (0, j)),
            ],
            out_specs=pl.BlockSpec((tokens, TILE), lambda j, p: (0, j)),
            scratch_shapes=scratch,
        ),
        out_shape=jax.ShapeDtypeStruct((tokens, half), kind),
        compiler_params=params(),
        cost_estimate=cost(PRODUCTS),
        name=name,
    )(place, *left, table, t_other)


def total_kernel(got, _, out):
    acc = got[0]
    for k in range(1, got.shape[0]):
        acc += got[k]
    out[...] = acc


def total_call(value, axes, after):
    got = spread(value, axes)
    return pl.pallas_call(
        total_kernel,
        in_specs=[pl.BlockSpec(memory_space=pltpu.VMEM), pl.BlockSpec(memory_space=pl.ANY)],
        out_specs=pl.BlockSpec(memory_space=pltpu.VMEM),
        out_shape=jax.ShapeDtypeStruct(value.shape, value.dtype),
        compiler_params=params(),
        cost_estimate=cost(0),
        name="total",
    )(got, after)


def combine_kernel(place, info, mean, pick, total, out):
    match = matching(place)
    for d in range(4):
        part = pl.ds(d * SLAB, SLAB)
        norm = as_column(match, total[d : d + 1, :])
        s = as_column(match, total[d + 4 : d + 5, :])
        weight = info[part, 3:4].astype(F32)
        target = weight * (jnp.exp(30.0 * s) / norm - 1.0) * (1.0 - s * s)
        value = mean[part, :] * (weight / norm) + pick[part, :].astype(F32) * target
        out[part, :] = value.astype(BF16)


def combine_call(place, hid, mean, pick, total):
    tokens, half = mean.shape
    block = pl.BlockSpec((tokens, TILE), lambda j, p: (0, j))
    return pl.pallas_call(
        combine_kernel,
        grid_spec=pltpu.PrefetchScalarGridSpec(
            num_scalar_prefetch=1,
            grid=(half // TILE,),
            in_specs=[pl.BlockSpec((tokens, INFO), lambda j, p: (0, half // INFO))]
            + [block, block, pl.BlockSpec((8, SLAB), lambda j, p: (0, 0))],
            out_specs=block,
        ),
        out_shape=jax.ShapeDtypeStruct((tokens, half), BF16),
        compiler_params=params(),
        cost_estimate=cost(0),
        name="combine",
    )(place, hid, mean, pick, total)


def sum_kernel(got, _, out):
    acc = got[0].astype(F32)
    for k in range(1, got.shape[0]):
        acc += got[k].astype(F32)
    out[...] = acc.astype(BF16)


def sum_call(got, after):
    peers, rows, half = got.shape
    return pl.pallas_call(
        sum_kernel,
        grid=(half // TILE,),
        in_specs=[
            pl.BlockSpec((peers, rows, TILE), lambda j: (0, 0, j)),
            pl.BlockSpec(memory_space=pl.ANY),
        ],
        out_specs=pl.BlockSpec((rows, TILE), lambda j: (0, j)),
        out_shape=jax.ShapeDtypeStruct((rows, half), BF16),
        compiler_params=params(),
        cost_estimate=cost(0),
        name="sum",
    )(got, after)


def dlogit_kernel(place, info, emb_info, q, e, total, _, turned):
    match = matching(place)
    columns = place[2] + lax.broadcasted_iota(jnp.int32, (SLAB, turned.shape[0]), 1)
    for d in range(4):
        part = pl.ds(d * SLAB, SLAB)
        tot = as_column(match, total[d : d + 1, :])
        hits = (columns == joined(info[part, :])).astype(F32)
        weight = info[part, 3:4].astype(F32)
        s = q[part, :]
        value = (weight * (e[part, :] / tot - hits) * (1.0 - s * s)).astype(BF16)
        turned[:, d * SLAB : (d + 1) * SLAB] = value.T
        hit = (columns == joined(emb_info[part, :])).astype(F32).astype(BF16)
        turned[:, (4 + d) * SLAB : (5 + d) * SLAB] = hit.T


def dlogit_call(place, hid, emb, q, e, total, after):
    (tokens, rows), half = q.shape, hid.shape[1] - INFO
    every = lambda a: pl.BlockSpec(a.shape, lambda i, p: (0, 0))
    return pl.pallas_call(
        dlogit_kernel,
        grid_spec=pltpu.PrefetchScalarGridSpec(
            num_scalar_prefetch=1,
            grid=(1,),
            in_specs=[pl.BlockSpec((tokens, INFO), lambda i, p: (0, half // INFO))] * 2
            + [every(a) for a in (q, e, total)]
            + [pl.BlockSpec(memory_space=pl.ANY)],
            out_specs=pl.BlockSpec((rows, 2 * tokens), lambda i, p: (0, 0)),
        ),
        out_shape=jax.ShapeDtypeStruct((rows, 2 * tokens), BF16),
        compiler_params=params(),
        cost_estimate=cost(0),
        name="dlogit",
    )(place, hid, emb, q, e, total, after)


def table_grad_kernel(place, turned, hid, emb, *refs):
    out, tokens = refs[-1], hid.shape[0]
    acc = jnp.dot(turned[:, :tokens], hid[...], preferred_element_type=F32)
    acc += jnp.dot(turned[:, tokens:], emb[...], preferred_element_type=F32)
    out[...] = acc.astype(BF16)


def table_grad_call(place, turned, hid, emb, other, before=None):
    rows, (tokens, width) = turned.shape[0], hid.shape
    half = width - INFO
    steps = half // TILE
    return pl.pallas_call(
        table_grad_kernel,
        grid_spec=pltpu.PrefetchScalarGridSpec(
            num_scalar_prefetch=1,
            grid=(steps,),
            in_specs=[pl.BlockSpec(turned.shape, lambda j, p: (0, 0))]
            + [pl.BlockSpec((tokens, TILE), lambda j, p: (0, j))] * 2
            + ([] if before is None else [pl.BlockSpec(memory_space=pl.ANY)]),
            out_specs=pl.BlockSpec(
                (rows, TILE),
                lambda j, p: (0, (1 - p[0] if other else p[0]) * steps + j),
            ),
        ),
        out_shape=jax.ShapeDtypeStruct((rows, 2 * half), BF16),
        input_output_aliases={} if before is None else {4: 0},
        compiler_params=params(),
        cost_estimate=cost(0),
        name="table_grad",
    )(place, turned, hid, emb, *([] if before is None else [before]))


def spread(value, axes, size=16):
    return lax.all_to_all(jnp.broadcast_to(value, (size,) + value.shape), axes, 0, 0)


def body(hidden, table, target_ids, loss_weight, input_ids, emb_grad_in):
    own_rows, width = table.shape
    half = width // 2
    core = lax.axis_index("c")
    row_start = lax.axis_index(AXES) * own_rows
    place = jnp.stack(
        [core, lax.axis_index("zh"), row_start, row_start + (1 - 2 * core) * own_rows]
    ).astype(jnp.int32)

    def my_half(a):
        return lax.dynamic_slice_in_dim(a, core * half, half, 1)

    joint = jnp.concatenate(
        [
            my_half(hidden),
            info_columns(digits(target_ids) + [loss_weight]),
            my_half(emb_grad_in),
            info_columns(digits(input_ids)),
        ],
        1,
    )
    joint = jnp.concatenate([joint] + [pull(joint, "zh", d) for d in (1, 2, 3)], 0)
    t_send = lax.dynamic_slice_in_dim(table, (1 - core) * half, half, 1)
    hid = joint[:, : half + INFO] + t_send[:1, :1] * 0
    hid = spread(hid, ("x", "y")).reshape(4 * SLAB, half + INFO)
    emb = joint[:, half + INFO :]
    emb = jnp.concatenate([emb] + [pull(emb, "y", d) for d in (1, 2, 3)], 0)
    t_other = swap(t_send, "c")

    hid_other = swap(hid, "c")
    q, e, slope, sums = logits_call(place, hid, hid_other, table, emb)
    emb = emb + (sums[:1, :1] * 0.0).astype(BF16)
    emb = jnp.concatenate([emb] + [pull(emb, "x", d) for d in (1, 2, 3)], 0)
    tokens, rows = slope.shape
    full = pl.BlockSpec((tokens, rows), lambda j, p: (0, 0))
    mean = product_call(
        mean_kernel, place, [slope, swap(slope, "c")], [full, full], table, t_other, F32, [], "mean"
    )
    total = total_call(sums, ("zh", "zl", "c"), mean)
    emb_other = swap(emb + (total[:1, :1] * 0.0).astype(BF16), "c")
    pick = product_call(
        pick_kernel,
        place,
        [hid, mean],
        [
            pl.BlockSpec((tokens, INFO), lambda j, p: (0, half // INFO)),
            pl.BlockSpec(memory_space=pl.ANY),
        ],
        table,
        t_other,
        BF16,
        [pltpu.VMEM((tokens, rows), BF16)] * 2,
        "pick",
    )
    total = total_call(total, ("x", "y"), pick)

    out = combine_call(place, hid, mean, pick, total)
    got = lax.all_to_all(out.reshape(16, 32, half), ("x", "y"), 0, 0)

    turned = dlogit_call(place, hid, emb, q, e, total, out)
    grad_table = table_grad_call(place, turned, hid, emb, 0)
    grad_table = table_grad_call(place, turned, hid_other, emb_other, 1, grad_table)

    acc = sum_call(got, grad_table)
    acc = lax.dynamic_slice_in_dim(
        jnp.concatenate([acc, acc], 0), (4 - lax.axis_index("zh")) % 4 * 8, 32, 0
    )
    acc = jnp.broadcast_to(acc.reshape(4, 1, 8, half), (4, 2, 8, half)).reshape(8, 8, half)
    acc = lax.all_to_all(acc, ("zh", "zl"), 0, 0)
    acc = jnp.sum(acc.astype(F32), 0).astype(BF16)
    grad_hidden = whole(core, acc, swap(acc, "c"))
    return grad_hidden, grad_table


def solution(mesh):
    fine = Mesh(mesh.devices.reshape(4, 4, 4, 2, 2), AXES)
    rows, every = P(DP, None), P(AXES, None)
    return jax.shard_map(
        body,
        mesh=fine,
        in_specs=(rows, every, P(DP), P(DP), P(DP), rows),
        out_specs=(rows, every),
        check_vma=False,
    )
```

time: 497 us -> 201 us (0.40)
  blocking collectives: 445 us -> 51.3 us
  Pallas kernels: 0 us -> 52 us
  starting transfers between devices: 0.08 us -> 44.8 us
  matrix products: 29.4 us -> 0 us
  waiting for transfers between devices: 1.38 us -> 25.9 us
  between operations: 14.7 us -> 2.11 us
  other arithmetic: 0.01 us -> 12.4 us
  local copies, waits for them, and re-layouts: 5.4 us -> 11.1 us
    unnamed x3 -> x0, blocking collectives: 331 us -> none
    psum x1 -> x0, blocking collectives: 107 us -> none  [body(): total = lax.psum(jnp.sum(expo, axis=1), ('dp', 'vocab'))]
    pallas_call x0 -> x10, Pallas kernels: none -> 52 us  [the longest x2 14 us: product_call(): pl.pallas_call(kernel, grid_spec=pltpu.PrefetchScalarGridSpec(num_scalar_...]
    all_to_all x0 -> x2, blocking collectives: none -> 51.3 us  [the longest x1 37.9 us: spread(): lax.all_to_all(jnp.broadcast_to(value, (size,) + value.shape), axes, 0, 0)]
    dot_general x4 -> x0, matrix products: 29.4 us -> none  [the longest x1 8.1 us: body(): lax.dot_general(onehot_in, all_grad_in, contract, preferred_element_type=...]
    ppermute x0 -> x14, starting transfers between devices: none -> 28.2 us  [the longest x9 18.1 us: pull(): lax.ppermute(value, axis, [(i, (i - shift) % size) for i in range(size)])]
    all_to_all x0 -> x3, starting transfers between devices: none -> 16.6 us  [the longest x2 10.9 us: spread(): lax.all_to_all(jnp.broadcast_to(value, (size,) + value.shape), axes, 0, 0)]
    all_to_all x0 -> x3, waiting for transfers between devices: none -> 13.3 us  [the longest x1 13.2 us: body(): got = lax.all_to_all(out.reshape(16, 32, half), ('x', 'y'), 0, 0)]
  transfers between devices with their start and end apart: 2 -> 17, of which waited for: 0 -> 8; matrix products, arithmetic and copies ran while one was open for 5% -> 8% of each run, Pallas kernels for 0% -> 25%
where the time goes in v4:
time: 201 us; the launch traced here: 200 us
  Pallas kernels  52 us (26%)
  blocking collectives  51.3 us (26%)
  starting transfers between devices  44.8 us (22%)
  waiting for transfers between devices  25.9 us (13%)
  other arithmetic  12.4 us (6%)
  local copies, waits for them, and re-layouts  11.1 us (6%)
  between operations  2.11 us (1%)
    all_to_all x1, blocking collectives, spread(): lax.all_to_all(jnp.broadcast_to(value, (size,) + value.shape), axes, 0, 0)  37.9 us
    ppermute x9, starting transfers between devices, pull(): lax.ppermute(value, axis, [(i, (i - shift) % size) for i in range(size)])  18.1 us
    pallas_call x2, Pallas kernels, product_call(): pl.pallas_call(kernel, grid_spec=pltpu.PrefetchScalarGridSpec(num_scalar_...  14 us
    pallas_call x2, Pallas kernels, table_grad_call(): pl.pallas_call(table_grad_kernel, grid_spec=pltpu.PrefetchScalarGridSpec(...  13.5 us
    all_to_all x1, blocking collectives, body(): acc = lax.all_to_all(acc, ('zh', 'zl'), 0, 0)  13.4 us
    all_to_all x1, waiting for transfers between devices, body(): got = lax.all_to_all(out.reshape(16, 32, half), ('x', 'y'), 0, 0)  13.2 us
    ppermute x9, waiting for transfers between devices, pull(): lax.ppermute(value, axis, [(i, (i - shift) % size) for i in range(size)])  11.8 us
    all_to_all x2, starting transfers between devices, spread(): lax.all_to_all(jnp.broadcast_to(value, (size,) + value.shape), axes, 0, 0)  10.9 us
  transfers between devices with their start and end apart: 17, of which 8 were waited for; matrix products, arithmetic and copies ran while one was open for 8% of the time, Pallas kernels for 25%

profile of v4, /device:TPU:1, one launch (start us, length us, event | category | flops | bytes accessed | tf_op | source)
XLA Modules:
  0.0 199.6 jit_solution(3323734229931569366)
XLA Ops:
  3.6 3.9 %collective-permute-start.2 = (bf16[8,4864]{1,0:T(8,128)(2,1)S(1)}, bf16[8,4864]{1,0:T(8,128)(2,1)S(1)}, u32[]{:S(2)}, u32[]{:S(2)}) collective-permute-start(bf16[8,4864]{1,0:T(8,128)(2,1)S(1)} %pad_maximum_fusion.3), channel_id=1, source_target_pairs={{0,16},{16,32},{32,48},{48,0},{1,17},{17,33},{33,49},{49,1},{2,18}... | collective-permute-start | bytes 233480 | tf_op jit(solution)/shard_map/ppermute | solution.py:21
  7.5 5.1 %collective-permute-start.1 = (bf16[8,4864]{1,0:T(8,128)(2,1)S(1)}, bf16[8,4864]{1,0:T(8,128)(2,1)S(1)}, u32[]{:S(2)}, u32[]{:S(2)}) collective-permute-start(bf16[8,4864]{1,0:T(8,128)(2,1)S(1)} %pad_maximum_fusion.3), channel_id=1, source_target_pairs={{0,32},{16,48},{32,0},{48,16},{1,33},{17,49},{33,1},{49,17},{2,34}... | collective-permute-start | bytes 233480 | tf_op jit(solution)/shard_map/ppermute | solution.py:21
  12.6 2.4 %collective-permute-start = (bf16[8,4864]{1,0:T(8,128)(2,1)S(1)}, bf16[8,4864]{1,0:T(8,128)(2,1)S(1)}, u32[]{:S(2)}, u32[]{:S(2)}) collective-permute-start(bf16[8,4864]{1,0:T(8,128)(2,1)S(1)} %pad_maximum_fusion.3), channel_id=1, source_target_pairs={{0,48},{16,0},{32,16},{48,32},{1,49},{17,1},{33,17},{49,33},{2,50}... | collective-permute-start | bytes 233480 | tf_op jit(solution)/shard_map/ppermute | solution.py:21
  17.4 3.9 %collective-permute-done = bf16[8,4864]{1,0:T(8,128)(2,1)S(1)} collective-permute-done((bf16[8,4864]{1,0:T(8,128)(2,1)S(1)}, bf16[8,4864]{1,0:T(8,128)(2,1)S(1)}, u32[]{:S(2)}, u32[]{:S(2)}) %collective-permute-start) | collective-permute-done | bytes 77856 | tf_op jit(solution)/shard_map/ppermute | solution.py:21
  22.1 37.9 %all_to_all.25 = bf16[16,32,2432]{2,1,0:T(8,128)(2,1)S(1)} all-to-all(bf16[16,32,2432]{2,1,0:T(8,128)(2,1)S(1)} %broadcast_in_dim.16), channel_id=1, replica_groups=mesh['x'=4,'zh'=4,'y'=4,'zl'=2,'c'=2] {'x','y'}, dimensions={0} | all-to-all | bytes 4980736 | tf_op jit(solution)/shard_map/all_to_all | solution.py:320
  60.0 2.3 %collective-permute-start.3 = (bf16[512,2432]{1,0:T(8,128)(2,1)S(1)}, bf16[512,2432]{1,0:T(8,128)(2,1)}, u32[]{:S(2)}, u32[]{:S(2)}) collective-permute-start(bf16[512,2432]{1,0:T(8,128)(2,1)S(1)} %bitcast.25), channel_id=1, source_target_pairs={{0,1},{1,0},{2,3},{3,2},{4,5},{5,4},{6,7},{7,6},{8,9},{9,8},{10,11... | collective-permute-start | bytes 7471112 | tf_op jit(solution)/shard_map/ppermute | solution.py:29
  68.8 3.7 %collective-permute-done.6 = bf16[32,2432]{1,0:T(8,128)(2,1)S(1)} collective-permute-done((bf16[32,2432]{1,0:T(8,128)(2,1)S(1)}, bf16[32,2432]{1,0:T(8,128)(2,1)S(1)}, u32[]{:S(2)}, u32[]{:S(2)}) %collective-permute-start.6) | collective-permute-done | bytes 155680 | tf_op jit(solution)/shard_map/ppermute | solution.py:21
  73.7 8.4 %logits.1 = (f32[512,512]{1,0:T(8,128)}, f32[512,512]{1,0:T(8,128)}, bf16[512,512]{1,0:T(8,128)(2,1)}, f32[8,128]{1,0:T(8,128)}) custom-call(s32[4]{0:T(128)} %pad_add_fusion.place, bf16[512,2432]{1,0:T(8,128)(2,1)} %bitcast.26, bf16[512,2432]{1,0:T(8,128)(2,1)} %collective-permute-done.3.other.hid, bf16[512,2432]{1,0:T(8,128)(2,1)} %bitcast.27, ...), custom_call_target="tpu_custom_call" | custom-call | flops 9999999827968 | bytes 1 | tf_op jit(solution)/shard_map/logits/pallas_call | solution.py:109
  87.2 2.4 %collective-permute-start.10 = (bf16[128,2432]{1,0:T(8,128)(2,1)}, bf16[128,2432]{1,0:T(8,128)(2,1)}, u32[]{:S(2)}, u32[]{:S(2)}) collective-permute-start(bf16[128,2432]{1,0:T(8,128)(2,1)} %broadcast_add_fusion.1), channel_id=1, source_target_pairs={{0,128},{64,192},{128,0},{192,64},{1,129},{65,193},{129,1},{193,65... | collective-permute-start | bytes 1867784 | tf_op jit(solution)/shard_map/ppermute | solution.py:21
  91.7 5.5 %all-to-all-start.1 = ((f32[16,8,128]{2,1,0:T(8,128)}), f32[16,8,128]{2,1,0:T(8,128)}, u32[]{:S(2)}, u32[]{:S(2)}) async-start(f32[16,8,128]{2,1,0:T(8,128)} %broadcast_in_dim.17), calls=%async_computation.1 | async-start | bytes 131072 | tf_op jit(solution)/shard_map/all_to_all | solution.py:320
  98.0 7.1 %mean.1._ = f32[512,2304]{1,0:T(8,128)} custom-call(s32[4]{0:T(128)} %pad_add_fusion.place, bf16[512,512]{1,0:T(8,128)(2,1)} %get-tuple-element.6.own, bf16[512,512]{1,0:T(8,128)(2,1)} %copy-done.8, bf16[512,4608]{1,0:T(8,128)(2,1)} %t_own.5, bf16[512,2304]{1,0:T(8,128)(2,1)} %collective-permute-done.8.t_other), custom_call_target="tpu_custom_call" | custom-call | flops 9999999827968 | bytes 1 | tf_op jit(solution)/shard_map/mean/pallas_call | solution.py:157
  109.7 5.4 %all-to-all-start.2 = ((f32[16,8,128]{2,1,0:T(8,128)}), f32[16,8,128]{2,1,0:T(8,128)}, u32[]{:S(2)}, u32[]{:S(2)}) async-start(f32[16,8,128]{2,1,0:T(8,128)} %broadcast_in_dim.18), calls=%async_computation.2 | async-start | bytes 131072 | tf_op jit(solution)/shard_map/all_to_all | solution.py:320
  115.1 2.4 %collective-permute-done.10 = bf16[128,2432]{1,0:T(8,128)(2,1)} collective-permute-done((bf16[128,2432]{1,0:T(8,128)(2,1)}, bf16[128,2432]{1,0:T(8,128)(2,1)}, u32[]{:S(2)}, u32[]{:S(2)}) %collective-permute-start.10) | collective-permute-done | bytes 622624 | tf_op jit(solution)/shard_map/ppermute | solution.py:21
  118.0 4.4 %broadcast_add_fusion = (bf16[512,2432]{1,0:T(8,128)(2,1)}, bf16[512,2432]{1,0:T(8,128)(2,1)}) fusion(bf16[]{:T(256)} %bitcast.15, bf16[128,2432]{1,0:T(8,128)(2,1)} %collective-permute-done.11, bf16[128,2432]{1,0:T(8,128)(2,1)} %collective-permute-done.10, bf16[128,2432]{1,0:T(8,128)(2,1)} %collective-permute-done.9, bf16[128,2432]{1,0:T(8,128)(2,1)} %broadcast_add_fusion.1), kind=kLoop, calls=%fused_computation.1 | loop fusion | flops 13697024 | bytes 7471106 | tf_op jit(solution)/shard_map/add | solution.py:362
  123.9 6.9 %pick.1._ = bf16[512,2304]{1,0:T(8,128)(2,1)} custom-call(s32[4]{0:T(128)} %pad_add_fusion.place, bf16[512,2432]{1,0:T(8,128)(2,1)} %bitcast.28, f32[512,2304]{1,0:T(8,128)} %mean.1._, bf16[512,4608]{1,0:T(8,128)(2,1)} %t_own.5, bf16[512,2304]{1,0:T(8,128)(2,1)} %collective-permute-done.8.t_other), custom_call_target="tpu_custom_call" | custom-call | flops 9999999827968 | bytes 1 | tf_op jit(solution)/shard_map/pick/pallas_call | solution.py:157
  132.2 5.5 %combine.1._ = bf16[512,2304]{1,0:T(8,128)(2,1)} custom-call(s32[4]{0:T(128)} %pad_add_fusion.place, bf16[512,2432]{1,0:T(8,128)(2,1)} %bitcast.29, f32[512,2304]{1,0:T(8,128)} %mean.1._, bf16[512,2304]{1,0:T(8,128)(2,1)} %pick.1._, f32[8,128]{1,0:T(8,128)} %total.3), custom_call_target="tpu_custom_call" | custom-call | flops 1 | bytes 1 | tf_op jit(solution)/shard_map/combine/pallas_call | solution.py:212
  137.7 5.7 %all-to-all-start.3 = ((bf16[16,32,2304]{2,1,0:T(8,128)(2,1)}), bf16[16,32,2304]{2,1,0:T(8,128)(2,1)S(1)}, u32[]{:S(2)}, u32[]{:S(2)}) async-start(bf16[16,32,2304]{2,1,0:T(8,128)(2,1)} %bitcast.32), calls=%async_computation.3 | async-start | bytes 4718592 | tf_op jit(solution)/shard_map/all_to_all | solution.py:380
  143.4 5.3 %dlogit.1.turned = bf16[512,1024]{1,0:T(8,128)(2,1)} custom-call(s32[4]{0:T(128)} %pad_add_fusion.place, bf16[512,2432]{1,0:T(8,128)(2,1)} %bitcast.30, bf16[512,2432]{1,0:T(8,128)(2,1)} %get-tuple-element.11.emb_info.emb, f32[512,512]{1,0:T(8,128)} %get-tuple-element.8.q, f32[512,512]{1,0:T(8,128)} %get-tuple-element.9.e, f32[8,128]{1,0:T(8,128)} %total.3, ...), custom_call_target="tpu_custom_call" | custom-call | flops 1 | bytes 1 | tf_op jit(solution)/shard_map/dlogit/pallas_call | solution.py:270
  148.8 6.7 %table_grad.2.refs_0_ = bf16[512,4608]{1,0:T(8,128)(2,1)} custom-call(s32[4]{0:T(128)} %pad_add_fusion.place, bf16[512,1024]{1,0:T(8,128)(2,1)} %dlogit.1.turned, bf16[512,2432]{1,0:T(8,128)(2,1)} %bitcast.31, bf16[512,2432]{1,0:T(8,128)(2,1)} %get-tuple-element.11.emb_info.emb), custom_call_target="tpu_custom_call" | custom-call | flops 1 | bytes 1 | tf_op jit(solution)/shard_map/table_grad/pallas_call | solution.py:298
  155.5 6.7 %table_grad.3._ = bf16[512,4608]{1,0:T(8,128)(2,1)} custom-call(s32[4]{0:T(128)} %pad_add_fusion.place, bf16[512,1024]{1,0:T(8,128)(2,1)} %dlogit.1.turned, bf16[512,2432]{1,0:T(8,128)(2,1)} %collective-permute-done.3.other.hid, bf16[512,2432]{1,0:T(8,128)(2,1)} %collective-permute-done.12.emb, ...), custom_call_target="tpu_custom_call", output_to_operand_aliasing={{}: (4, {})} | custom-call | flops 1 | bytes 1 | tf_op jit(solution)/shard_map/table_grad/pallas_call | solution.py:298
  162.3 13.2 %all-to-all-done.3.got = bf16[16,32,2304]{2,1,0:T(8,128)(2,1)S(1)} async-done(((bf16[16,32,2304]{2,1,0:T(8,128)(2,1)}), bf16[16,32,2304]{2,1,0:T(8,128)(2,1)S(1)}, u32[]{:S(2)}, u32[]{:S(2)}) %all-to-all-start.3) | async-done | bytes 2359328 | tf_op jit(solution)/shard_map/all_to_all | solution.py:380
  176.9 2.4 %sum.1 = bf16[32,2304]{1,0:T(8,128)(2,1)} custom-call(bf16[16,32,2304]{2,1,0:T(8,128)(2,1)} %copy-done.1, bf16[512,4608]{1,0:T(8,128)(2,1)} %table_grad.3._), custom_call_target="tpu_custom_call" | custom-call | flops 1 | bytes 1 | tf_op jit(solution)/shard_map/sum/pallas_call | solution.py:237
  180.4 13.4 %all_to_all.26 = bf16[8,8,2304]{2,1,0:T(8,128)(2,1)S(1)} all-to-all(bf16[8,8,2304]{2,1,0:T(8,128)(2,1)S(1)} %bitcast.33), channel_id=1, replica_groups=mesh['x'=4,'zh'=4,'y'=4,'zl'=2,'c'=2] {'zh','zl'}, dimensions={0} | all-to-all | bytes 589824 | tf_op jit(solution)/shard_map/all_to_all | solution.py:391
  193.8 4.3 %collective-permute-start.13 = (bf16[8,2304]{1,0:T(8,128)(2,1)S(1)}, bf16[8,2304]{1,0:T(8,128)(2,1)S(1)}, u32[]{:S(2)}, u32[]{:S(2)}) collective-permute-start(bf16[8,2304]{1,0:T(8,128)(2,1)S(1)} %reduce_sum.12), channel_id=1, source_target_pairs={{0,1},{1,0},{2,3},{3,2},{4,5},{5,4},{6,7},{7,6},{8,9},{9,8},{10,11... | collective-permute-start | bytes 110600 | tf_op jit(solution)/shard_map/ppermute | solution.py:29
  (69 shorter events, 32.6 us)
Async XLA Ops:
  3.6 12.7 %collective-permute-start.2 = (bf16[8,4864]{1,0:T(8,128)(2,1)S(1)}, bf16[8,4864]{1,0:T(8,128)(2,1)S(1)}, u32[]{:S(2)}, u32[]{:S(2)}) collective-permute-start(bf16[8,4864]{1,0:T(8,128)(2,1)S(1)} %pad_maximum_fusion.3), channel_id=1, source_target_pairs={{0,16},{16,32},{32,48},{48,0},{1,17},{17,33},{33,49},{49,1},{2,18}... | collective-permute-start | bytes 233480 | tf_op jit(solution)/shard_map/ppermute | solution.py:21
  7.5 9.8 %collective-permute-start.1 = (bf16[8,4864]{1,0:T(8,128)(2,1)S(1)}, bf16[8,4864]{1,0:T(8,128)(2,1)S(1)}, u32[]{:S(2)}, u32[]{:S(2)}) collective-permute-start(bf16[8,4864]{1,0:T(8,128)(2,1)S(1)} %pad_maximum_fusion.3), channel_id=1, source_target_pairs={{0,32},{16,48},{32,0},{48,16},{1,33},{17,49},{33,1},{49,17},{2,34}... | collective-permute-start | bytes 233480 | tf_op jit(solution)/shard_map/ppermute | solution.py:21
  12.6 8.6 %collective-permute-start = (bf16[8,4864]{1,0:T(8,128)(2,1)S(1)}, bf16[8,4864]{1,0:T(8,128)(2,1)S(1)}, u32[]{:S(2)}, u32[]{:S(2)}) collective-permute-start(bf16[8,4864]{1,0:T(8,128)(2,1)S(1)} %pad_maximum_fusion.3), channel_id=1, source_target_pairs={{0,48},{16,0},{32,16},{48,32},{1,49},{17,1},{33,17},{49,33},{2,50}... | collective-permute-start | bytes 233480 | tf_op jit(solution)/shard_map/ppermute | solution.py:21
  21.9 50.8 %copy-start.2 = (bf16[32,2432]{1,0:T(8,128)(2,1)}, bf16[32,2432]{1,0:T(8,128)(2,1)S(1)}, u32[]{:S(2)}) copy-start(bf16[32,2432]{1,0:T(8,128)(2,1)S(1)} %get-tuple-element.12) | copy-start | bytes 466948
  22.1 43.6 %copy-start.4 = (bf16[512,4608]{1,0:T(8,128)(2,1)S(1)}, bf16[512,4608]{1,0:T(8,128)(2,1)}, u32[]{:S(2)}) copy-start(bf16[512,4608]{1,0:T(8,128)(2,1)} %t_own.5) | copy-start | bytes 14155780
  60.0 13.7 %copy-start = (bf16[16,32,2432]{2,1,0:T(8,128)(2,1)}, bf16[16,32,2432]{2,1,0:T(8,128)(2,1)S(1)}, u32[]{:S(2)}) copy-start(bf16[16,32,2432]{2,1,0:T(8,128)(2,1)S(1)} %all_to_all.25) | copy-start | bytes 7471108
  60.0 13.7 %collective-permute-start.3 = (bf16[512,2432]{1,0:T(8,128)(2,1)S(1)}, bf16[512,2432]{1,0:T(8,128)(2,1)}, u32[]{:S(2)}, u32[]{:S(2)}) collective-permute-start(bf16[512,2432]{1,0:T(8,128)(2,1)S(1)} %bitcast.25), channel_id=1, source_target_pairs={{0,1},{1,0},{2,3},{3,2},{4,5},{5,4},{6,7},{7,6},{8,9},{9,8},{10,11... | collective-permute-start | bytes 7471112 | tf_op jit(solution)/shard_map/ppermute | solution.py:29
  62.2 10.2 %collective-permute-start.6 = (bf16[32,2432]{1,0:T(8,128)(2,1)S(1)}, bf16[32,2432]{1,0:T(8,128)(2,1)S(1)}, u32[]{:S(2)}, u32[]{:S(2)}) collective-permute-start(bf16[32,2432]{1,0:T(8,128)(2,1)S(1)} %get-tuple-element.12), channel_id=1, source_target_pairs={{0,4},{4,8},{8,12},{12,0},{1,5},{5,9},{9,13},{13,1},{2,6},{6,10},{... | collective-permute-start | bytes 466952 | tf_op jit(solution)/shard_map/ppermute | solution.py:21
  62.5 10.0 %collective-permute-start.5 = (bf16[32,2432]{1,0:T(8,128)(2,1)S(1)}, bf16[32,2432]{1,0:T(8,128)(2,1)S(1)}, u32[]{:S(2)}, u32[]{:S(2)}) collective-permute-start(bf16[32,2432]{1,0:T(8,128)(2,1)S(1)} %get-tuple-element.12), channel_id=1, source_target_pairs={{0,8},{4,12},{8,0},{12,4},{1,9},{5,13},{9,1},{13,5},{2,10},{6,14},... | collective-permute-start | bytes 466952 | tf_op jit(solution)/shard_map/ppermute | solution.py:21
  64.4 8.4 %collective-permute-start.4 = (bf16[32,2432]{1,0:T(8,128)(2,1)S(1)}, bf16[32,2432]{1,0:T(8,128)(2,1)S(1)}, u32[]{:S(2)}, u32[]{:S(2)}) collective-permute-start(bf16[32,2432]{1,0:T(8,128)(2,1)S(1)} %get-tuple-element.12), channel_id=1, source_target_pairs={{0,12},{4,0},{8,4},{12,8},{1,13},{5,1},{9,5},{13,9},{2,14},{6,2},{... | collective-permute-start | bytes 466952 | tf_op jit(solution)/shard_map/ppermute | solution.py:21
  67.3 29.9 %collective-permute-start.8 = (bf16[512,2304]{1,0:T(8,128)(2,1)}, bf16[512,2304]{1,0:T(8,128)(2,1)}, u32[]{:S(2)}, u32[]{:S(2)}) collective-permute-start(bf16[512,2304]{1,0:T(8,128)(2,1)} %constant_dynamic-slice_fusion.1), channel_id=1, source_target_pairs={{0,1},{1,0},{2,3},{3,2},{4,5},{5,4},{6,7},{7,6},{8,9},{9,8},{10,11... | collective-permute-start | bytes 7077896 | tf_op jit(solution)/shard_map/ppermute | solution.py:29
  72.5 9.6 %copy-start.5 = (bf16[32,2432]{1,0:T(8,128)(2,1)}, bf16[32,2432]{1,0:T(8,128)(2,1)S(1)}, u32[]{:S(2)}) copy-start(bf16[32,2432]{1,0:T(8,128)(2,1)S(1)} %collective-permute-done.6) | copy-start | bytes 466948
  72.5 9.6 %copy-start.6 = (bf16[32,2432]{1,0:T(8,128)(2,1)}, bf16[32,2432]{1,0:T(8,128)(2,1)S(1)}, u32[]{:S(2)}) copy-start(bf16[32,2432]{1,0:T(8,128)(2,1)S(1)} %collective-permute-done.5) | copy-start | bytes 466948
  72.8 9.3 %copy-start.7 = (bf16[32,2432]{1,0:T(8,128)(2,1)}, bf16[32,2432]{1,0:T(8,128)(2,1)S(1)}, u32[]{:S(2)}) copy-start(bf16[32,2432]{1,0:T(8,128)(2,1)S(1)} %collective-permute-done.4) | copy-start | bytes 466948
  73.7 11.5 %copy-start.3 = (bf16[32,2432]{1,0:T(8,128)(2,1)S(1)}, bf16[32,2432]{1,0:T(8,128)(2,1)}, u32[]{:S(2)}) copy-start(bf16[32,2432]{1,0:T(8,128)(2,1)} %copy-done.2) | copy-start | bytes 466948
  82.1 15.2 %collective-permute-start.7 = (bf16[512,512]{1,0:T(8,128)(2,1)}, bf16[512,512]{1,0:T(8,128)(2,1)S(1)}, u32[]{:S(2)}, u32[]{:S(2)}) collective-permute-start(bf16[512,512]{1,0:T(8,128)(2,1)} %get-tuple-element.6.own), channel_id=1, source_target_pairs={{0,1},{1,0},{2,3},{3,2},{4,5},{5,4},{6,7},{7,6},{8,9},{9,8},{10,11... | collective-permute-start | bytes 1572872 | tf_op jit(solution)/shard_map/ppermute | solution.py:29
  87.1 28.0 %collective-permute-start.11 = (bf16[128,2432]{1,0:T(8,128)(2,1)}, bf16[128,2432]{1,0:T(8,128)(2,1)}, u32[]{:S(2)}, u32[]{:S(2)}) collective-permute-start(bf16[128,2432]{1,0:T(8,128)(2,1)} %broadcast_add_fusion.1), channel_id=1, source_target_pairs={{0,64},{64,128},{128,192},{192,0},{1,65},{65,129},{129,193},{193,1... | collective-permute-start | bytes 1867784 | tf_op jit(solution)/shard_map/ppermute | solution.py:21
  87.2 30.2 %collective-permute-start.10 = (bf16[128,2432]{1,0:T(8,128)(2,1)}, bf16[128,2432]{1,0:T(8,128)(2,1)}, u32[]{:S(2)}, u32[]{:S(2)}) collective-permute-start(bf16[128,2432]{1,0:T(8,128)(2,1)} %broadcast_add_fusion.1), channel_id=1, source_target_pairs={{0,128},{64,192},{128,0},{192,64},{1,129},{65,193},{129,1},{193,65... | collective-permute-start | bytes 1867784 | tf_op jit(solution)/shard_map/ppermute | solution.py:21
  89.6 28.4 %collective-permute-start.9 = (bf16[128,2432]{1,0:T(8,128)(2,1)}, bf16[128,2432]{1,0:T(8,128)(2,1)}, u32[]{:S(2)}, u32[]{:S(2)}) collective-permute-start(bf16[128,2432]{1,0:T(8,128)(2,1)} %broadcast_add_fusion.1), channel_id=1, source_target_pairs={{0,192},{64,0},{128,64},{192,128},{1,193},{65,1},{129,65},{193,129... | collective-permute-start | bytes 1867784 | tf_op jit(solution)/shard_map/ppermute | solution.py:21
  91.7 13.4 %all-to-all-start.1 = ((f32[16,8,128]{2,1,0:T(8,128)}), f32[16,8,128]{2,1,0:T(8,128)}, u32[]{:S(2)}, u32[]{:S(2)}) async-start(f32[16,8,128]{2,1,0:T(8,128)} %broadcast_in_dim.17), calls=%async_computation.1 | async-start | bytes 131072 | tf_op jit(solution)/shard_map/all_to_all | solution.py:320
  109.7 21.0 %all-to-all-start.2 = ((f32[16,8,128]{2,1,0:T(8,128)}), f32[16,8,128]{2,1,0:T(8,128)}, u32[]{:S(2)}, u32[]{:S(2)}) async-start(f32[16,8,128]{2,1,0:T(8,128)} %broadcast_in_dim.18), calls=%async_computation.2 | async-start | bytes 131072 | tf_op jit(solution)/shard_map/all_to_all | solution.py:320
  122.4 33.1 %collective-permute-start.12 = (bf16[512,2432]{1,0:T(8,128)(2,1)}, bf16[512,2432]{1,0:T(8,128)(2,1)}, u32[]{:S(2)}, u32[]{:S(2)}) collective-permute-start(bf16[512,2432]{1,0:T(8,128)(2,1)} %get-tuple-element.10), channel_id=1, source_target_pairs={{0,1},{1,0},{2,3},{3,2},{4,5},{5,4},{6,7},{7,6},{8,9},{9,8},{10,11... | collective-permute-start | bytes 7471112 | tf_op jit(solution)/shard_map/ppermute | solution.py:29
  137.7 37.8 %all-to-all-start.3 = ((bf16[16,32,2304]{2,1,0:T(8,128)(2,1)}), bf16[16,32,2304]{2,1,0:T(8,128)(2,1)S(1)}, u32[]{:S(2)}, u32[]{:S(2)}) async-start(bf16[16,32,2304]{2,1,0:T(8,128)(2,1)} %bitcast.32), calls=%async_computation.3 | async-start | bytes 4718592 | tf_op jit(solution)/shard_map/all_to_all | solution.py:380
  193.8 5.2 %collective-permute-start.13 = (bf16[8,2304]{1,0:T(8,128)(2,1)S(1)}, bf16[8,2304]{1,0:T(8,128)(2,1)S(1)}, u32[]{:S(2)}, u32[]{:S(2)}) collective-permute-start(bf16[8,2304]{1,0:T(8,128)(2,1)S(1)} %reduce_sum.12), channel_id=1, source_target_pairs={{0,1},{1,0},{2,3},{3,2},{4,5},{5,4},{6,7},{7,6},{8,9},{9,8},{10,11... | collective-permute-start | bytes 110600 | tf_op jit(solution)/shard_map/ppermute | solution.py:29
  (2 other events, 2.2 us)

commit v5 on v4

--- a/solution.py
+++ b/solution.py
@@ -72,7 +72,8 @@
     return jnp.sum(jnp.where(match, lanes, 0.0), 1, keepdims=True)
 
 
-def logits_kernel(place, own, other, info, t_own, t_other, _, squash, expo, slope, sums):
+def logits_kernel(place, own, other, info, t_own, t_other, _, squash, expo, slope, sums, gate):
+    gate[...] = jnp.zeros_like(gate)
     trans = (((1,), (1,)), ((), ()))
     step, tile = pl.program_id(0), expo.shape[1]
 
@@ -119,13 +120,20 @@
                 pl.BlockSpec((tile, half), lambda v, p: (v, 1 - p[0])),
                 pl.BlockSpec(memory_space=pl.ANY),
             ],
-            out_specs=[out, out, out, pl.BlockSpec((8, SLAB), lambda v, p: (0, 0))],
+            out_specs=[
+                out,
+                out,
+                out,
+                pl.BlockSpec((8, SLAB), lambda v, p: (0, 0)),
+                pl.BlockSpec((1, 1), lambda v, p: (0, 0)),
+            ],
         ),
         out_shape=[
             jax.ShapeDtypeStruct((tokens, rows), F32),
             jax.ShapeDtypeStruct((tokens, rows), F32),
             jax.ShapeDtypeStruct((tokens, rows), BF16),
             jax.ShapeDtypeStruct((8, SLAB), F32),
+            jax.ShapeDtypeStruct((1, 1), F32),
         ],
         compiler_params=params(),
         cost_estimate=cost(PRODUCTS),
@@ -174,20 +182,21 @@
     )(place, *left, table, t_other)
 
 
-def total_kernel(got, _, out):
+def total_kernel(got, _, out, gate):
+    gate[...] = jnp.zeros_like(gate)
     acc = got[0]
     for k in range(1, got.shape[0]):
         acc += got[k]
-    out[...] = acc
-
-
-def total_call(value, axes, after):
-    got = spread(value, axes)
+    out[...] = jnp.broadcast_to(acc, out.shape)
+
+
+def total_call(value, axes, after, shape):
+    got = lax.all_to_all(value, axes, 0, 0)
     return pl.pallas_call(
         total_kernel,
         in_specs=[pl.BlockSpec(memory_space=pltpu.VMEM), pl.BlockSpec(memory_space=pl.ANY)],
-        out_specs=pl.BlockSpec(memory_space=pltpu.VMEM),
-        out_shape=jax.ShapeDtypeStruct(value.shape, value.dtype),
+        out_specs=[pl.BlockSpec(memory_space=pltpu.VMEM)] * 2,
+        out_shape=[jax.ShapeDtypeStruct(shape, F32), jax.ShapeDtypeStruct((1, 1), F32)],
         compiler_params=params(),
         cost_estimate=cost(0),
         name="total",
@@ -350,16 +359,17 @@
     t_other = swap(t_send, "c")
 
     hid_other = swap(hid, "c")
-    q, e, slope, sums = logits_call(place, hid, hid_other, table, emb)
-    emb = emb + (sums[:1, :1] * 0.0).astype(BF16)
+    q, e, slope, sums, gate = logits_call(place, hid, hid_other, table, emb)
+    emb = emb + gate.astype(BF16)
     emb = jnp.concatenate([emb] + [pull(emb, "x", d) for d in (1, 2, 3)], 0)
     tokens, rows = slope.shape
     full = pl.BlockSpec((tokens, rows), lambda j, p: (0, 0))
     mean = product_call(
         mean_kernel, place, [slope, swap(slope, "c")], [full, full], table, t_other, F32, [], "mean"
     )
-    total = total_call(sums, ("zh", "zl", "c"), mean)
-    emb_other = swap(emb + (total[:1, :1] * 0.0).astype(BF16), "c")
+    each = jnp.broadcast_to(sums, (16,) + sums.shape)
+    total, gate = total_call(each, ("zh", "zl", "c"), mean, each.shape)
+    emb_other = swap(emb + gate.astype(BF16), "c")
     pick = product_call(
         pick_kernel,
         place,
@@ -374,7 +384,7 @@
         [pltpu.VMEM((tokens, rows), BF16)] * 2,
         "pick",
     )
-    total = total_call(total, ("x", "y"), pick)
+    total, _ = total_call(total, ("x", "y"), pick, sums.shape)
 
     out = combine_call(place, hid, mean, pick, total)
     got = lax.all_to_all(out.reshape(16, 32, half), ("x", "y"), 0, 0)

time: 201 us -> 200 us (level)
  local copies, waits for them, and re-layouts: 11.1 us -> 7.39 us
  waiting for transfers between devices: 25.9 us -> 28.2 us
    broadcast_in_dim x3 -> x1, local copies, waits for them, and re-layouts: 2.79 us -> 0.17 us  [spread(): jnp.broadcast_to(value, (size,) + value.shape)]
    slice x2 -> x0, local copies, waits for them, and re-layouts: 2.38 us -> none  [the longest x1 1.19 us: body(): emb = emb + (sums[:1, :1] * 0.0).astype(BF16)]
    ppermute x9, waiting for transfers between devices: 11.8 us -> 14.1 us  [pull(): lax.ppermute(value, axis, [(i, (i - shift) % size) for i in range(size)])]
  transfers between devices with their start and end apart: 17 -> 17, of which waited for: 8 -> 8; matrix products, arithmetic and copies ran while one was open for 8% -> 6% of each run, Pallas kernels for 25% -> 25%
where the time goes in v5:
time: 200 us; the launch traced here: 199 us
  Pallas kernels  52.1 us (26%)
  blocking collectives  51.5 us (26%)
  starting transfers between devices  44.8 us (22%)
  waiting for transfers between devices  28.2 us (14%)
  other arithmetic  12.5 us (6%)
  local copies, waits for them, and re-layouts  7.39 us (4%)
  between operations  2.16 us (1%)
    all_to_all x1, blocking collectives, spread(): lax.all_to_all(jnp.broadcast_to(value, (size,) + value.shape), axes, 0, 0)  37.9 us
    ppermute x9, starting transfers between devices, pull(): lax.ppermute(value, axis, [(i, (i - shift) % size) for i in range(size)])  18.1 us
    ppermute x9, waiting for transfers between devices, pull(): lax.ppermute(value, axis, [(i, (i - shift) % size) for i in range(size)])  14.1 us
    pallas_call x2, Pallas kernels, product_call(): pl.pallas_call(kernel, grid_spec=pltpu.PrefetchScalarGridSpec(num_scalar_...  13.9 us
    all_to_all x1, blocking collectives, body(): acc = lax.all_to_all(acc, ('zh', 'zl'), 0, 0)  13.6 us
    pallas_call x2, Pallas kernels, table_grad_call(): pl.pallas_call(table_grad_kernel, grid_spec=pltpu.PrefetchScalarGridSpec(...  13.5 us
    all_to_all x1, waiting for transfers between devices, body(): got = lax.all_to_all(out.reshape(16, 32, half), ('x', 'y'), 0, 0)  13.2 us
    all_to_all x2, starting transfers between devices, total_call(): got = lax.all_to_all(value, axes, 0, 0)  10.9 us
  transfers between devices with their start and end apart: 17, of which 8 were waited for; matrix products, arithmetic and copies ran while one was open for 6% of the time, Pallas kernels for 25%

profile of v5, /device:TPU:1, one launch (start us, length us, event | category | flops | bytes accessed | tf_op | source)
XLA Modules:
  0.0 198.6 jit_solution(2549390961066349494)
XLA Ops:
  3.6 3.9 %collective-permute-start.2 = (bf16[8,4864]{1,0:T(8,128)(2,1)S(1)}, bf16[8,4864]{1,0:T(8,128)(2,1)S(1)}, u32[]{:S(2)}, u32[]{:S(2)}) collective-permute-start(bf16[8,4864]{1,0:T(8,128)(2,1)S(1)} %pad_maximum_fusion.3), channel_id=1, source_target_pairs={{0,16},{16,32},{32,48},{48,0},{1,17},{17,33},{33,49},{49,1},{2,18}... | collective-permute-start | bytes 233480 | tf_op jit(solution)/shard_map/ppermute | solution.py:21
  7.5 5.1 %collective-permute-start.1 = (bf16[8,4864]{1,0:T(8,128)(2,1)S(1)}, bf16[8,4864]{1,0:T(8,128)(2,1)S(1)}, u32[]{:S(2)}, u32[]{:S(2)}) collective-permute-start(bf16[8,4864]{1,0:T(8,128)(2,1)S(1)} %pad_maximum_fusion.3), channel_id=1, source_target_pairs={{0,32},{16,48},{32,0},{48,16},{1,33},{17,49},{33,1},{49,17},{2,34}... | collective-permute-start | bytes 233480 | tf_op jit(solution)/shard_map/ppermute | solution.py:21
  12.6 2.4 %collective-permute-start = (bf16[8,4864]{1,0:T(8,128)(2,1)S(1)}, bf16[8,4864]{1,0:T(8,128)(2,1)S(1)}, u32[]{:S(2)}, u32[]{:S(2)}) collective-permute-start(bf16[8,4864]{1,0:T(8,128)(2,1)S(1)} %pad_maximum_fusion.3), channel_id=1, source_target_pairs={{0,48},{16,0},{32,16},{48,32},{1,49},{17,1},{33,17},{49,33},{2,50}... | collective-permute-start | bytes 233480 | tf_op jit(solution)/shard_map/ppermute | solution.py:21
  17.4 3.9 %collective-permute-done = bf16[8,4864]{1,0:T(8,128)(2,1)S(1)} collective-permute-done((bf16[8,4864]{1,0:T(8,128)(2,1)S(1)}, bf16[8,4864]{1,0:T(8,128)(2,1)S(1)}, u32[]{:S(2)}, u32[]{:S(2)}) %collective-permute-start) | collective-permute-done | bytes 77856 | tf_op jit(solution)/shard_map/ppermute | solution.py:21
  22.1 37.9 %all_to_all.25 = bf16[16,32,2432]{2,1,0:T(8,128)(2,1)S(1)} all-to-all(bf16[16,32,2432]{2,1,0:T(8,128)(2,1)S(1)} %broadcast_in_dim.13), channel_id=1, replica_groups=mesh['x'=4,'zh'=4,'y'=4,'zl'=2,'c'=2] {'x','y'}, dimensions={0} | all-to-all | bytes 4980736 | tf_op jit(solution)/shard_map/all_to_all | solution.py:329
  60.0 2.3 %collective-permute-start.3 = (bf16[512,2432]{1,0:T(8,128)(2,1)S(1)}, bf16[512,2432]{1,0:T(8,128)(2,1)}, u32[]{:S(2)}, u32[]{:S(2)}) collective-permute-start(bf16[512,2432]{1,0:T(8,128)(2,1)S(1)} %bitcast.25), channel_id=1, source_target_pairs={{0,1},{1,0},{2,3},{3,2},{4,5},{5,4},{6,7},{7,6},{8,9},{9,8},{10,11... | collective-permute-start | bytes 7471112 | tf_op jit(solution)/shard_map/ppermute | solution.py:29
  68.8 3.6 %collective-permute-done.6 = bf16[32,2432]{1,0:T(8,128)(2,1)S(1)} collective-permute-done((bf16[32,2432]{1,0:T(8,128)(2,1)S(1)}, bf16[32,2432]{1,0:T(8,128)(2,1)S(1)}, u32[]{:S(2)}, u32[]{:S(2)}) %collective-permute-start.6) | collective-permute-done | bytes 155680 | tf_op jit(solution)/shard_map/ppermute | solution.py:21
  73.7 8.4 %logits.1 = (f32[512,512]{1,0:T(8,128)}, f32[512,512]{1,0:T(8,128)}, bf16[512,512]{1,0:T(8,128)(2,1)}, f32[8,128]{1,0:T(8,128)}, f32[1,1]{1,0:T(1,128)}) custom-call(s32[4]{0:T(128)} %pad_add_fusion.place, bf16[512,2432]{1,0:T(8,128)(2,1)} %bitcast.26, bf16[512,2432]{1,0:T(8,128)(2,1)} %collective-permute-done.3.other.hid, bf16[512,2432]{1,0:T(8,128)(2,1)} %bitcast.27, ...), custom_call_target="tpu_custom_call" | custom-call | flops 9999999827968 | bytes 1 | tf_op jit(solution)/shard_map/logits/pallas_call | solution.py:110
  86.1 2.4 %collective-permute-start.10 = (bf16[128,2432]{1,0:T(8,128)(2,1)}, bf16[128,2432]{1,0:T(8,128)(2,1)}, u32[]{:S(2)}, u32[]{:S(2)}) collective-permute-start(bf16[128,2432]{1,0:T(8,128)(2,1)} %broadcast_add_fusion.1), channel_id=1, source_target_pairs={{0,128},{64,192},{128,0},{192,64},{1,129},{65,193},{129,1},{193,65... | collective-permute-start | bytes 1867784 | tf_op jit(solution)/shard_map/ppermute | solution.py:21
  90.6 5.5 %all-to-all-start.1 = ((f32[16,8,128]{2,1,0:T(8,128)}), f32[16,8,128]{2,1,0:T(8,128)}, u32[]{:S(2)}, u32[]{:S(2)}) async-start(f32[16,8,128]{2,1,0:T(8,128)} %broadcast_in_dim.14), calls=%async_computation.1 | async-start | bytes 131072 | tf_op jit(solution)/shard_map/all_to_all | solution.py:194
  96.9 7.1 %mean.1._ = f32[512,2304]{1,0:T(8,128)} custom-call(s32[4]{0:T(128)} %pad_add_fusion.place, bf16[512,512]{1,0:T(8,128)(2,1)} %get-tuple-element.10.own, bf16[512,512]{1,0:T(8,128)(2,1)} %copy-done.8, bf16[512,4608]{1,0:T(8,128)(2,1)} %t_own.5, bf16[512,2304]{1,0:T(8,128)(2,1)} %collective-permute-done.8.t_other), custom_call_target="tpu_custom_call" | custom-call | flops 9999999827968 | bytes 1 | tf_op jit(solution)/shard_map/mean/pallas_call | solution.py:165
  106.2 5.4 %all-to-all-start.2 = ((f32[16,8,128]{2,1,0:T(8,128)}), f32[16,8,128]{2,1,0:T(8,128)}, u32[]{:S(2)}, u32[]{:S(2)}) async-start(f32[16,8,128]{2,1,0:T(8,128)} %get-tuple-element.12), calls=%async_computation.2 | async-start | bytes 131072 | tf_op jit(solution)/shard_map/all_to_all | solution.py:194
  111.6 4.8 %collective-permute-done.10 = bf16[128,2432]{1,0:T(8,128)(2,1)} collective-permute-done((bf16[128,2432]{1,0:T(8,128)(2,1)}, bf16[128,2432]{1,0:T(8,128)(2,1)}, u32[]{:S(2)}, u32[]{:S(2)}) %collective-permute-start.10) | collective-permute-done | bytes 622624 | tf_op jit(solution)/shard_map/ppermute | solution.py:21
  116.8 4.4 %broadcast_add_fusion = (bf16[512,2432]{1,0:T(8,128)(2,1)}, bf16[512,2432]{1,0:T(8,128)(2,1)}) fusion(bf16[]{:T(256)} %bitcast.15, bf16[128,2432]{1,0:T(8,128)(2,1)} %collective-permute-done.11, bf16[128,2432]{1,0:T(8,128)(2,1)} %collective-permute-done.10, bf16[128,2432]{1,0:T(8,128)(2,1)} %collective-permute-done.9, bf16[128,2432]{1,0:T(8,128)(2,1)} %broadcast_add_fusion.1), kind=kLoop, calls=%fused_computation.1 | loop fusion | flops 13697024 | bytes 7471106 | tf_op jit(solution)/shard_map/add | solution.py:372
  122.7 6.8 %pick.1._ = bf16[512,2304]{1,0:T(8,128)(2,1)} custom-call(s32[4]{0:T(128)} %pad_add_fusion.place, bf16[512,2432]{1,0:T(8,128)(2,1)} %bitcast.28, f32[512,2304]{1,0:T(8,128)} %mean.1._, bf16[512,4608]{1,0:T(8,128)(2,1)} %t_own.5, bf16[512,2304]{1,0:T(8,128)(2,1)} %collective-permute-done.8.t_other), custom_call_target="tpu_custom_call" | custom-call | flops 9999999827968 | bytes 1 | tf_op jit(solution)/shard_map/pick/pallas_call | solution.py:165
  131.0 5.5 %combine.1._ = bf16[512,2304]{1,0:T(8,128)(2,1)} custom-call(s32[4]{0:T(128)} %pad_add_fusion.place, bf16[512,2432]{1,0:T(8,128)(2,1)} %bitcast.29, f32[512,2304]{1,0:T(8,128)} %mean.1._, bf16[512,2304]{1,0:T(8,128)(2,1)} %pick.1._, f32[8,128]{1,0:T(8,128)} %get-tuple-element.13.total), custom_call_target="tpu_custom_call" | custom-call | flops 1 | bytes 1 | tf_op jit(solution)/shard_map/combine/pallas_call | solution.py:221
  136.5 5.7 %all-to-all-start.3 = ((bf16[16,32,2304]{2,1,0:T(8,128)(2,1)}), bf16[16,32,2304]{2,1,0:T(8,128)(2,1)S(1)}, u32[]{:S(2)}, u32[]{:S(2)}) async-start(bf16[16,32,2304]{2,1,0:T(8,128)(2,1)} %bitcast.32), calls=%async_computation.3 | async-start | bytes 4718592 | tf_op jit(solution)/shard_map/all_to_all | solution.py:390
  142.3 5.4 %dlogit.1.turned = bf16[512,1024]{1,0:T(8,128)(2,1)} custom-call(s32[4]{0:T(128)} %pad_add_fusion.place, bf16[512,2432]{1,0:T(8,128)(2,1)} %bitcast.30, bf16[512,2432]{1,0:T(8,128)(2,1)} %get-tuple-element.19.emb_info.emb, f32[512,512]{1,0:T(8,128)} %get-tuple-element.15.q, f32[512,512]{1,0:T(8,128)} %get-tuple-element.16.e, ...), custom_call_target="tpu_custom_call" | custom-call | flops 1 | bytes 1 | tf_op jit(solution)/shard_map/dlogit/pallas_call | solution.py:279
  147.6 6.8 %table_grad.2.refs_0_ = bf16[512,4608]{1,0:T(8,128)(2,1)} custom-call(s32[4]{0:T(128)} %pad_add_fusion.place, bf16[512,1024]{1,0:T(8,128)(2,1)} %dlogit.1.turned, bf16[512,2432]{1,0:T(8,128)(2,1)} %bitcast.31, bf16[512,2432]{1,0:T(8,128)(2,1)} %get-tuple-element.19.emb_info.emb), custom_call_target="tpu_custom_call" | custom-call | flops 1 | bytes 1 | tf_op jit(solution)/shard_map/table_grad/pallas_call | solution.py:307
  154.4 6.7 %table_grad.3._ = bf16[512,4608]{1,0:T(8,128)(2,1)} custom-call(s32[4]{0:T(128)} %pad_add_fusion.place, bf16[512,1024]{1,0:T(8,128)(2,1)} %dlogit.1.turned, bf16[512,2432]{1,0:T(8,128)(2,1)} %collective-permute-done.3.other.hid, bf16[512,2432]{1,0:T(8,128)(2,1)} %collective-permute-done.12.emb, ...), custom_call_target="tpu_custom_call", output_to_operand_aliasing={{}: (4, {})} | custom-call | flops 1 | bytes 1 | tf_op jit(solution)/shard_map/table_grad/pallas_call | solution.py:307
  161.2 13.2 %all-to-all-done.3.got = bf16[16,32,2304]{2,1,0:T(8,128)(2,1)S(1)} async-done(((bf16[16,32,2304]{2,1,0:T(8,128)(2,1)}), bf16[16,32,2304]{2,1,0:T(8,128)(2,1)S(1)}, u32[]{:S(2)}, u32[]{:S(2)}) %all-to-all-start.3) | async-done | bytes 2359328 | tf_op jit(solution)/shard_map/all_to_all | solution.py:390
  175.8 2.4 %sum.1 = bf16[32,2304]{1,0:T(8,128)(2,1)} custom-call(bf16[16,32,2304]{2,1,0:T(8,128)(2,1)} %copy-done.1, bf16[512,4608]{1,0:T(8,128)(2,1)} %table_grad.3._), custom_call_target="tpu_custom_call" | custom-call | flops 1 | bytes 1 | tf_op jit(solution)/shard_map/sum/pallas_call | solution.py:246
  179.2 13.6 %all_to_all.26 = bf16[8,8,2304]{2,1,0:T(8,128)(2,1)S(1)} all-to-all(bf16[8,8,2304]{2,1,0:T(8,128)(2,1)S(1)} %bitcast.33), channel_id=1, replica_groups=mesh['x'=4,'zh'=4,'y'=4,'zl'=2,'c'=2] {'zh','zl'}, dimensions={0} | all-to-all | bytes 589824 | tf_op jit(solution)/shard_map/all_to_all | solution.py:401
  192.9 4.3 %collective-permute-start.13 = (bf16[8,2304]{1,0:T(8,128)(2,1)S(1)}, bf16[8,2304]{1,0:T(8,128)(2,1)S(1)}, u32[]{:S(2)}, u32[]{:S(2)}) collective-permute-start(bf16[8,2304]{1,0:T(8,128)(2,1)S(1)} %reduce_sum.12), channel_id=1, source_target_pairs={{0,1},{1,0},{2,3},{3,2},{4,5},{5,4},{6,7},{7,6},{8,9},{9,8},{10,11... | collective-permute-start | bytes 110600 | tf_op jit(solution)/shard_map/ppermute | solution.py:29
  (66 shorter events, 29.0 us)
Async XLA Ops:
  3.6 12.7 %collective-permute-start.2 = (bf16[8,4864]{1,0:T(8,128)(2,1)S(1)}, bf16[8,4864]{1,0:T(8,128)(2,1)S(1)}, u32[]{:S(2)}, u32[]{:S(2)}) collective-permute-start(bf16[8,4864]{1,0:T(8,128)(2,1)S(1)} %pad_maximum_fusion.3), channel_id=1, source_target_pairs={{0,16},{16,32},{32,48},{48,0},{1,17},{17,33},{33,49},{49,1},{2,18}... | collective-permute-start | bytes 233480 | tf_op jit(solution)/shard_map/ppermute | solution.py:21
  7.5 9.8 %collective-permute-start.1 = (bf16[8,4864]{1,0:T(8,128)(2,1)S(1)}, bf16[8,4864]{1,0:T(8,128)(2,1)S(1)}, u32[]{:S(2)}, u32[]{:S(2)}) collective-permute-start(bf16[8,4864]{1,0:T(8,128)(2,1)S(1)} %pad_maximum_fusion.3), channel_id=1, source_target_pairs={{0,32},{16,48},{32,0},{48,16},{1,33},{17,49},{33,1},{49,17},{2,34}... | collective-permute-start | bytes 233480 | tf_op jit(solution)/shard_map/ppermute | solution.py:21
  12.6 8.6 %collective-permute-start = (bf16[8,4864]{1,0:T(8,128)(2,1)S(1)}, bf16[8,4864]{1,0:T(8,128)(2,1)S(1)}, u32[]{:S(2)}, u32[]{:S(2)}) collective-permute-start(bf16[8,4864]{1,0:T(8,128)(2,1)S(1)} %pad_maximum_fusion.3), channel_id=1, source_target_pairs={{0,48},{16,0},{32,16},{48,32},{1,49},{17,1},{33,17},{49,33},{2,50}... | collective-permute-start | bytes 233480 | tf_op jit(solution)/shard_map/ppermute | solution.py:21
  21.9 50.8 %copy-start.2 = (bf16[32,2432]{1,0:T(8,128)(2,1)}, bf16[32,2432]{1,0:T(8,128)(2,1)S(1)}, u32[]{:S(2)}) copy-start(bf16[32,2432]{1,0:T(8,128)(2,1)S(1)} %get-tuple-element.20) | copy-start | bytes 466948
  22.1 43.6 %copy-start.4 = (bf16[512,4608]{1,0:T(8,128)(2,1)S(1)}, bf16[512,4608]{1,0:T(8,128)(2,1)}, u32[]{:S(2)}) copy-start(bf16[512,4608]{1,0:T(8,128)(2,1)} %t_own.5) | copy-start | bytes 14155780
  60.0 13.7 %copy-start = (bf16[16,32,2432]{2,1,0:T(8,128)(2,1)}, bf16[16,32,2432]{2,1,0:T(8,128)(2,1)S(1)}, u32[]{:S(2)}) copy-start(bf16[16,32,2432]{2,1,0:T(8,128)(2,1)S(1)} %all_to_all.25) | copy-start | bytes 7471108
  60.0 13.7 %collective-permute-start.3 = (bf16[512,2432]{1,0:T(8,128)(2,1)S(1)}, bf16[512,2432]{1,0:T(8,128)(2,1)}, u32[]{:S(2)}, u32[]{:S(2)}) collective-permute-start(bf16[512,2432]{1,0:T(8,128)(2,1)S(1)} %bitcast.25), channel_id=1, source_target_pairs={{0,1},{1,0},{2,3},{3,2},{4,5},{5,4},{6,7},{7,6},{8,9},{9,8},{10,11... | collective-permute-start | bytes 7471112 | tf_op jit(solution)/shard_map/ppermute | solution.py:29
  62.2 10.2 %collective-permute-start.6 = (bf16[32,2432]{1,0:T(8,128)(2,1)S(1)}, bf16[32,2432]{1,0:T(8,128)(2,1)S(1)}, u32[]{:S(2)}, u32[]{:S(2)}) collective-permute-start(bf16[32,2432]{1,0:T(8,128)(2,1)S(1)} %get-tuple-element.20), channel_id=1, source_target_pairs={{0,4},{4,8},{8,12},{12,0},{1,5},{5,9},{9,13},{13,1},{2,6},{6,10},{... | collective-permute-start | bytes 466952 | tf_op jit(solution)/shard_map/ppermute | solution.py:21
  62.5 10.0 %collective-permute-start.5 = (bf16[32,2432]{1,0:T(8,128)(2,1)S(1)}, bf16[32,2432]{1,0:T(8,128)(2,1)S(1)}, u32[]{:S(2)}, u32[]{:S(2)}) collective-permute-start(bf16[32,2432]{1,0:T(8,128)(2,1)S(1)} %get-tuple-element.20), channel_id=1, source_target_pairs={{0,8},{4,12},{8,0},{12,4},{1,9},{5,13},{9,1},{13,5},{2,10},{6,14},... | collective-permute-start | bytes 466952 | tf_op jit(solution)/shard_map/ppermute | solution.py:21
  64.4 8.4 %collective-permute-start.4 = (bf16[32,2432]{1,0:T(8,128)(2,1)S(1)}, bf16[32,2432]{1,0:T(8,128)(2,1)S(1)}, u32[]{:S(2)}, u32[]{:S(2)}) collective-permute-start(bf16[32,2432]{1,0:T(8,128)(2,1)S(1)} %get-tuple-element.20), channel_id=1, source_target_pairs={{0,12},{4,0},{8,4},{12,8},{1,13},{5,1},{9,5},{13,9},{2,14},{6,2},{... | collective-permute-start | bytes 466952 | tf_op jit(solution)/shard_map/ppermute | solution.py:21
  67.3 28.8 %collective-permute-start.8 = (bf16[512,2304]{1,0:T(8,128)(2,1)}, bf16[512,2304]{1,0:T(8,128)(2,1)}, u32[]{:S(2)}, u32[]{:S(2)}) collective-permute-start(bf16[512,2304]{1,0:T(8,128)(2,1)} %constant_dynamic-slice_fusion.1), channel_id=1, source_target_pairs={{0,1},{1,0},{2,3},{3,2},{4,5},{5,4},{6,7},{7,6},{8,9},{9,8},{10,11... | collective-permute-start | bytes 7077896 | tf_op jit(solution)/shard_map/ppermute | solution.py:29
  72.5 9.7 %copy-start.5 = (bf16[32,2432]{1,0:T(8,128)(2,1)}, bf16[32,2432]{1,0:T(8,128)(2,1)S(1)}, u32[]{:S(2)}) copy-start(bf16[32,2432]{1,0:T(8,128)(2,1)S(1)} %collective-permute-done.6) | copy-start | bytes 466948
  72.5 9.7 %copy-start.6 = (bf16[32,2432]{1,0:T(8,128)(2,1)}, bf16[32,2432]{1,0:T(8,128)(2,1)S(1)}, u32[]{:S(2)}) copy-start(bf16[32,2432]{1,0:T(8,128)(2,1)S(1)} %collective-permute-done.5) | copy-start | bytes 466948
  72.8 9.4 %copy-start.7 = (bf16[32,2432]{1,0:T(8,128)(2,1)}, bf16[32,2432]{1,0:T(8,128)(2,1)S(1)}, u32[]{:S(2)}) copy-start(bf16[32,2432]{1,0:T(8,128)(2,1)S(1)} %collective-permute-done.4) | copy-start | bytes 466948
  73.7 10.3 %copy-start.3 = (bf16[32,2432]{1,0:T(8,128)(2,1)S(1)}, bf16[32,2432]{1,0:T(8,128)(2,1)}, u32[]{:S(2)}) copy-start(bf16[32,2432]{1,0:T(8,128)(2,1)} %copy-done.2) | copy-start | bytes 466948
  82.1 14.0 %collective-permute-start.7 = (bf16[512,512]{1,0:T(8,128)(2,1)}, bf16[512,512]{1,0:T(8,128)(2,1)S(1)}, u32[]{:S(2)}, u32[]{:S(2)}) collective-permute-start(bf16[512,512]{1,0:T(8,128)(2,1)} %get-tuple-element.10.own), channel_id=1, source_target_pairs={{0,1},{1,0},{2,3},{3,2},{4,5},{5,4},{6,7},{7,6},{8,9},{9,8},{10,11... | collective-permute-start | bytes 1572872 | tf_op jit(solution)/shard_map/ppermute | solution.py:29
  86.0 25.6 %collective-permute-start.11 = (bf16[128,2432]{1,0:T(8,128)(2,1)}, bf16[128,2432]{1,0:T(8,128)(2,1)}, u32[]{:S(2)}, u32[]{:S(2)}) collective-permute-start(bf16[128,2432]{1,0:T(8,128)(2,1)} %broadcast_add_fusion.1), channel_id=1, source_target_pairs={{0,64},{64,128},{128,192},{192,0},{1,65},{65,129},{129,193},{193,1... | collective-permute-start | bytes 1867784 | tf_op jit(solution)/shard_map/ppermute | solution.py:21
  86.1 30.3 %collective-permute-start.10 = (bf16[128,2432]{1,0:T(8,128)(2,1)}, bf16[128,2432]{1,0:T(8,128)(2,1)}, u32[]{:S(2)}, u32[]{:S(2)}) collective-permute-start(bf16[128,2432]{1,0:T(8,128)(2,1)} %broadcast_add_fusion.1), channel_id=1, source_target_pairs={{0,128},{64,192},{128,0},{192,64},{1,129},{65,193},{129,1},{193,65... | collective-permute-start | bytes 1867784 | tf_op jit(solution)/shard_map/ppermute | solution.py:21
  88.5 28.4 %collective-permute-start.9 = (bf16[128,2432]{1,0:T(8,128)(2,1)}, bf16[128,2432]{1,0:T(8,128)(2,1)}, u32[]{:S(2)}, u32[]{:S(2)}) collective-permute-start(bf16[128,2432]{1,0:T(8,128)(2,1)} %broadcast_add_fusion.1), channel_id=1, source_target_pairs={{0,192},{64,0},{128,64},{192,128},{1,193},{65,1},{129,65},{193,129... | collective-permute-start | bytes 1867784 | tf_op jit(solution)/shard_map/ppermute | solution.py:21
  90.6 13.4 %all-to-all-start.1 = ((f32[16,8,128]{2,1,0:T(8,128)}), f32[16,8,128]{2,1,0:T(8,128)}, u32[]{:S(2)}, u32[]{:S(2)}) async-start(f32[16,8,128]{2,1,0:T(8,128)} %broadcast_in_dim.14), calls=%async_computation.1 | async-start | bytes 131072 | tf_op jit(solution)/shard_map/all_to_all | solution.py:194
  106.2 23.4 %all-to-all-start.2 = ((f32[16,8,128]{2,1,0:T(8,128)}), f32[16,8,128]{2,1,0:T(8,128)}, u32[]{:S(2)}, u32[]{:S(2)}) async-start(f32[16,8,128]{2,1,0:T(8,128)} %get-tuple-element.12), calls=%async_computation.2 | async-start | bytes 131072 | tf_op jit(solution)/shard_map/all_to_all | solution.py:194
  121.3 33.2 %collective-permute-start.12 = (bf16[512,2432]{1,0:T(8,128)(2,1)}, bf16[512,2432]{1,0:T(8,128)(2,1)}, u32[]{:S(2)}, u32[]{:S(2)}) collective-permute-start(bf16[512,2432]{1,0:T(8,128)(2,1)} %get-tuple-element.18), channel_id=1, source_target_pairs={{0,1},{1,0},{2,3},{3,2},{4,5},{5,4},{6,7},{7,6},{8,9},{9,8},{10,11... | collective-permute-start | bytes 7471112 | tf_op jit(solution)/shard_map/ppermute | solution.py:29
  136.5 37.8 %all-to-all-start.3 = ((bf16[16,32,2304]{2,1,0:T(8,128)(2,1)}), bf16[16,32,2304]{2,1,0:T(8,128)(2,1)S(1)}, u32[]{:S(2)}, u32[]{:S(2)}) async-start(bf16[16,32,2304]{2,1,0:T(8,128)(2,1)} %bitcast.32), calls=%async_computation.3 | async-start | bytes 4718592 | tf_op jit(solution)/shard_map/all_to_all | solution.py:390
  192.9 5.1 %collective-permute-start.13 = (bf16[8,2304]{1,0:T(8,128)(2,1)S(1)}, bf16[8,2304]{1,0:T(8,128)(2,1)S(1)}, u32[]{:S(2)}, u32[]{:S(2)}) collective-permute-start(bf16[8,2304]{1,0:T(8,128)(2,1)S(1)} %reduce_sum.12), channel_id=1, source_target_pairs={{0,1},{1,0},{2,3},{3,2},{4,5},{5,4},{6,7},{7,6},{8,9},{9,8},{10,11... | collective-permute-start | bytes 110600 | tf_op jit(solution)/shard_map/ppermute | solution.py:29
  (2 other events, 2.2 us)

commit v6 on v5

--- a/solution.py
+++ b/solution.py
@@ -141,12 +141,15 @@
     )(place, own, other, own, table, table, after)
 
 
-def mean_kernel(place, own, other, t_own, t_other, out):
+def mean_kernel(place, own, other, t_own, t_other, out, gate):
+    gate[...] = jnp.zeros_like(gate)
     acc = jnp.dot(own[...], t_own[...], preferred_element_type=F32)
     out[...] = acc + jnp.dot(other[...], t_other[...], preferred_element_type=F32)
 
 
-def pick_kernel(place, info, _, t_own, t_other, out, mine, theirs):
+def pick_kernel(place, info, _, t_own, t_other, out, gate, mine, theirs):
+    gate[...] = jnp.zeros_like(gate)
+
     @pl.when(pl.program_id(0) == 0)
     def _():
         columns = lax.broadcasted_iota(jnp.int32, mine.shape, 1)
@@ -172,10 +175,16 @@
                 pl.BlockSpec((rows, TILE), lambda j, p: (0, p[0] * steps + j)),
                 pl.BlockSpec((rows, TILE), lambda j, p: (0, j)),
             ],
-            out_specs=pl.BlockSpec((tokens, TILE), lambda j, p: (0, j)),
+            out_specs=[
+                pl.BlockSpec((tokens, TILE), lambda j, p: (0, j)),
+                pl.BlockSpec((1, 1), lambda j, p: (0, 0)),
+            ],
             scratch_shapes=scratch,
         ),
-        out_shape=jax.ShapeDtypeStruct((tokens, half), kind),
+        out_shape=[
+            jax.ShapeDtypeStruct((tokens, half), kind),
+            jax.ShapeDtypeStruct((1, 1), F32),
+        ],
         compiler_params=params(),
         cost_estimate=cost(PRODUCTS),
         name=name,
@@ -229,7 +238,7 @@
         ),
         out_shape=jax.ShapeDtypeStruct((tokens, half), BF16),
         compiler_params=params(),
-        cost_estimate=cost(0),
+        cost_estimate=cost(PRODUCTS),
         name="combine",
     )(place, hid, mean, pick, total)
 
@@ -364,13 +373,12 @@
     emb = jnp.concatenate([emb] + [pull(emb, "x", d) for d in (1, 2, 3)], 0)
     tokens, rows = slope.shape
     full = pl.BlockSpec((tokens, rows), lambda j, p: (0, 0))
-    mean = product_call(
+    mean, _ = product_call(
         mean_kernel, place, [slope, swap(slope, "c")], [full, full], table, t_other, F32, [], "mean"
     )
     each = jnp.broadcast_to(sums, (16,) + sums.shape)
     total, gate = total_call(each, ("zh", "zl", "c"), mean, each.shape)
-    emb_other = swap(emb + gate.astype(BF16), "c")
-    pick = product_call(
+    pick, gate = product_call(
         pick_kernel,
         place,
         [hid, mean],
@@ -384,6 +392,7 @@
         [pltpu.VMEM((tokens, rows), BF16)] * 2,
         "pick",
     )
+    emb_other = swap(emb + gate.astype(BF16), "c")
     total, _ = total_call(total, ("x", "y"), pick, sums.shape)
 
     out = combine_call(place, hid, mean, pick, total)

time: 200 us -> 197 us (0.985)
  waiting for transfers between devices: 28.2 us -> 24.1 us
  blocking collectives: 51.5 us -> 53.8 us
    ppermute x9, waiting for transfers between devices: 14.1 us -> 8.95 us  [pull(): lax.ppermute(value, axis, [(i, (i - shift) % size) for i in range(size)])]
    all_to_all x1, blocking collectives: 13.6 us -> 16 us  [body(): acc = lax.all_to_all(acc, ('zh', 'zl'), 0, 0)]
  transfers between devices with their start and end apart: 17 -> 17, of which waited for: 8 -> 7; matrix products, arithmetic and copies ran while one was open for 6% -> 4% of each run, Pallas kernels for 25% -> 25%
where the time goes in v6:
time: 197 us; the launch traced here: 196 us
  blocking collectives  53.8 us (27%)
  Pallas kernels  52.1 us (26%)
  starting transfers between devices  43.8 us (22%)
  waiting for transfers between devices  24.1 us (12%)
  other arithmetic  12.4 us (6%)
  local copies, waits for them, and re-layouts  7.44 us (4%)
  between operations  2.11 us (1%)
    all_to_all x1, blocking collectives, spread(): lax.all_to_all(jnp.broadcast_to(value, (size,) + value.shape), axes, 0, 0)  37.9 us
    ppermute x9, starting transfers between devices, pull(): lax.ppermute(value, axis, [(i, (i - shift) % size) for i in range(size)])  18.1 us
    all_to_all x1, blocking collectives, body(): acc = lax.all_to_all(acc, ('zh', 'zl'), 0, 0)  16 us
    pallas_call x2, Pallas kernels, product_call(): pl.pallas_call(kernel, grid_spec=pltpu.PrefetchScalarGridSpec(num_scalar_...  14 us
    pallas_call x2, Pallas kernels, table_grad_call(): pl.pallas_call(table_grad_kernel, grid_spec=pltpu.PrefetchScalarGridSpec(...  13.6 us
    all_to_all x1, waiting for transfers between devices, body(): got = lax.all_to_all(out.reshape(16, 32, half), ('x', 'y'), 0, 0)  13.1 us
    all_to_all x2, starting transfers between devices, total_call(): got = lax.all_to_all(value, axes, 0, 0)  10.9 us
    ppermute x5, starting transfers between devices, swap(): return lax.ppermute(value, axis, [(0, 1), (1, 0)])  9.71 us
  transfers between devices with their start and end apart: 17, of which 7 were waited for; matrix products, arithmetic and copies ran while one was open for 4% of the time, Pallas kernels for 25%

profile of v6, /device:TPU:1, one launch (start us, length us, event | category | flops | bytes accessed | tf_op | source)
XLA Modules:
  0.0 195.8 jit_solution(9165115141276860378)
XLA Ops:
  3.6 3.9 %collective-permute-start.2 = (bf16[8,4864]{1,0:T(8,128)(2,1)S(1)}, bf16[8,4864]{1,0:T(8,128)(2,1)S(1)}, u32[]{:S(2)}, u32[]{:S(2)}) collective-permute-start(bf16[8,4864]{1,0:T(8,128)(2,1)S(1)} %pad_maximum_fusion.3), channel_id=1, source_target_pairs={{0,16},{16,32},{32,48},{48,0},{1,17},{17,33},{33,49},{49,1},{2,18}... | collective-permute-start | bytes 233480 | tf_op jit(solution)/shard_map/ppermute | solution.py:21
  7.5 5.1 %collective-permute-start.1 = (bf16[8,4864]{1,0:T(8,128)(2,1)S(1)}, bf16[8,4864]{1,0:T(8,128)(2,1)S(1)}, u32[]{:S(2)}, u32[]{:S(2)}) collective-permute-start(bf16[8,4864]{1,0:T(8,128)(2,1)S(1)} %pad_maximum_fusion.3), channel_id=1, source_target_pairs={{0,32},{16,48},{32,0},{48,16},{1,33},{17,49},{33,1},{49,17},{2,34}... | collective-permute-start | bytes 233480 | tf_op jit(solution)/shard_map/ppermute | solution.py:21
  12.6 2.4 %collective-permute-start = (bf16[8,4864]{1,0:T(8,128)(2,1)S(1)}, bf16[8,4864]{1,0:T(8,128)(2,1)S(1)}, u32[]{:S(2)}, u32[]{:S(2)}) collective-permute-start(bf16[8,4864]{1,0:T(8,128)(2,1)S(1)} %pad_maximum_fusion.3), channel_id=1, source_target_pairs={{0,48},{16,0},{32,16},{48,32},{1,49},{17,1},{33,17},{49,33},{2,50}... | collective-permute-start | bytes 233480 | tf_op jit(solution)/shard_map/ppermute | solution.py:21
  17.4 3.9 %collective-permute-done = bf16[8,4864]{1,0:T(8,128)(2,1)S(1)} collective-permute-done((bf16[8,4864]{1,0:T(8,128)(2,1)S(1)}, bf16[8,4864]{1,0:T(8,128)(2,1)S(1)}, u32[]{:S(2)}, u32[]{:S(2)}) %collective-permute-start) | collective-permute-done | bytes 77856 | tf_op jit(solution)/shard_map/ppermute | solution.py:21
  22.1 37.9 %all_to_all.25 = bf16[16,32,2432]{2,1,0:T(8,128)(2,1)S(1)} all-to-all(bf16[16,32,2432]{2,1,0:T(8,128)(2,1)S(1)} %broadcast_in_dim.13), channel_id=1, replica_groups=mesh['x'=4,'zh'=4,'y'=4,'zl'=2,'c'=2] {'x','y'}, dimensions={0} | all-to-all | bytes 4980736 | tf_op jit(solution)/shard_map/all_to_all | solution.py:338
  60.0 2.3 %collective-permute-start.3 = (bf16[512,2432]{1,0:T(8,128)(2,1)S(1)}, bf16[512,2432]{1,0:T(8,128)(2,1)}, u32[]{:S(2)}, u32[]{:S(2)}) collective-permute-start(bf16[512,2432]{1,0:T(8,128)(2,1)S(1)} %bitcast.25), channel_id=1, source_target_pairs={{0,1},{1,0},{2,3},{3,2},{4,5},{5,4},{6,7},{7,6},{8,9},{9,8},{10,11... | collective-permute-start | bytes 7471112 | tf_op jit(solution)/shard_map/ppermute | solution.py:29
  68.8 3.7 %collective-permute-done.6 = bf16[32,2432]{1,0:T(8,128)(2,1)S(1)} collective-permute-done((bf16[32,2432]{1,0:T(8,128)(2,1)S(1)}, bf16[32,2432]{1,0:T(8,128)(2,1)S(1)}, u32[]{:S(2)}, u32[]{:S(2)}) %collective-permute-start.6) | collective-permute-done | bytes 155680 | tf_op jit(solution)/shard_map/ppermute | solution.py:21
  73.7 8.4 %logits.1 = (f32[512,512]{1,0:T(8,128)}, f32[512,512]{1,0:T(8,128)}, bf16[512,512]{1,0:T(8,128)(2,1)}, f32[8,128]{1,0:T(8,128)}, f32[1,1]{1,0:T(1,128)}) custom-call(s32[4]{0:T(128)} %pad_add_fusion.place, bf16[512,2432]{1,0:T(8,128)(2,1)} %bitcast.26, bf16[512,2432]{1,0:T(8,128)(2,1)} %collective-permute-done.3.other.hid, bf16[512,2432]{1,0:T(8,128)(2,1)} %bitcast.27, ...), custom_call_target="tpu_custom_call" | custom-call | flops 9999999827968 | bytes 1 | tf_op jit(solution)/shard_map/logits/pallas_call | solution.py:110
  84.0 2.0 %broadcast_add_fusion.1 = bf16[128,2432]{1,0:T(8,128)(2,1)} fusion(bf16[]{:T(256)} %bitcast.14, bf16[32,2432]{1,0:T(8,128)(2,1)} %copy-done.5, bf16[32,2432]{1,0:T(8,128)(2,1)} %copy-done.6, bf16[32,2432]{1,0:T(8,128)(2,1)} %copy-done.7, bf16[32,2432]{1,0:T(8,128)(2,1)S(1)} %copy-done.3), kind=kLoop, calls=%fused_computation.4 | loop fusion | flops 3112960 | bytes 1245186 | tf_op jit(solution)/shard_map/add | solution.py:372
  86.1 2.4 %collective-permute-start.10 = (bf16[128,2432]{1,0:T(8,128)(2,1)}, bf16[128,2432]{1,0:T(8,128)(2,1)}, u32[]{:S(2)}, u32[]{:S(2)}) collective-permute-start(bf16[128,2432]{1,0:T(8,128)(2,1)} %broadcast_add_fusion.1), channel_id=1, source_target_pairs={{0,128},{64,192},{128,0},{192,64},{1,129},{65,193},{129,1},{193,65... | collective-permute-start | bytes 1867784 | tf_op jit(solution)/shard_map/ppermute | solution.py:21
  90.5 5.5 %all-to-all-start.1 = ((f32[16,8,128]{2,1,0:T(8,128)}), f32[16,8,128]{2,1,0:T(8,128)}, u32[]{:S(2)}, u32[]{:S(2)}) async-start(f32[16,8,128]{2,1,0:T(8,128)} %broadcast_in_dim.14), calls=%async_computation.1 | async-start | bytes 131072 | tf_op jit(solution)/shard_map/all_to_all | solution.py:203
  96.9 7.1 %mean.1 = (f32[512,2304]{1,0:T(8,128)}, f32[1,1]{1,0:T(1,128)}) custom-call(s32[4]{0:T(128)} %pad_add_fusion.place, bf16[512,512]{1,0:T(8,128)(2,1)} %get-tuple-element.12.own, bf16[512,512]{1,0:T(8,128)(2,1)} %copy-done.8, bf16[512,4608]{1,0:T(8,128)(2,1)} %t_own.5, bf16[512,2304]{1,0:T(8,128)(2,1)} %collective-permute-done.8.t_other), custom_call_target="tpu_custom_call" | custom-call | flops 9999999827968 | bytes 1 | tf_op jit(solution)/shard_map/mean/pallas_call | solution.py:168
  105.5 5.4 %all-to-all-start.2 = ((f32[16,8,128]{2,1,0:T(8,128)}), f32[16,8,128]{2,1,0:T(8,128)}, u32[]{:S(2)}, u32[]{:S(2)}) async-start(f32[16,8,128]{2,1,0:T(8,128)} %get-tuple-element.16), calls=%async_computation.2 | async-start | bytes 131072 | tf_op jit(solution)/shard_map/all_to_all | solution.py:203
  110.9 6.9 %pick.1 = (bf16[512,2304]{1,0:T(8,128)(2,1)}, f32[1,1]{1,0:T(1,128)}) custom-call(s32[4]{0:T(128)} %pad_add_fusion.place, bf16[512,2432]{1,0:T(8,128)(2,1)} %bitcast.28, f32[512,2304]{1,0:T(8,128)} %get-tuple-element.13._.mean, bf16[512,4608]{1,0:T(8,128)(2,1)} %t_own.5, bf16[512,2304]{1,0:T(8,128)(2,1)} %collective-permute-done.8.t_other), custom_call_target="tpu_custom_call" | custom-call | flops 9999999827968 | bytes 1 | tf_op jit(solution)/shard_map/pick/pallas_call | solution.py:168
  121.0 4.4 %broadcast_add_fusion = (bf16[512,2432]{1,0:T(8,128)(2,1)}, bf16[512,2432]{1,0:T(8,128)(2,1)}) fusion(bf16[]{:T(256)} %bitcast.15, bf16[128,2432]{1,0:T(8,128)(2,1)} %collective-permute-done.11, bf16[128,2432]{1,0:T(8,128)(2,1)} %collective-permute-done.10, bf16[128,2432]{1,0:T(8,128)(2,1)} %collective-permute-done.9, bf16[128,2432]{1,0:T(8,128)(2,1)} %broadcast_add_fusion.1), kind=kLoop, calls=%fused_computation.1 | loop fusion | flops 13697024 | bytes 7471106 | tf_op jit(solution)/shard_map/add | solution.py:395
  126.5 5.5 %combine.1._ = bf16[512,2304]{1,0:T(8,128)(2,1)} custom-call(s32[4]{0:T(128)} %pad_add_fusion.place, bf16[512,2432]{1,0:T(8,128)(2,1)} %bitcast.29, f32[512,2304]{1,0:T(8,128)} %get-tuple-element.13._.mean, bf16[512,2304]{1,0:T(8,128)(2,1)} %get-tuple-element.14._.pick, f32[8,128]{1,0:T(8,128)} %get-tuple-element.17.total), custom_call_target="tpu_custom_call" | custom-call | flops 9999999827968 | bytes 1 | tf_op jit(solution)/shard_map/combine/pallas_call | solution.py:230
  132.0 5.1 %all-to-all-start.3 = ((bf16[16,32,2304]{2,1,0:T(8,128)(2,1)}), bf16[16,32,2304]{2,1,0:T(8,128)(2,1)S(1)}, u32[]{:S(2)}, u32[]{:S(2)}) async-start(bf16[16,32,2304]{2,1,0:T(8,128)(2,1)} %bitcast.32), calls=%async_computation.3 | async-start | bytes 4718592 | tf_op jit(solution)/shard_map/all_to_all | solution.py:399
  137.1 5.4 %dlogit.1.turned = bf16[512,1024]{1,0:T(8,128)(2,1)} custom-call(s32[4]{0:T(128)} %pad_add_fusion.place, bf16[512,2432]{1,0:T(8,128)(2,1)} %bitcast.30, bf16[512,2432]{1,0:T(8,128)(2,1)} %get-tuple-element.23.emb_info.emb, f32[512,512]{1,0:T(8,128)} %get-tuple-element.19.q, f32[512,512]{1,0:T(8,128)} %get-tuple-element.20.e, ...), custom_call_target="tpu_custom_call" | custom-call | flops 1 | bytes 1 | tf_op jit(solution)/shard_map/dlogit/pallas_call | solution.py:288
  142.5 6.7 %table_grad.2.refs_0_ = bf16[512,4608]{1,0:T(8,128)(2,1)} custom-call(s32[4]{0:T(128)} %pad_add_fusion.place, bf16[512,1024]{1,0:T(8,128)(2,1)} %dlogit.1.turned, bf16[512,2432]{1,0:T(8,128)(2,1)} %bitcast.31, bf16[512,2432]{1,0:T(8,128)(2,1)} %get-tuple-element.23.emb_info.emb), custom_call_target="tpu_custom_call" | custom-call | flops 1 | bytes 1 | tf_op jit(solution)/shard_map/table_grad/pallas_call | solution.py:316
  149.2 6.8 %table_grad.3._ = bf16[512,4608]{1,0:T(8,128)(2,1)} custom-call(s32[4]{0:T(128)} %pad_add_fusion.place, bf16[512,1024]{1,0:T(8,128)(2,1)} %dlogit.1.turned, bf16[512,2432]{1,0:T(8,128)(2,1)} %collective-permute-done.3.other.hid, bf16[512,2432]{1,0:T(8,128)(2,1)} %collective-permute-done.12.emb, ...), custom_call_target="tpu_custom_call", output_to_operand_aliasing={{}: (4, {})} | custom-call | flops 1 | bytes 1 | tf_op jit(solution)/shard_map/table_grad/pallas_call | solution.py:316
  156.0 13.1 %all-to-all-done.3.got = bf16[16,32,2304]{2,1,0:T(8,128)(2,1)S(1)} async-done(((bf16[16,32,2304]{2,1,0:T(8,128)(2,1)}), bf16[16,32,2304]{2,1,0:T(8,128)(2,1)S(1)}, u32[]{:S(2)}, u32[]{:S(2)}) %all-to-all-start.3) | async-done | bytes 2359328 | tf_op jit(solution)/shard_map/all_to_all | solution.py:399
  170.6 2.4 %sum.1 = bf16[32,2304]{1,0:T(8,128)(2,1)} custom-call(bf16[16,32,2304]{2,1,0:T(8,128)(2,1)} %copy-done.1, bf16[512,4608]{1,0:T(8,128)(2,1)} %table_grad.3._), custom_call_target="tpu_custom_call" | custom-call | flops 1 | bytes 1 | tf_op jit(solution)/shard_map/sum/pallas_call | solution.py:255
  174.0 16.0 %all_to_all.26 = bf16[8,8,2304]{2,1,0:T(8,128)(2,1)S(1)} all-to-all(bf16[8,8,2304]{2,1,0:T(8,128)(2,1)S(1)} %bitcast.33), channel_id=1, replica_groups=mesh['x'=4,'zh'=4,'y'=4,'zl'=2,'c'=2] {'zh','zl'}, dimensions={0} | all-to-all | bytes 589824 | tf_op jit(solution)/shard_map/all_to_all | solution.py:410
  190.0 4.3 %collective-permute-start.13 = (bf16[8,2304]{1,0:T(8,128)(2,1)S(1)}, bf16[8,2304]{1,0:T(8,128)(2,1)S(1)}, u32[]{:S(2)}, u32[]{:S(2)}) collective-permute-start(bf16[8,2304]{1,0:T(8,128)(2,1)S(1)} %reduce_sum.12), channel_id=1, source_target_pairs={{0,1},{1,0},{2,3},{3,2},{4,5},{5,4},{6,7},{7,6},{8,9},{9,8},{10,11... | collective-permute-start | bytes 110600 | tf_op jit(solution)/shard_map/ppermute | solution.py:29
  (66 shorter events, 27.3 us)
Async XLA Ops:
  3.6 12.7 %collective-permute-start.2 = (bf16[8,4864]{1,0:T(8,128)(2,1)S(1)}, bf16[8,4864]{1,0:T(8,128)(2,1)S(1)}, u32[]{:S(2)}, u32[]{:S(2)}) collective-permute-start(bf16[8,4864]{1,0:T(8,128)(2,1)S(1)} %pad_maximum_fusion.3), channel_id=1, source_target_pairs={{0,16},{16,32},{32,48},{48,0},{1,17},{17,33},{33,49},{49,1},{2,18}... | collective-permute-start | bytes 233480 | tf_op jit(solution)/shard_map/ppermute | solution.py:21
  7.5 9.8 %collective-permute-start.1 = (bf16[8,4864]{1,0:T(8,128)(2,1)S(1)}, bf16[8,4864]{1,0:T(8,128)(2,1)S(1)}, u32[]{:S(2)}, u32[]{:S(2)}) collective-permute-start(bf16[8,4864]{1,0:T(8,128)(2,1)S(1)} %pad_maximum_fusion.3), channel_id=1, source_target_pairs={{0,32},{16,48},{32,0},{48,16},{1,33},{17,49},{33,1},{49,17},{2,34}... | collective-permute-start | bytes 233480 | tf_op jit(solution)/shard_map/ppermute | solution.py:21
  12.6 8.6 %collective-permute-start = (bf16[8,4864]{1,0:T(8,128)(2,1)S(1)}, bf16[8,4864]{1,0:T(8,128)(2,1)S(1)}, u32[]{:S(2)}, u32[]{:S(2)}) collective-permute-start(bf16[8,4864]{1,0:T(8,128)(2,1)S(1)} %pad_maximum_fusion.3), channel_id=1, source_target_pairs={{0,48},{16,0},{32,16},{48,32},{1,49},{17,1},{33,17},{49,33},{2,50}... | collective-permute-start | bytes 233480 | tf_op jit(solution)/shard_map/ppermute | solution.py:21
  21.9 50.8 %copy-start.2 = (bf16[32,2432]{1,0:T(8,128)(2,1)}, bf16[32,2432]{1,0:T(8,128)(2,1)S(1)}, u32[]{:S(2)}) copy-start(bf16[32,2432]{1,0:T(8,128)(2,1)S(1)} %get-tuple-element.24) | copy-start | bytes 466948
  22.1 43.6 %copy-start.4 = (bf16[512,4608]{1,0:T(8,128)(2,1)S(1)}, bf16[512,4608]{1,0:T(8,128)(2,1)}, u32[]{:S(2)}) copy-start(bf16[512,4608]{1,0:T(8,128)(2,1)} %t_own.5) | copy-start | bytes 14155780
  60.0 13.7 %copy-start = (bf16[16,32,2432]{2,1,0:T(8,128)(2,1)}, bf16[16,32,2432]{2,1,0:T(8,128)(2,1)S(1)}, u32[]{:S(2)}) copy-start(bf16[16,32,2432]{2,1,0:T(8,128)(2,1)S(1)} %all_to_all.25) | copy-start | bytes 7471108
  60.0 13.7 %collective-permute-start.3 = (bf16[512,2432]{1,0:T(8,128)(2,1)S(1)}, bf16[512,2432]{1,0:T(8,128)(2,1)}, u32[]{:S(2)}, u32[]{:S(2)}) collective-permute-start(bf16[512,2432]{1,0:T(8,128)(2,1)S(1)} %bitcast.25), channel_id=1, source_target_pairs={{0,1},{1,0},{2,3},{3,2},{4,5},{5,4},{6,7},{7,6},{8,9},{9,8},{10,11... | collective-permute-start | bytes 7471112 | tf_op jit(solution)/shard_map/ppermute | solution.py:29
  62.2 10.2 %collective-permute-start.6 = (bf16[32,2432]{1,0:T(8,128)(2,1)S(1)}, bf16[32,2432]{1,0:T(8,128)(2,1)S(1)}, u32[]{:S(2)}, u32[]{:S(2)}) collective-permute-start(bf16[32,2432]{1,0:T(8,128)(2,1)S(1)} %get-tuple-element.24), channel_id=1, source_target_pairs={{0,4},{4,8},{8,12},{12,0},{1,5},{5,9},{9,13},{13,1},{2,6},{6,10},{... | collective-permute-start | bytes 466952 | tf_op jit(solution)/shard_map/ppermute | solution.py:21
  62.5 10.0 %collective-permute-start.5 = (bf16[32,2432]{1,0:T(8,128)(2,1)S(1)}, bf16[32,2432]{1,0:T(8,128)(2,1)S(1)}, u32[]{:S(2)}, u32[]{:S(2)}) collective-permute-start(bf16[32,2432]{1,0:T(8,128)(2,1)S(1)} %get-tuple-element.24), channel_id=1, source_target_pairs={{0,8},{4,12},{8,0},{12,4},{1,9},{5,13},{9,1},{13,5},{2,10},{6,14},... | collective-permute-start | bytes 466952 | tf_op jit(solution)/shard_map/ppermute | solution.py:21
  64.4 8.4 %collective-permute-start.4 = (bf16[32,2432]{1,0:T(8,128)(2,1)S(1)}, bf16[32,2432]{1,0:T(8,128)(2,1)S(1)}, u32[]{:S(2)}, u32[]{:S(2)}) collective-permute-start(bf16[32,2432]{1,0:T(8,128)(2,1)S(1)} %get-tuple-element.24), channel_id=1, source_target_pairs={{0,12},{4,0},{8,4},{12,8},{1,13},{5,1},{9,5},{13,9},{2,14},{6,2},{... | collective-permute-start | bytes 466952 | tf_op jit(solution)/shard_map/ppermute | solution.py:21
  67.3 28.7 %collective-permute-start.8 = (bf16[512,2304]{1,0:T(8,128)(2,1)}, bf16[512,2304]{1,0:T(8,128)(2,1)}, u32[]{:S(2)}, u32[]{:S(2)}) collective-permute-start(bf16[512,2304]{1,0:T(8,128)(2,1)} %constant_dynamic-slice_fusion.1), channel_id=1, source_target_pairs={{0,1},{1,0},{2,3},{3,2},{4,5},{5,4},{6,7},{7,6},{8,9},{9,8},{10,11... | collective-permute-start | bytes 7077896 | tf_op jit(solution)/shard_map/ppermute | solution.py:29
  72.5 9.6 %copy-start.5 = (bf16[32,2432]{1,0:T(8,128)(2,1)}, bf16[32,2432]{1,0:T(8,128)(2,1)S(1)}, u32[]{:S(2)}) copy-start(bf16[32,2432]{1,0:T(8,128)(2,1)S(1)} %collective-permute-done.6) | copy-start | bytes 466948
  72.5 9.6 %copy-start.6 = (bf16[32,2432]{1,0:T(8,128)(2,1)}, bf16[32,2432]{1,0:T(8,128)(2,1)S(1)}, u32[]{:S(2)}) copy-start(bf16[32,2432]{1,0:T(8,128)(2,1)S(1)} %collective-permute-done.5) | copy-start | bytes 466948
  72.8 9.3 %copy-start.7 = (bf16[32,2432]{1,0:T(8,128)(2,1)}, bf16[32,2432]{1,0:T(8,128)(2,1)S(1)}, u32[]{:S(2)}) copy-start(bf16[32,2432]{1,0:T(8,128)(2,1)S(1)} %collective-permute-done.4) | copy-start | bytes 466948
  73.7 10.2 %copy-start.3 = (bf16[32,2432]{1,0:T(8,128)(2,1)S(1)}, bf16[32,2432]{1,0:T(8,128)(2,1)}, u32[]{:S(2)}) copy-start(bf16[32,2432]{1,0:T(8,128)(2,1)} %copy-done.2) | copy-start | bytes 466948
  82.1 14.0 %collective-permute-start.7 = (bf16[512,512]{1,0:T(8,128)(2,1)}, bf16[512,512]{1,0:T(8,128)(2,1)S(1)}, u32[]{:S(2)}, u32[]{:S(2)}) collective-permute-start(bf16[512,512]{1,0:T(8,128)(2,1)} %get-tuple-element.12.own), channel_id=1, source_target_pairs={{0,1},{1,0},{2,3},{3,2},{4,5},{5,4},{6,7},{7,6},{8,9},{9,8},{10,11... | collective-permute-start | bytes 1572872 | tf_op jit(solution)/shard_map/ppermute | solution.py:29
  86.0 35.0 %collective-permute-start.11 = (bf16[128,2432]{1,0:T(8,128)(2,1)}, bf16[128,2432]{1,0:T(8,128)(2,1)}, u32[]{:S(2)}, u32[]{:S(2)}) collective-permute-start(bf16[128,2432]{1,0:T(8,128)(2,1)} %broadcast_add_fusion.1), channel_id=1, source_target_pairs={{0,64},{64,128},{128,192},{192,0},{1,65},{65,129},{129,193},{193,1... | collective-permute-start | bytes 1867784 | tf_op jit(solution)/shard_map/ppermute | solution.py:21
  86.1 34.9 %collective-permute-start.10 = (bf16[128,2432]{1,0:T(8,128)(2,1)}, bf16[128,2432]{1,0:T(8,128)(2,1)}, u32[]{:S(2)}, u32[]{:S(2)}) collective-permute-start(bf16[128,2432]{1,0:T(8,128)(2,1)} %broadcast_add_fusion.1), channel_id=1, source_target_pairs={{0,128},{64,192},{128,0},{192,64},{1,129},{65,193},{129,1},{193,65... | collective-permute-start | bytes 1867784 | tf_op jit(solution)/shard_map/ppermute | solution.py:21
  88.4 32.5 %collective-permute-start.9 = (bf16[128,2432]{1,0:T(8,128)(2,1)}, bf16[128,2432]{1,0:T(8,128)(2,1)}, u32[]{:S(2)}, u32[]{:S(2)}) collective-permute-start(bf16[128,2432]{1,0:T(8,128)(2,1)} %broadcast_add_fusion.1), channel_id=1, source_target_pairs={{0,192},{64,0},{128,64},{192,128},{1,193},{65,1},{129,65},{193,129... | collective-permute-start | bytes 1867784 | tf_op jit(solution)/shard_map/ppermute | solution.py:21
  90.5 13.5 %all-to-all-start.1 = ((f32[16,8,128]{2,1,0:T(8,128)}), f32[16,8,128]{2,1,0:T(8,128)}, u32[]{:S(2)}, u32[]{:S(2)}) async-start(f32[16,8,128]{2,1,0:T(8,128)} %broadcast_in_dim.14), calls=%async_computation.1 | async-start | bytes 131072 | tf_op jit(solution)/shard_map/all_to_all | solution.py:203
  105.5 14.0 %all-to-all-start.2 = ((f32[16,8,128]{2,1,0:T(8,128)}), f32[16,8,128]{2,1,0:T(8,128)}, u32[]{:S(2)}, u32[]{:S(2)}) async-start(f32[16,8,128]{2,1,0:T(8,128)} %get-tuple-element.16), calls=%async_computation.2 | async-start | bytes 131072 | tf_op jit(solution)/shard_map/all_to_all | solution.py:203
  125.4 23.9 %collective-permute-start.12 = (bf16[512,2432]{1,0:T(8,128)(2,1)}, bf16[512,2432]{1,0:T(8,128)(2,1)}, u32[]{:S(2)}, u32[]{:S(2)}) collective-permute-start(bf16[512,2432]{1,0:T(8,128)(2,1)} %get-tuple-element.22), channel_id=1, source_target_pairs={{0,1},{1,0},{2,3},{3,2},{4,5},{5,4},{6,7},{7,6},{8,9},{9,8},{10,11... | collective-permute-start | bytes 7471112 | tf_op jit(solution)/shard_map/ppermute | solution.py:29
  132.0 37.2 %all-to-all-start.3 = ((bf16[16,32,2304]{2,1,0:T(8,128)(2,1)}), bf16[16,32,2304]{2,1,0:T(8,128)(2,1)S(1)}, u32[]{:S(2)}, u32[]{:S(2)}) async-start(bf16[16,32,2304]{2,1,0:T(8,128)(2,1)} %bitcast.32), calls=%async_computation.3 | async-start | bytes 4718592 | tf_op jit(solution)/shard_map/all_to_all | solution.py:399
  190.0 5.1 %collective-permute-start.13 = (bf16[8,2304]{1,0:T(8,128)(2,1)S(1)}, bf16[8,2304]{1,0:T(8,128)(2,1)S(1)}, u32[]{:S(2)}, u32[]{:S(2)}) collective-permute-start(bf16[8,2304]{1,0:T(8,128)(2,1)S(1)} %reduce_sum.12), channel_id=1, source_target_pairs={{0,1},{1,0},{2,3},{3,2},{4,5},{5,4},{6,7},{7,6},{8,9},{9,8},{10,11... | collective-permute-start | bytes 110600 | tf_op jit(solution)/shard_map/ppermute | solution.py:29
  (2 other events, 2.3 us)

commit v7 on v6

--- a/solution.py
+++ b/solution.py
@@ -370,7 +370,7 @@
     hid_other = swap(hid, "c")
     q, e, slope, sums, gate = logits_call(place, hid, hid_other, table, emb)
     emb = emb + gate.astype(BF16)
-    emb = jnp.concatenate([emb] + [pull(emb, "x", d) for d in (1, 2, 3)], 0)
+    columns = [pull(emb, "x", d) for d in (1, 2, 3)]
     tokens, rows = slope.shape
     full = pl.BlockSpec((tokens, rows), lambda j, p: (0, 0))
     mean, _ = product_call(
@@ -392,7 +392,8 @@
         [pltpu.VMEM((tokens, rows), BF16)] * 2,
         "pick",
     )
-    emb_other = swap(emb + gate.astype(BF16), "c")
+    emb = jnp.concatenate([emb + gate.astype(BF16)] + columns, 0)
+    emb_other = swap(emb, "c")
     total, _ = total_call(total, ("x", "y"), pick, sums.shape)
 
     out = combine_call(place, hid, mean, pick, total)

time: 197 us -> 205 us (1.041)
  blocking collectives: 53.8 us -> 82 us
  starting transfers between devices: 43.8 us -> 29.7 us
  other arithmetic: 12.4 us -> 7.82 us
    all_to_all x0 -> x2, blocking collectives: none -> 29.2 us  [total_call(): got = lax.all_to_all(value, axes, 0, 0)]
    all_to_all x2 -> x0, starting transfers between devices: 10.9 us -> none  [total_call(): got = lax.all_to_all(value, axes, 0, 0)]
    add x2 -> x1, other arithmetic: 6.43 us -> 0.17 us  [body(): emb = jnp.concatenate([emb + gate.astype(BF16)] + columns, 0)]
  transfers between devices with their start and end apart: 17 -> 15, of which waited for: 7 -> 7; matrix products, arithmetic and copies ran while one was open for 4% -> 2% of each run, Pallas kernels for 25% -> 17%
where the time goes in v7:
time: 205 us; the launch traced here: 204 us
  blocking collectives  82 us (40%)
  Pallas kernels  52 us (25%)
  starting transfers between devices  29.7 us (14%)
  waiting for transfers between devices  24.4 us (12%)
  other arithmetic  7.82 us (4%)
  local copies, waits for them, and re-layouts  6.16 us (3%)
  between operations  2.09 us (1%)
    all_to_all x1, blocking collectives, spread(): lax.all_to_all(jnp.broadcast_to(value, (size,) + value.shape), axes, 0, 0)  37.9 us
    all_to_all x2, blocking collectives, total_call(): got = lax.all_to_all(value, axes, 0, 0)  29.2 us
    ppermute x9, starting transfers between devices, pull(): lax.ppermute(value, axis, [(i, (i - shift) % size) for i in range(size)])  17.6 us
    all_to_all x1, blocking collectives, body(): acc = lax.all_to_all(acc, ('zh', 'zl'), 0, 0)  15 us
    pallas_call x2, Pallas kernels, product_call(): pl.pallas_call(kernel, grid_spec=pltpu.PrefetchScalarGridSpec(num_scalar_...  14.1 us
    pallas_call x2, Pallas kernels, table_grad_call(): pl.pallas_call(table_grad_kernel, grid_spec=pltpu.PrefetchScalarGridSpec(...  13.5 us
    all_to_all x1, waiting for transfers between devices, body(): got = lax.all_to_all(out.reshape(16, 32, half), ('x', 'y'), 0, 0)  13.4 us
    ppermute x9, waiting for transfers between devices, pull(): lax.ppermute(value, axis, [(i, (i - shift) % size) for i in range(size)])  8.98 us
  transfers between devices with their start and end apart: 15, of which 7 were waited for; matrix products, arithmetic and copies ran while one was open for 2% of the time, Pallas kernels for 17%

profile of v7, /device:TPU:1, one launch (start us, length us, event | category | flops | bytes accessed | tf_op | source)
XLA Modules:
  0.0 204.2 jit_solution(16820178742715053131)
XLA Ops:
  3.6 3.9 %collective-permute-start.2 = (bf16[8,4864]{1,0:T(8,128)(2,1)S(1)}, bf16[8,4864]{1,0:T(8,128)(2,1)S(1)}, u32[]{:S(2)}, u32[]{:S(2)}) collective-permute-start(bf16[8,4864]{1,0:T(8,128)(2,1)S(1)} %pad_maximum_fusion.3), channel_id=1, source_target_pairs={{0,16},{16,32},{32,48},{48,0},{1,17},{17,33},{33,49},{49,1},{2,18}... | collective-permute-start | bytes 233480 | tf_op jit(solution)/shard_map/ppermute | solution.py:21
  7.5 5.1 %collective-permute-start.1 = (bf16[8,4864]{1,0:T(8,128)(2,1)S(1)}, bf16[8,4864]{1,0:T(8,128)(2,1)S(1)}, u32[]{:S(2)}, u32[]{:S(2)}) collective-permute-start(bf16[8,4864]{1,0:T(8,128)(2,1)S(1)} %pad_maximum_fusion.3), channel_id=1, source_target_pairs={{0,32},{16,48},{32,0},{48,16},{1,33},{17,49},{33,1},{49,17},{2,34}... | collective-permute-start | bytes 233480 | tf_op jit(solution)/shard_map/ppermute | solution.py:21
  12.6 2.4 %collective-permute-start = (bf16[8,4864]{1,0:T(8,128)(2,1)S(1)}, bf16[8,4864]{1,0:T(8,128)(2,1)S(1)}, u32[]{:S(2)}, u32[]{:S(2)}) collective-permute-start(bf16[8,4864]{1,0:T(8,128)(2,1)S(1)} %pad_maximum_fusion.3), channel_id=1, source_target_pairs={{0,48},{16,0},{32,16},{48,32},{1,49},{17,1},{33,17},{49,33},{2,50}... | collective-permute-start | bytes 233480 | tf_op jit(solution)/shard_map/ppermute | solution.py:21
  17.4 3.9 %collective-permute-done = bf16[8,4864]{1,0:T(8,128)(2,1)S(1)} collective-permute-done((bf16[8,4864]{1,0:T(8,128)(2,1)S(1)}, bf16[8,4864]{1,0:T(8,128)(2,1)S(1)}, u32[]{:S(2)}, u32[]{:S(2)}) %collective-permute-start) | collective-permute-done | bytes 77856 | tf_op jit(solution)/shard_map/ppermute | solution.py:21
  22.1 37.9 %all_to_all.25 = bf16[16,32,2432]{2,1,0:T(8,128)(2,1)S(1)} all-to-all(bf16[16,32,2432]{2,1,0:T(8,128)(2,1)S(1)} %broadcast_in_dim.13), channel_id=1, replica_groups=mesh['x'=4,'zh'=4,'y'=4,'zl'=2,'c'=2] {'x','y'}, dimensions={0} | all-to-all | bytes 4980736 | tf_op jit(solution)/shard_map/all_to_all | solution.py:338
  60.0 2.3 %collective-permute-start.3 = (bf16[512,2432]{1,0:T(8,128)(2,1)S(1)}, bf16[512,2432]{1,0:T(8,128)(2,1)}, u32[]{:S(2)}, u32[]{:S(2)}) collective-permute-start(bf16[512,2432]{1,0:T(8,128)(2,1)S(1)} %bitcast.25), channel_id=1, source_target_pairs={{0,1},{1,0},{2,3},{3,2},{4,5},{5,4},{6,7},{7,6},{8,9},{9,8},{10,11... | collective-permute-start | bytes 7471112 | tf_op jit(solution)/shard_map/ppermute | solution.py:29
  62.5 1.9 collective-permute-start.5
  65.8 1.6 constant_dynamic-slice_fusion.1
  68.7 3.7 %collective-permute-done.6 = bf16[32,2432]{1,0:T(8,128)(2,1)S(1)} collective-permute-done((bf16[32,2432]{1,0:T(8,128)(2,1)S(1)}, bf16[32,2432]{1,0:T(8,128)(2,1)S(1)}, u32[]{:S(2)}, u32[]{:S(2)}) %collective-permute-start.6) | collective-permute-done | bytes 155680 | tf_op jit(solution)/shard_map/ppermute | solution.py:21
  73.7 8.2 %logits.1 = (f32[512,512]{1,0:T(8,128)}, f32[512,512]{1,0:T(8,128)}, bf16[512,512]{1,0:T(8,128)(2,1)}, f32[8,128]{1,0:T(8,128)}, f32[1,1]{1,0:T(1,128)}) custom-call(s32[4]{0:T(128)} %pad_add_fusion.place, bf16[512,2432]{1,0:T(8,128)(2,1)} %bitcast.26, bf16[512,2432]{1,0:T(8,128)(2,1)} %collective-permute-done.3.other.hid, bf16[512,2432]{1,0:T(8,128)(2,1)} %bitcast.27, ...), custom_call_target="tpu_custom_call" | custom-call | flops 9999999827968 | bytes 1 | tf_op jit(solution)/shard_map/logits/pallas_call | solution.py:110
  85.7 7.1 %mean.1 = (f32[512,2304]{1,0:T(8,128)}, f32[1,1]{1,0:T(1,128)}) custom-call(s32[4]{0:T(128)} %pad_add_fusion.place, bf16[512,512]{1,0:T(8,128)(2,1)} %get-tuple-element.12.own, bf16[512,512]{1,0:T(8,128)(2,1)} %copy-done.12, bf16[512,4608]{1,0:T(8,128)(2,1)} %t_own.5, bf16[512,2304]{1,0:T(8,128)(2,1)} %collective-permute-done.8.t_other), custom_call_target="tpu_custom_call" | custom-call | flops 9999999827968 | bytes 1 | tf_op jit(solution)/shard_map/mean/pallas_call | solution.py:168
  92.9 7.0 %pick.1 = (bf16[512,2304]{1,0:T(8,128)(2,1)}, f32[1,1]{1,0:T(1,128)}) custom-call(s32[4]{0:T(128)} %pad_add_fusion.place, bf16[512,2432]{1,0:T(8,128)(2,1)} %bitcast.28, f32[512,2304]{1,0:T(8,128)} %get-tuple-element.13._.mean, bf16[512,4608]{1,0:T(8,128)(2,1)} %t_own.5, bf16[512,2304]{1,0:T(8,128)(2,1)} %collective-permute-done.8.t_other), custom_call_target="tpu_custom_call" | custom-call | flops 9999999827968 | bytes 1 | tf_op jit(solution)/shard_map/pick/pallas_call | solution.py:168
  103.5 13.7 %all_to_all.26.got = f32[16,8,128]{2,1,0:T(8,128)} all-to-all(f32[16,8,128]{2,1,0:T(8,128)S(1)} %broadcast_in_dim.14), channel_id=1, replica_groups=mesh['x'=4,'zh'=4,'y'=4,'zl'=2,'c'=2] {'zh','zl','c'}, dimensions={0} | all-to-all | bytes 131072 | tf_op jit(solution)/shard_map/all_to_all | solution.py:203
  118.6 15.5 %all_to_all.27.got = f32[16,8,128]{2,1,0:T(8,128)} all-to-all(f32[16,8,128]{2,1,0:T(8,128)} %get-tuple-element.16), channel_id=1, replica_groups=mesh['x'=4,'zh'=4,'y'=4,'zl'=2,'c'=2] {'x','y'}, dimensions={0} | all-to-all | bytes 131072 | tf_op jit(solution)/shard_map/all_to_all | solution.py:203
  135.6 1.7 pad_maximum_fusion.emb_info.emb
  138.1 5.5 %combine.1._ = bf16[512,2304]{1,0:T(8,128)(2,1)} custom-call(s32[4]{0:T(128)} %pad_add_fusion.place, bf16[512,2432]{1,0:T(8,128)(2,1)} %bitcast.29, f32[512,2304]{1,0:T(8,128)} %get-tuple-element.13._.mean, bf16[512,2304]{1,0:T(8,128)(2,1)} %get-tuple-element.14._.pick, f32[8,128]{1,0:T(8,128)} %get-tuple-element.17.total), custom_call_target="tpu_custom_call" | custom-call | flops 9999999827968 | bytes 1 | tf_op jit(solution)/shard_map/combine/pallas_call | solution.py:230
  143.6 3.7 %all-to-all-start.3 = ((bf16[16,32,2304]{2,1,0:T(8,128)(2,1)}), bf16[16,32,2304]{2,1,0:T(8,128)(2,1)S(1)}, u32[]{:S(2)}, u32[]{:S(2)}) async-start(bf16[16,32,2304]{2,1,0:T(8,128)(2,1)} %bitcast.32), calls=%async_computation.3 | async-start | bytes 4718592 | tf_op jit(solution)/shard_map/all_to_all | solution.py:400
  147.4 5.4 %dlogit.1.turned = bf16[512,1024]{1,0:T(8,128)(2,1)} custom-call(s32[4]{0:T(128)} %pad_add_fusion.place, bf16[512,2432]{1,0:T(8,128)(2,1)} %bitcast.30, bf16[512,2432]{1,0:T(8,128)(2,1)} %pad_maximum_fusion.emb_info.emb, f32[512,512]{1,0:T(8,128)} %get-tuple-element.20.q, f32[512,512]{1,0:T(8,128)} %get-tuple-element.21.e, ...), custom_call_target="tpu_custom_call" | custom-call | flops 1 | bytes 1 | tf_op jit(solution)/shard_map/dlogit/pallas_call | solution.py:288
  152.7 6.7 %table_grad.2.refs_0_ = bf16[512,4608]{1,0:T(8,128)(2,1)} custom-call(s32[4]{0:T(128)} %pad_add_fusion.place, bf16[512,1024]{1,0:T(8,128)(2,1)} %dlogit.1.turned, bf16[512,2432]{1,0:T(8,128)(2,1)} %bitcast.31, bf16[512,2432]{1,0:T(8,128)(2,1)} %pad_maximum_fusion.emb_info.emb), custom_call_target="tpu_custom_call" | custom-call | flops 1 | bytes 1 | tf_op jit(solution)/shard_map/table_grad/pallas_call | solution.py:316
  159.5 6.7 %table_grad.3._ = bf16[512,4608]{1,0:T(8,128)(2,1)} custom-call(s32[4]{0:T(128)} %pad_add_fusion.place, bf16[512,1024]{1,0:T(8,128)(2,1)} %dlogit.1.turned, bf16[512,2432]{1,0:T(8,128)(2,1)} %collective-permute-done.3.other.hid, bf16[512,2432]{1,0:T(8,128)(2,1)} %collective-permute-done.12.emb, ...), custom_call_target="tpu_custom_call", output_to_operand_aliasing={{}: (4, {})} | custom-call | flops 1 | bytes 1 | tf_op jit(solution)/shard_map/table_grad/pallas_call | solution.py:316
  166.2 13.4 %all-to-all-done.3.got = bf16[16,32,2304]{2,1,0:T(8,128)(2,1)S(1)} async-done(((bf16[16,32,2304]{2,1,0:T(8,128)(2,1)}), bf16[16,32,2304]{2,1,0:T(8,128)(2,1)S(1)}, u32[]{:S(2)}, u32[]{:S(2)}) %all-to-all-start.3) | async-done | bytes 2359328 | tf_op jit(solution)/shard_map/all_to_all | solution.py:400
  181.0 2.4 %sum.1 = bf16[32,2304]{1,0:T(8,128)(2,1)} custom-call(bf16[16,32,2304]{2,1,0:T(8,128)(2,1)} %copy-done.1, bf16[512,4608]{1,0:T(8,128)(2,1)} %table_grad.3._), custom_call_target="tpu_custom_call" | custom-call | flops 1 | bytes 1 | tf_op jit(solution)/shard_map/sum/pallas_call | solution.py:255
  184.4 15.0 %all_to_all.28 = bf16[8,8,2304]{2,1,0:T(8,128)(2,1)S(1)} all-to-all(bf16[8,8,2304]{2,1,0:T(8,128)(2,1)S(1)} %bitcast.33), channel_id=1, replica_groups=mesh['x'=4,'zh'=4,'y'=4,'zl'=2,'c'=2] {'zh','zl'}, dimensions={0} | all-to-all | bytes 589824 | tf_op jit(solution)/shard_map/all_to_all | solution.py:411
  199.5 3.2 %collective-permute-start.13 = (bf16[8,2304]{1,0:T(8,128)(2,1)S(1)}, bf16[8,2304]{1,0:T(8,128)(2,1)S(1)}, u32[]{:S(2)}, u32[]{:S(2)}) collective-permute-start(bf16[8,2304]{1,0:T(8,128)(2,1)S(1)} %reduce_sum.12), channel_id=1, source_target_pairs={{0,1},{1,0},{2,3},{3,2},{4,5},{5,4},{6,7},{7,6},{8,9},{9,8},{10,11... | collective-permute-start | bytes 110600 | tf_op jit(solution)/shard_map/ppermute | solution.py:29
  (72 shorter events, 24.3 us)
Async XLA Ops:
  3.6 12.7 %collective-permute-start.2 = (bf16[8,4864]{1,0:T(8,128)(2,1)S(1)}, bf16[8,4864]{1,0:T(8,128)(2,1)S(1)}, u32[]{:S(2)}, u32[]{:S(2)}) collective-permute-start(bf16[8,4864]{1,0:T(8,128)(2,1)S(1)} %pad_maximum_fusion.3), channel_id=1, source_target_pairs={{0,16},{16,32},{32,48},{48,0},{1,17},{17,33},{33,49},{49,1},{2,18}... | collective-permute-start | bytes 233480 | tf_op jit(solution)/shard_map/ppermute | solution.py:21
  7.5 9.8 %collective-permute-start.1 = (bf16[8,4864]{1,0:T(8,128)(2,1)S(1)}, bf16[8,4864]{1,0:T(8,128)(2,1)S(1)}, u32[]{:S(2)}, u32[]{:S(2)}) collective-permute-start(bf16[8,4864]{1,0:T(8,128)(2,1)S(1)} %pad_maximum_fusion.3), channel_id=1, source_target_pairs={{0,32},{16,48},{32,0},{48,16},{1,33},{17,49},{33,1},{49,17},{2,34}... | collective-permute-start | bytes 233480 | tf_op jit(solution)/shard_map/ppermute | solution.py:21
  12.6 8.6 %collective-permute-start = (bf16[8,4864]{1,0:T(8,128)(2,1)S(1)}, bf16[8,4864]{1,0:T(8,128)(2,1)S(1)}, u32[]{:S(2)}, u32[]{:S(2)}) collective-permute-start(bf16[8,4864]{1,0:T(8,128)(2,1)S(1)} %pad_maximum_fusion.3), channel_id=1, source_target_pairs={{0,48},{16,0},{32,16},{48,32},{1,49},{17,1},{33,17},{49,33},{2,50}... | collective-permute-start | bytes 233480 | tf_op jit(solution)/shard_map/ppermute | solution.py:21
  21.9 50.8 %copy-start.2 = (bf16[32,2432]{1,0:T(8,128)(2,1)}, bf16[32,2432]{1,0:T(8,128)(2,1)S(1)}, u32[]{:S(2)}) copy-start(bf16[32,2432]{1,0:T(8,128)(2,1)S(1)} %get-tuple-element.24) | copy-start | bytes 466948
  22.1 43.6 %copy-start.4 = (bf16[512,4608]{1,0:T(8,128)(2,1)S(1)}, bf16[512,4608]{1,0:T(8,128)(2,1)}, u32[]{:S(2)}) copy-start(bf16[512,4608]{1,0:T(8,128)(2,1)} %t_own.5) | copy-start | bytes 14155780
  60.0 13.7 %collective-permute-start.3 = (bf16[512,2432]{1,0:T(8,128)(2,1)S(1)}, bf16[512,2432]{1,0:T(8,128)(2,1)}, u32[]{:S(2)}, u32[]{:S(2)}) collective-permute-start(bf16[512,2432]{1,0:T(8,128)(2,1)S(1)} %bitcast.25), channel_id=1, source_target_pairs={{0,1},{1,0},{2,3},{3,2},{4,5},{5,4},{6,7},{7,6},{8,9},{9,8},{10,11... | collective-permute-start | bytes 7471112 | tf_op jit(solution)/shard_map/ppermute | solution.py:29
  62.2 10.2 %collective-permute-start.6 = (bf16[32,2432]{1,0:T(8,128)(2,1)S(1)}, bf16[32,2432]{1,0:T(8,128)(2,1)S(1)}, u32[]{:S(2)}, u32[]{:S(2)}) collective-permute-start(bf16[32,2432]{1,0:T(8,128)(2,1)S(1)} %get-tuple-element.24), channel_id=1, source_target_pairs={{0,4},{4,8},{8,12},{12,0},{1,5},{5,9},{9,13},{13,1},{2,6},{6,10},{... | collective-permute-start | bytes 466952 | tf_op jit(solution)/shard_map/ppermute | solution.py:21
  62.5 10.0 %collective-permute-start.5 = (bf16[32,2432]{1,0:T(8,128)(2,1)S(1)}, bf16[32,2432]{1,0:T(8,128)(2,1)S(1)}, u32[]{:S(2)}, u32[]{:S(2)}) collective-permute-start(bf16[32,2432]{1,0:T(8,128)(2,1)S(1)} %get-tuple-element.24), channel_id=1, source_target_pairs={{0,8},{4,12},{8,0},{12,4},{1,9},{5,13},{9,1},{13,5},{2,10},{6,14},... | collective-permute-start | bytes 466952 | tf_op jit(solution)/shard_map/ppermute | solution.py:21
  64.4 8.4 %collective-permute-start.4 = (bf16[32,2432]{1,0:T(8,128)(2,1)S(1)}, bf16[32,2432]{1,0:T(8,128)(2,1)S(1)}, u32[]{:S(2)}, u32[]{:S(2)}) collective-permute-start(bf16[32,2432]{1,0:T(8,128)(2,1)S(1)} %get-tuple-element.24), channel_id=1, source_target_pairs={{0,12},{4,0},{8,4},{12,8},{1,13},{5,1},{9,5},{13,9},{2,14},{6,2},{... | collective-permute-start | bytes 466952 | tf_op jit(solution)/shard_map/ppermute | solution.py:21
  67.3 16.4 %collective-permute-start.8 = (bf16[512,2304]{1,0:T(8,128)(2,1)}, bf16[512,2304]{1,0:T(8,128)(2,1)}, u32[]{:S(2)}, u32[]{:S(2)}) collective-permute-start(bf16[512,2304]{1,0:T(8,128)(2,1)} %constant_dynamic-slice_fusion.1), channel_id=1, source_target_pairs={{0,1},{1,0},{2,3},{3,2},{4,5},{5,4},{6,7},{7,6},{8,9},{9,8},{10,11... | collective-permute-start | bytes 7077896 | tf_op jit(solution)/shard_map/ppermute | solution.py:29
  72.5 9.5 %copy-start.5 = (bf16[32,2432]{1,0:T(8,128)(2,1)}, bf16[32,2432]{1,0:T(8,128)(2,1)S(1)}, u32[]{:S(2)}) copy-start(bf16[32,2432]{1,0:T(8,128)(2,1)S(1)} %collective-permute-done.6) | copy-start | bytes 466948
  72.5 9.5 %copy-start.7 = (bf16[32,2432]{1,0:T(8,128)(2,1)}, bf16[32,2432]{1,0:T(8,128)(2,1)S(1)}, u32[]{:S(2)}) copy-start(bf16[32,2432]{1,0:T(8,128)(2,1)S(1)} %collective-permute-done.5) | copy-start | bytes 466948
  72.8 9.2 %copy-start.9 = (bf16[32,2432]{1,0:T(8,128)(2,1)}, bf16[32,2432]{1,0:T(8,128)(2,1)S(1)}, u32[]{:S(2)}) copy-start(bf16[32,2432]{1,0:T(8,128)(2,1)S(1)} %collective-permute-done.4) | copy-start | bytes 466948
  81.9 2.9 %collective-permute-start.7 = (bf16[512,512]{1,0:T(8,128)(2,1)}, bf16[512,512]{1,0:T(8,128)(2,1)S(1)}, u32[]{:S(2)}, u32[]{:S(2)}) collective-permute-start(bf16[512,512]{1,0:T(8,128)(2,1)} %get-tuple-element.12.own), channel_id=1, source_target_pairs={{0,1},{1,0},{2,3},{3,2},{4,5},{5,4},{6,7},{7,6},{8,9},{9,8},{10,11... | collective-permute-start | bytes 1572872 | tf_op jit(solution)/shard_map/ppermute | solution.py:29
  92.8 7.7 %copy-start.6 = (bf16[32,2432]{1,0:T(8,128)(2,1)S(1)}, bf16[32,2432]{1,0:T(8,128)(2,1)}, u32[]{:S(2)}) copy-start(bf16[32,2432]{1,0:T(8,128)(2,1)} %copy-done.5) | copy-start | bytes 466948
  92.8 7.7 %copy-start.8 = (bf16[32,2432]{1,0:T(8,128)(2,1)S(1)}, bf16[32,2432]{1,0:T(8,128)(2,1)}, u32[]{:S(2)}) copy-start(bf16[32,2432]{1,0:T(8,128)(2,1)} %copy-done.7) | copy-start | bytes 466948
  92.8 7.7 %copy-start.10 = (bf16[32,2432]{1,0:T(8,128)(2,1)S(1)}, bf16[32,2432]{1,0:T(8,128)(2,1)}, u32[]{:S(2)}) copy-start(bf16[32,2432]{1,0:T(8,128)(2,1)} %copy-done.9) | copy-start | bytes 466948
  92.8 10.7 %copy-start.11 = (f32[8,128]{1,0:T(8,128)S(1)}, f32[8,128]{1,0:T(8,128)}, u32[]{:S(2)}) copy-start(f32[8,128]{1,0:T(8,128)} %get-tuple-element.15) | copy-start | bytes 12292
  100.8 34.9 %collective-permute-start.10 = (bf16[128,2432]{1,0:T(8,128)(2,1)S(1)}, bf16[128,2432]{1,0:T(8,128)(2,1)S(1)}, u32[]{:S(2)}, u32[]{:S(2)}) collective-permute-start(bf16[128,2432]{1,0:T(8,128)(2,1)S(1)} %get-tuple-element.23), channel_id=1, source_target_pairs={{0,128},{64,192},{128,0},{192,64},{1,129},{65,193},{129,1},{193,65... | collective-permute-start | bytes 1867784 | tf_op jit(solution)/shard_map/ppermute | solution.py:21
  102.0 33.6 %collective-permute-start.9 = (bf16[128,2432]{1,0:T(8,128)(2,1)S(1)}, bf16[128,2432]{1,0:T(8,128)(2,1)S(1)}, u32[]{:S(2)}, u32[]{:S(2)}) collective-permute-start(bf16[128,2432]{1,0:T(8,128)(2,1)S(1)} %get-tuple-element.23), channel_id=1, source_target_pairs={{0,192},{64,0},{128,64},{192,128},{1,193},{65,1},{129,65},{193,129... | collective-permute-start | bytes 1867784 | tf_op jit(solution)/shard_map/ppermute | solution.py:21
  103.3 32.3 %collective-permute-start.11 = (bf16[128,2432]{1,0:T(8,128)(2,1)S(1)}, bf16[128,2432]{1,0:T(8,128)(2,1)S(1)}, u32[]{:S(2)}, u32[]{:S(2)}) collective-permute-start(bf16[128,2432]{1,0:T(8,128)(2,1)S(1)} %get-tuple-element.23), channel_id=1, source_target_pairs={{0,64},{64,128},{128,192},{192,0},{1,65},{65,129},{129,193},{193,1... | collective-permute-start | bytes 1867784 | tf_op jit(solution)/shard_map/ppermute | solution.py:21
  137.3 22.1 %collective-permute-start.12 = (bf16[512,2432]{1,0:T(8,128)(2,1)}, bf16[512,2432]{1,0:T(8,128)(2,1)}, u32[]{:S(2)}, u32[]{:S(2)}) collective-permute-start(bf16[512,2432]{1,0:T(8,128)(2,1)} %pad_maximum_fusion.emb_info.emb), channel_id=1, source_target_pairs={{0,1},{1,0},{2,3},{3,2},{4,5},{5,4},{6,7},{7,6},{8,9},{9,8},{10,11... | collective-permute-start | bytes 7471112 | tf_op jit(solution)/shard_map/ppermute | solution.py:29
  143.6 36.0 %all-to-all-start.3 = ((bf16[16,32,2304]{2,1,0:T(8,128)(2,1)}), bf16[16,32,2304]{2,1,0:T(8,128)(2,1)S(1)}, u32[]{:S(2)}, u32[]{:S(2)}) async-start(bf16[16,32,2304]{2,1,0:T(8,128)(2,1)} %bitcast.32), calls=%async_computation.3 | async-start | bytes 4718592 | tf_op jit(solution)/shard_map/all_to_all | solution.py:400
  199.5 4.1 %collective-permute-start.13 = (bf16[8,2304]{1,0:T(8,128)(2,1)S(1)}, bf16[8,2304]{1,0:T(8,128)(2,1)S(1)}, u32[]{:S(2)}, u32[]{:S(2)}) collective-permute-start(bf16[8,2304]{1,0:T(8,128)(2,1)S(1)} %reduce_sum.12), channel_id=1, source_target_pairs={{0,1},{1,0},{2,3},{3,2},{4,5},{5,4},{6,7},{7,6},{8,9},{9,8},{10,11... | collective-permute-start | bytes 110600 | tf_op jit(solution)/shard_map/ppermute | solution.py:29
  (4 other events, 17.3 us)
